TPU v7x, 32 devices: a whole 2x2x4 slice. The times are simulated.
32 devices in a mesh: seq: 8 (over z, y), wsh: 4 (over x, core).
Axes of the slice: x: 2, y: 2, z: 4, core: 2. Of those that a mesh axis runs over, the one named last changes fastest.
Arguments:
- tokens: bfloat16 [2, 4, 8192, 768], P(None, 'wsh', 'seq'), may hold values from -6 to 6
- cotangent: bfloat16 [2, 4, 8192, 768], P(None, 'wsh', 'seq'), may hold values from -6 to 6
- lengths: int32 [2, 4], P(None, 'wsh'), may hold values from 2048 to 8192, as said below
- ema_alpha: bfloat16 [768, 16], P('wsh'), may hold values from -7 to -1
- ema_delta: bfloat16 [768, 16], P('wsh'), may hold values from -7 to -2
- ema_beta: bfloat16 [768, 16], P('wsh'), may hold values from -1.5 to 1.5
- ema_eta: bfloat16 [768, 16], P('wsh'), may hold values from -1.5 to 1.5
- ema_omega: bfloat16 [768], P('wsh'), may hold values from -4 to 4
- mix_weight: bfloat16 [768, 3200], P('wsh'), may hold values from -0.4375 to 0.4375
- mix_bias: bfloat16 [3200], P('wsh'), may hold values from -1.796875 to 1.796875
- value_weight: bfloat16 [768, 1536], P('wsh'), may hold values from -0.21875 to 0.21875
- value_bias: bfloat16 [1536], P('wsh'), may hold values from -1.796875 to 1.796875
- qk_gain: bfloat16 [128, 2], P('wsh'), may hold values from 0.5 to 1.5
- qk_bias: bfloat16 [128], P('wsh'), may hold values from -1.796875 to 1.796875
- rel_bias: bfloat16 [256], P('wsh'), may hold values from -5 to 5
- out_weight: bfloat16 [1536, 768], P('wsh'), may hold values from -0.625 to 0.625
- norm_gain: bfloat16 [768, 2], P('wsh'), may hold values from 0.5 to 1.5
- norm_bias: bfloat16 [768, 2], P('wsh'), may hold values from -1.796875 to 1.796875
- ffn_in: bfloat16 [768, 1536], P('wsh'), may hold values from -0.21875 to 0.21875
- ffn_in_bias: bfloat16 [1536], P('wsh'), may hold values from -1.796875 to 1.796875
- ffn_out: bfloat16 [1536, 768], P('wsh'), may hold values from -0.15625 to 0.15625
- ffn_out_bias: bfloat16 [768], P('wsh'), may hold values from -1.796875 to 1.796875
Outputs:
- output: bfloat16 [2, 4, 8192, 768], P(None, 'wsh', 'seq')
- input_grad: bfloat16 [2, 4, 8192, 768], P(None, 'wsh', 'seq')
- alpha_grad: float32 [768, 16], P('wsh')
- delta_grad: float32 [768, 16], P('wsh')
- beta_grad: float32 [768, 16], P('wsh')
- eta_grad: float32 [768, 16], P('wsh')
- omega_grad: float32 [768], P('wsh')
- mix_weight_grad: float32 [768, 3200], P('wsh')
- mix_bias_grad: float32 [3200], P('wsh')
- value_weight_grad: float32 [768, 1536], P('wsh')
- value_bias_grad: float32 [1536], P('wsh')
- qk_gain_grad: float32 [128, 2], P('wsh')
- qk_bias_grad: float32 [128], P('wsh')
- rel_bias_grad: float32 [256], P('wsh')
- out_weight_grad: float32 [1536, 768], P('wsh')
- norm_gain_grad: float32 [768, 2], P('wsh')
- norm_bias_grad: float32 [768, 2], P('wsh')
- ffn_in_grad: float32 [768, 1536], P('wsh')
- ffn_in_bias_grad: float32 [1536], P('wsh')
- ffn_out_grad: float32 [1536, 768], P('wsh')
- ffn_out_bias_grad: float32 [768], P('wsh')
Inputs may be any that keep to these rules, and one draw needn't show every extreme that they name: `lengths`: in every micro-batch some sequence uses all 8192 positions.
All inputs are finite; a program needn't handle non-finite values.
Results may differ from a plain program's by a relative error of at most 0.015.
Values may be sent and summed in bfloat16 or wider, within the bound.
A program may use at most 1.125 GiB of HBM per device.

v0:
```python
import math

import jax
import jax.numpy as jnp
from jax import lax
from jax.sharding import PartitionSpec as P

BLOCK = 128


HIGHEST = lax.Precision.HIGHEST
EPSILON = 1e-05


def silu_slope(pre_act):
    logistic = jax.nn.sigmoid(pre_act)
    return logistic * (1.0 + pre_act * (1.0 - logistic))


def dot_plain(left_op, right_op):
    return jnp.dot(left_op, right_op, preferred_element_type=jnp.float32)


def dot_rows(left_op, right_op):
    return jnp.einsum("ri,rj->ij", left_op, right_op, preferred_element_type=jnp.float32)


def dot_back(grad_rows, weight):
    return jnp.einsum("rj,ij->ri", grad_rows, weight, preferred_element_type=jnp.float32)


def normalize(values):
    center = values - jnp.mean(values, axis=-1, keepdims=True)
    inverse = lax.rsqrt(jnp.mean(center * center, axis=-1, keepdims=True) + EPSILON)
    return (center * inverse, inverse)


def norm_back(weighted, normed, inverse):
    return inverse * (
        weighted
        - jnp.mean(weighted, axis=-1, keepdims=True)
        - normed * jnp.mean(weighted * normed, axis=-1, keepdims=True)
    )


def skew_matrix(wrapped):
    lead = wrapped.shape[:-1]
    flat = jnp.tile(wrapped, (1,) * len(lead) + (BLOCK,))[..., : BLOCK * (2 * BLOCK - 1)]
    return flat.reshape(lead + (BLOCK, 2 * BLOCK - 1))[..., :BLOCK]


def ema_local(ema_params, chan_x):
    rate_logit, damp_logit, in_scale, out_scale, skip_scale = ema_params
    chan_count, seq_rows, length = chan_x.shape
    blocks = length // BLOCK
    rate_in = jax.nn.sigmoid(rate_logit)
    damping = jax.nn.sigmoid(damp_logit)
    log_keep = jnp.log(1.0 - rate_in * damping)
    in_gain = in_scale * rate_in
    kernel_weight = out_scale * in_gain
    lag_float = jnp.arange(BLOCK, dtype=jnp.float32)
    kernel = jnp.einsum(
        "ch,chl->cl",
        kernel_weight,
        jnp.exp(lag_float[None, None, :] * log_keep[:, :, None]),
        precision=HIGHEST,
    )
    wrapped = jnp.concatenate(
        [kernel[:, :1], jnp.zeros((chan_count, BLOCK), jnp.float32), kernel[:, :0:-1]], axis=1
    )
    toeplitz = skew_matrix(wrapped)
    blocked = chan_x.reshape(chan_count, seq_rows, blocks, BLOCK)
    inner_part = jnp.einsum("ctj,crbj->crbt", toeplitz, blocked, precision=HIGHEST)
    tail_weight = (
        jnp.exp((BLOCK - 1.0 - lag_float)[None, None, :] * log_keep[:, :, None])
        * in_gain[:, :, None]
    )
    block_input = jnp.einsum("chj,crbj->chrb", tail_weight, blocked, precision=HIGHEST)
    block_float = jnp.arange(blocks, dtype=jnp.float32)
    block_gap = block_float[:, None] - block_float[None, :]
    reach_table = jnp.exp(
        (BLOCK * jnp.maximum(block_gap, 0.0))[None, None] * log_keep[:, :, None, None]
    ) * (block_gap >= 0.0).astype(jnp.float32)
    states = jnp.einsum("chbk,chrk->chrb", reach_table, block_input, precision=HIGHEST)
    carried = jnp.concatenate([jnp.zeros_like(states[..., :1]), states[..., :-1]], axis=-1)
    head_weight = (
        jnp.exp((lag_float + 1.0)[None, None, :] * log_keep[:, :, None]) * out_scale[:, :, None]
    )
    outer_part = jnp.einsum("cht,chrb->crbt", head_weight, carried, precision=HIGHEST)
    smoothed = (inner_part + outer_part).reshape(chan_count, seq_rows, length)
    return jax.nn.silu(smoothed + skip_scale[:, None, None] * chan_x)


def body(
    tokens,
    cotangent,
    lengths,
    ema_alpha,
    ema_delta,
    ema_beta,
    ema_eta,
    ema_omega,
    mix_weight,
    mix_bias,
    value_weight,
    value_bias,
    qk_gain,
    qk_bias,
    rel_bias,
    out_weight,
    norm_gain,
    norm_bias,
    ffn_in,
    ffn_in_bias,
    ffn_out,
    ffn_out_bias,
):
    shards = (
        ema_alpha,
        ema_delta,
        ema_beta,
        ema_eta,
        ema_omega,
        mix_weight,
        mix_bias,
        value_weight,
        value_bias,
        qk_gain,
        qk_bias,
        rel_bias,
        out_weight,
        norm_gain,
        norm_bias,
        ffn_in,
        ffn_in_bias,
        ffn_out,
        ffn_out_bias,
    )
    gathered = (
        lax.all_gather(ema_alpha, "wsh", axis=0, tiled=True),
        lax.all_gather(ema_delta, "wsh", axis=0, tiled=True),
        lax.all_gather(ema_beta, "wsh", axis=0, tiled=True),
        lax.all_gather(ema_eta, "wsh", axis=0, tiled=True),
        lax.all_gather(ema_omega, "wsh", axis=0, tiled=True),
        lax.all_gather(mix_weight, "wsh", axis=0, tiled=True),
        lax.all_gather(mix_bias, "wsh", axis=0, tiled=True),
        lax.all_gather(value_weight, "wsh", axis=0, tiled=True),
        lax.all_gather(value_bias, "wsh", axis=0, tiled=True),
        lax.all_gather(qk_gain, "wsh", axis=0, tiled=True),
        lax.all_gather(qk_bias, "wsh", axis=0, tiled=True),
        lax.all_gather(rel_bias, "wsh", axis=0, tiled=True),
        lax.all_gather(out_weight, "wsh", axis=0, tiled=True),
        lax.all_gather(norm_gain, "wsh", axis=0, tiled=True),
        lax.all_gather(norm_bias, "wsh", axis=0, tiled=True),
        lax.all_gather(ffn_in, "wsh", axis=0, tiled=True),
        lax.all_gather(ffn_in_bias, "wsh", axis=0, tiled=True),
        lax.all_gather(ffn_out, "wsh", axis=0, tiled=True),
        lax.all_gather(ffn_out_bias, "wsh", axis=0, tiled=True),
    )
    (
        rate_full,
        damp_full,
        in_full,
        out_full,
        skip_full,
        w_mix,
        b_mix,
        w_value,
        b_value,
        qk_scale,
        qk_shift,
        rel_full,
        w_out,
        norm_scale,
        norm_shift,
        w_ffn_in,
        b_ffn_in,
        w_ffn_out,
        b_ffn_out,
    ) = gathered
    micro_count, seq_count, slice_len, model_width = tokens.shape
    seq_devices = lax.axis_size("seq")
    wsh_devices = lax.axis_size("wsh")
    seq_place = lax.axis_index("seq")
    chan_count = model_width // seq_devices
    chan_start = seq_place * chan_count
    ema_params = tuple(
        (
            lax.dynamic_slice_in_dim(member.astype(jnp.float32), chan_start, chan_count, 0)
            for member in (rate_full, damp_full, in_full, out_full, skip_full)
        )
    )
    row_count = seq_count * slice_len
    total_rows = micro_count * row_count
    z_width = qk_scale.shape[0]
    v_width = w_value.shape[1]
    block_count = total_rows // BLOCK
    position = seq_place * slice_len + jnp.arange(slice_len, dtype=jnp.int32)
    live_all = (
        (position[None, None, :] < lengths[:, :, None]).astype(jnp.float32).reshape(total_rows)
    )
    within = jnp.arange(BLOCK, dtype=jnp.int32)
    causal = within[:, None] >= within[None, :]
    rel_matrix = skew_matrix(jnp.roll(rel_full.astype(jnp.float32)[::-1], BLOCK))
    score_scale = z_width ** (-0.5)
    qk_scales = qk_scale.astype(jnp.float32)
    norm_s = norm_scale.astype(jnp.float32)
    norm_b = norm_shift.astype(jnp.float32)

    def score_blocks(queries, key_rows):
        raw_scores = jnp.einsum(
            "nid,njd->nij",
            queries.reshape(block_count, BLOCK, z_width),
            key_rows.reshape(block_count, BLOCK, z_width),
            preferred_element_type=jnp.float32,
        )
        return jnp.where(causal, raw_scores * score_scale + rel_matrix, -1e30)

    pullbacks = []
    xp_list = []
    for micro_index in range(micro_count):
        part_rows = tokens[micro_index].transpose(2, 0, 1)
        chan_in = lax.all_to_all(part_rows, "seq", split_axis=0, concat_axis=2, tiled=True)
        chan_out, ema_pullback = jax.vjp(ema_local, ema_params, chan_in.astype(jnp.float32))
        back_rows = lax.all_to_all(
            chan_out.astype(jnp.bfloat16), "seq", split_axis=2, concat_axis=0, tiled=True
        )
        xp_list.append(back_rows.transpose(1, 2, 0))
        pullbacks.append(ema_pullback)
    tok_rows = tokens.reshape(total_rows, model_width)
    cot_rows = cotangent.reshape(total_rows, model_width)
    xp_rows = jnp.stack(xp_list).reshape(total_rows, model_width)
    base_rows = dot_plain(xp_rows, w_mix) + b_mix.astype(jnp.float32)
    update_gate = jax.nn.sigmoid(base_rows[:, :model_width])
    z_pre = base_rows[:, model_width : model_width + z_width]
    r_pre = base_rows[:, model_width + z_width : model_width + z_width + v_width]
    h_lin = base_rows[:, model_width + z_width + v_width :]
    shared = jax.nn.silu(z_pre)
    reset_gate = jax.nn.silu(r_pre)
    v_pre = dot_plain(tok_rows, w_value) + b_value.astype(jnp.float32)
    values = jax.nn.silu(v_pre).astype(jnp.bfloat16)
    queries = (shared * qk_scales[:, 0] + qk_shift.astype(jnp.float32)).astype(jnp.bfloat16)
    key_rows = (shared * qk_scales[:, 1]).astype(jnp.bfloat16)
    scores = score_blocks(queries, key_rows)
    row_max = jnp.max(scores, axis=-1, keepdims=True)
    log_total = row_max + jnp.log(jnp.sum(jnp.exp(scores - row_max), axis=-1, keepdims=True))
    weights_low = jnp.exp(scores - log_total).astype(jnp.bfloat16)
    attended = jnp.einsum(
        "nij,njd->nid",
        weights_low,
        values.reshape(block_count, BLOCK, v_width),
        preferred_element_type=jnp.float32,
    ).reshape(total_rows, v_width)
    mixed_rows = (reset_gate * attended).astype(jnp.bfloat16)
    h_pre = h_lin + dot_plain(mixed_rows, w_out)
    hidden = jax.nn.silu(h_pre)
    tok_float = tok_rows.astype(jnp.float32)
    residual = tok_float + update_gate * (hidden - tok_float)
    normed_one, inverse_one = normalize(residual)
    first_norm = normed_one * norm_s[:, 0] + norm_b[:, 0]
    first_low = first_norm.astype(jnp.bfloat16)
    f_pre = dot_plain(first_low, w_ffn_in) + b_ffn_in.astype(jnp.float32)
    f_act = jax.nn.silu(f_pre).astype(jnp.bfloat16)
    second = first_norm + dot_plain(f_act, w_ffn_out) + b_ffn_out.astype(jnp.float32)
    normed_two, inverse_two = normalize(second)
    result_rows = ((normed_two * norm_s[:, 1] + norm_b[:, 1]) * live_all[:, None]).astype(
        jnp.bfloat16
    )
    saved_state = (
        update_gate,
        z_pre,
        r_pre,
        shared,
        reset_gate,
        v_pre,
        values,
        queries,
        key_rows,
        log_total,
        attended,
        mixed_rows,
        h_pre,
        hidden,
        tok_float,
        normed_one,
        inverse_one,
        first_low,
        f_pre,
        f_act,
        normed_two,
        inverse_two,
    )
    result_rows, saved_state = (result_rows, saved_state)
    (
        update_gate,
        z_pre,
        r_pre,
        shared,
        reset_gate,
        v_pre,
        values,
        queries,
        key_rows,
        log_total,
        attended,
        mixed_rows,
        h_pre,
        hidden,
        tok_float,
        normed_one,
        inverse_one,
        first_low,
        f_pre,
        f_act,
        normed_two,
        inverse_two,
    ) = saved_state
    d_result = cot_rows.astype(jnp.float32) * live_all[:, None]
    gain_two = jnp.sum(d_result * normed_two, axis=0)
    shift_two = jnp.sum(d_result, axis=0)
    d_second = norm_back(d_result * norm_s[:, 1], normed_two, inverse_two)
    d_ffn_out_bias = jnp.sum(d_second, axis=0)
    d_branch = d_second.astype(jnp.bfloat16)
    d_ffn_out = dot_rows(f_act, d_branch)
    d_f_pre = (dot_back(d_branch, w_ffn_out) * silu_slope(f_pre)).astype(jnp.bfloat16)
    d_ffn_in_bias = jnp.sum(d_f_pre.astype(jnp.float32), axis=0)
    d_ffn_in = dot_rows(first_low, d_f_pre)
    d_first = d_second + dot_back(d_f_pre, w_ffn_in)
    gain_one = jnp.sum(d_first * normed_one, axis=0)
    shift_one = jnp.sum(d_first, axis=0)
    d_resid = norm_back(d_first * norm_s[:, 0], normed_one, inverse_one)
    d_h_pre = d_resid * update_gate * silu_slope(h_pre)
    d_mixed_out = d_h_pre.astype(jnp.bfloat16)
    d_out_weight = dot_rows(mixed_rows, d_mixed_out)
    d_mixed = dot_back(d_mixed_out, w_out)
    d_attended = (d_mixed * reset_gate).astype(jnp.bfloat16).reshape(block_count, BLOCK, v_width)
    value_blocks = values.reshape(block_count, BLOCK, v_width)
    weights_full = jnp.exp(score_blocks(queries, key_rows) - log_total)
    weights_low = weights_full.astype(jnp.bfloat16)
    d_weights = jnp.einsum(
        "nid,njd->nij", d_attended, value_blocks, preferred_element_type=jnp.float32
    )
    d_values = jnp.einsum(
        "nij,nid->njd", weights_low, d_attended, preferred_element_type=jnp.float32
    ).reshape(total_rows, v_width)
    d_scores = weights_full * (
        d_weights - jnp.sum(weights_full * d_weights, axis=-1, keepdims=True)
    )
    d_scores_low = d_scores.astype(jnp.bfloat16)
    score_sum = jnp.sum(d_scores_low.astype(jnp.float32), axis=0)
    widened = jnp.pad(score_sum, ((0, 0), (0, BLOCK - 1))).reshape(-1)
    diagonal_sums = jnp.sum(jnp.pad(widened, (0, BLOCK)).reshape(BLOCK, 2 * BLOCK), axis=0)
    d_rel = jnp.roll(diagonal_sums[::-1], BLOCK)
    d_queries = (
        jnp.einsum(
            "nij,njd->nid",
            d_scores_low,
            key_rows.reshape(block_count, BLOCK, z_width),
            preferred_element_type=jnp.float32,
        ).reshape(total_rows, z_width)
        * score_scale
    )
    d_keys = (
        jnp.einsum(
            "nij,nid->njd",
            d_scores_low,
            queries.reshape(block_count, BLOCK, z_width),
            preferred_element_type=jnp.float32,
        ).reshape(total_rows, z_width)
        * score_scale
    )
    d_qk_scale = jnp.stack(
        [jnp.sum(d_queries * shared, axis=0), jnp.sum(d_keys * shared, axis=0)], axis=1
    )
    d_qk_shift = jnp.sum(d_queries, axis=0)
    d_shared = d_queries * qk_scales[:, 0] + d_keys * qk_scales[:, 1]
    d_base = jnp.concatenate(
        [
            d_resid * (hidden - tok_float) * update_gate * (1.0 - update_gate),
            d_shared * silu_slope(z_pre),
            d_mixed * attended * silu_slope(r_pre),
            d_h_pre,
        ],
        axis=1,
    ).astype(jnp.bfloat16)
    d_mix_bias = jnp.sum(d_base.astype(jnp.float32), axis=0)
    d_mix_weight = dot_rows(xp_rows, d_base)
    d_xp = dot_back(d_base, w_mix).astype(jnp.bfloat16)
    d_v_pre = (d_values * silu_slope(v_pre)).astype(jnp.bfloat16)
    d_value_bias = jnp.sum(d_v_pre.astype(jnp.float32), axis=0)
    d_value_weight = dot_rows(tok_rows, d_v_pre)
    d_tokens = d_resid * (1.0 - update_gate) + dot_back(d_v_pre, w_value)
    gradients = (
        d_mix_weight,
        d_mix_bias,
        d_value_weight,
        d_value_bias,
        d_qk_scale,
        d_qk_shift,
        d_rel,
        d_out_weight,
        jnp.stack([gain_one, gain_two], axis=1),
        jnp.stack([shift_one, shift_two], axis=1),
        d_ffn_in,
        d_ffn_in_bias,
        d_ffn_out,
        d_ffn_out_bias,
    )
    d_tokens, d_xp, gradients = (d_tokens, d_xp, gradients)
    result_rows, d_tokens, d_xp, token_sums = (result_rows, d_tokens, d_xp, gradients)
    d_xp_parts = d_xp.reshape(micro_count, seq_count, slice_len, model_width)
    ema_sums = None
    d_ema_list = []
    for micro_index in range(micro_count):
        d_chan_in = lax.all_to_all(
            d_xp_parts[micro_index].transpose(2, 0, 1),
            "seq",
            split_axis=0,
            concat_axis=2,
            tiled=True,
        )
        ema_grads, d_chan = pullbacks[micro_index](d_chan_in.astype(jnp.float32))
        ema_sums = ema_grads if ema_sums is None else jax.tree.map(jnp.add, ema_sums, ema_grads)
        d_back = lax.all_to_all(
            d_chan.astype(jnp.bfloat16), "seq", split_axis=2, concat_axis=0, tiled=True
        )
        d_ema_list.append(d_back.transpose(1, 2, 0).reshape(row_count, model_width))
    d_ema_all = jnp.concatenate(d_ema_list, axis=0)
    output = result_rows.reshape(micro_count, seq_count, slice_len, model_width)
    input_grad = (
        (d_tokens + d_ema_all.astype(jnp.float32))
        .astype(jnp.bfloat16)
        .reshape(micro_count, seq_count, slice_len, model_width)
    )
    full_ema = tuple(
        (
            lax.dynamic_update_slice_in_dim(
                jnp.zeros((model_width,) + member.shape[1:], jnp.float32), member, chan_start, 0
            )
            for member in ema_sums
        )
    )
    all_grads = full_ema + tuple(token_sums)
    share = sum((math.prod(member.shape) for member in all_grads)) // wsh_devices
    padded = -(-share // seq_devices) * seq_devices
    pieces = [member.reshape(wsh_devices, -1) for member in all_grads]
    flat = jnp.concatenate(pieces, axis=1)
    parted = (
        flat.reshape(wsh_devices, seq_devices, padded // seq_devices)
        .transpose(1, 0, 2)
        .reshape(seq_devices * wsh_devices, padded // seq_devices)
    )
    mine = lax.psum_scatter(parted, ("seq", "wsh"), scatter_dimension=0, tiled=True)
    summed = (
        lax.all_gather(mine.astype(jnp.bfloat16), "seq", axis=0, tiled=True)
        .astype(mine.dtype)
        .reshape(-1)
    )
    final = []
    start_at = 0
    for member in shards:
        piece_size = math.prod(member.shape)
        final.append(summed[start_at : start_at + piece_size].reshape(member.shape))
        start_at = start_at + piece_size
    return (output, input_grad) + tuple(final)


def solution(mesh):
    in_specs = (
        P(None, "wsh", "seq", None),
        P(None, "wsh", "seq", None),
        P(None, "wsh"),
        P("wsh", None),
        P("wsh", None),
        P("wsh", None),
        P("wsh", None),
        P("wsh"),
        P("wsh", None),
        P("wsh"),
        P("wsh", None),
        P("wsh"),
        P("wsh", None),
        P("wsh"),
        P("wsh"),
        P("wsh", None),
        P("wsh", None),
        P("wsh", None),
        P("wsh", None),
        P("wsh"),
        P("wsh", None),
        P("wsh"),
    )
    out_specs = (
        P(None, "wsh", "seq", None),
        P(None, "wsh", "seq", None),
        P("wsh", None),
        P("wsh", None),
        P("wsh", None),
        P("wsh", None),
        P("wsh"),
        P("wsh", None),
        P("wsh"),
        P("wsh", None),
        P("wsh"),
        P("wsh", None),
        P("wsh"),
        P("wsh"),
        P("wsh", None),
        P("wsh", None),
        P("wsh", None),
        P("wsh", None),
        P("wsh"),
        P("wsh", None),
        P("wsh"),
    )
    return jax.shard_map(body, mesh=mesh, in_specs=in_specs, out_specs=out_specs, check_vma=False)
```

profile of v0, /device:TPU:0, one launch (start us, length us, event | category | flops | bytes accessed | tf_op | source)
XLA Modules:
  0.0 3271.5 jit_solution(9995476404544592133)
XLA Ops:
  52.0 12.6 all-reduce.18
  87.2 17.8 copy.454
  105.1 10.1 slice.231
  115.1 22.6 reshape.986
  139.0 11.5 fusion
  150.5 49.9 %copy.439 = f32[96,16,64,64]{3,2,1,0:T(8,128)} copy(f32[96,16,64,64]{0,3,2,1:T(8,128)} %fusion) | data formatting | bytes 50331648 | tf_op jit(solution)/shard_map/jvp()/mul | solution.py:81
  226.1 9.0 fusion.18
  235.1 82.9 %fusion.148 = f32[96,16,1,64]{3,2,1,0:T(1,128)} fusion(f32[96,16,64,1]{2,3,1,0:T(1,128)S(1)} %bitcast.443, f32[96,16,64,64]{3,2,1,0:T(8,128)} %copy.439), kind=kOutput, calls=%fused_computation.317 | convolution fusion | flops 75497472 | bytes 25952256 | tf_op jit(solution)/shard_map/jvp(chbk,chrk->chrb)/dot_general | solution.py:84
  318.0 82.6 %fusion.147 = f32[96,16,1,64]{3,2,1,0:T(1,128)S(1)} fusion(f32[96,16,64,1]{2,3,1,0:T(1,128)S(1)} %bitcast.444, f32[96,16,64,64]{3,2,1,0:T(8,128)} %copy.439), kind=kOutput, calls=%fused_computation.316 | convolution fusion | flops 75497472 | bytes 25952256 | tf_op jit(solution)/shard_map/jvp(chbk,chrk->chrb)/dot_general | solution.py:84
  418.5 9.0 fusion.16
  442.6 9.4 copy.359
  452.0 46.9 %reduce.29 = bf16[8192,96]{1,0:T(8,128)(2,1)} reduce(bf16[8192,1,96]{2,1,0:T(2,128)(2,1)} %bitcast.422, bf16[]{:T(256)} %broadcast.559), dimensions={1}, to_apply=%bitcast.311.reduce_sub_computation | reduce | bytes 3145730
  540.8 9.4 copy.366
  550.2 46.5 %reduce.28 = bf16[8192,96]{1,0:T(8,128)(2,1)} reduce(bf16[8192,1,96]{2,1,0:T(2,128)(2,1)} %bitcast.423, bf16[]{:T(256)} %broadcast.559), dimensions={1}, to_apply=%bitcast.309.reduce_sub_computation | reduce | bytes 3145730
  626.3 11.6 multiply_convert_fusion.3
  645.1 9.0 copy.360
  668.3 9.0 copy.367
  688.1 18.9 convolution_add_fusion
  716.5 10.3 fusion.2
  726.8 13.5 fusion.136
  743.8 10.8 fusion.131
  754.6 12.3 fusion.146
  775.8 10.6 fusion.42
  786.5 13.4 convert_reduce_fusion.1
  800.0 11.0 fusion.129
  810.9 10.6 multiply_reduce_fusion.3
  821.5 10.9 multiply_convert_fusion.4
  834.1 8.7 fusion.157
  842.8 20.3 fusion.4
  911.4 16.5 convolution_convert_fusion
  945.2 18.4 fusion.133
  963.5 12.2 reshape.1022
  983.4 9.0 fusion.109
  998.5 13.3 convert_reduce_fusion.2
  1012.4 8.7 convolution_bitcast_fusion
  1090.3 9.1 fusion.14
  1143.2 47.8 %fusion.152 = f32[96,16,1,64]{3,2,1,0:T(1,128)} fusion(f32[96,16,64,1]{2,3,1,0:T(1,128)} %bitcast.466, f32[96,16,64,64]{3,2,1,0:T(8,128)} %copy.439), kind=kOutput, calls=%fused_computation.321 | convolution fusion | flops 75497472 | bytes 25952256 | tf_op jit(solution)/shard_map/transpose(jvp(chbk,chrk->chrb))/dot_general | solution.py:84
  1191.0 47.7 %fusion.151 = f32[96,16,1,64]{3,2,1,0:T(1,128)} fusion(f32[96,16,64,1]{2,3,1,0:T(1,128)S(1)} %bitcast.465, f32[96,16,64,64]{3,2,1,0:T(8,128)} %copy.439), kind=kOutput, calls=%fused_computation.320 | convolution fusion | flops 75497472 | bytes 25952256 | tf_op jit(solution)/shard_map/transpose(jvp(chbk,chrk->chrb))/dot_general | solution.py:84
  1272.1 10.6 fusion.24
  1282.7 9.4 copy.380
  1292.1 45.2 %reduce.33 = bf16[8192,96]{1,0:T(8,128)(2,1)S(1)} reduce(bf16[8192,1,96]{2,1,0:T(2,128)(2,1)} %bitcast.426, bf16[]{:T(256)} %broadcast.559), dimensions={1}, to_apply=%bitcast.315.reduce_sub_computation | reduce | bytes 3145730
  1348.3 8.8 pad.46
  1357.1 13.4 reshape.1013
  1370.5 10.4 pad.47
  1381.0 13.1 copy.462
  1400.1 13.2 reshape.1011
  1413.3 10.3 pad.43
  1423.6 13.0 copy.461
  1436.6 9.9 bitcast_reduce_fusion
  1468.4 20.1 multiply_reduce_fusion
  1494.7 51.6 %dynamic-update-slice.10 = f32[4,1809216]{1,0:T(4,128)} dynamic-update-slice(f32[4,1809216]{1,0:T(4,128)} %dynamic-update-slice.9, f32[4,614400]{1,0:T(4,128)} %reshape.1022, s32[]{} %constant.134, s32[]{} %constant.139) | dynamic-update-slice | bytes 19660804
  1547.8 25.7 dynamic-update-slice.12
  1592.7 84.3 %reshape.1140 = f32[7236864]{0:T(1024)} reshape(f32[4,1809216]{1,0:T(4,128)} %constant_dynamic-update-slice_fusion) | data formatting | bytes 57894912
  1676.9 38.2 %reshape.1037 = f32[4,8,226152]{2,1,0:T(8,128)} reshape(f32[7236864]{0:T(1024)} %reshape.1140) | data formatting | bytes 57894912 | tf_op jit(solution)/shard_map/reshape | solution.py:449
  1715.1 22.1 copy.419
  1737.2 33.8 %reshape.1038 = f32[32,226152]{1,0:T(8,128)} reshape(f32[8,4,226152]{2,1,0:T(4,128)} %copy.419) | data formatting | bytes 57894912 | tf_op jit(solution)/shard_map/reshape | solution.py:451
  1771.0 464.2 %all-reduce.20 = bf16[32,226152]{1,0:T(8,128)(2,1)} all-reduce(f32[32,226152]{1,0:T(8,128)} %reshape.1038), channel_id=2, replica_groups=mesh['seq'=8,'wsh'=4] {'seq','wsh'}, use_global_device_ids=true, to_apply=%region_40.41.clone | all-reduce | flops 7236864 | bytes 43421184
  2245.3 45.2 %reduce.32 = bf16[8192,96]{1,0:T(8,128)(2,1)S(1)} reduce(bf16[8192,1,96]{2,1,0:T(2,128)(2,1)} %bitcast.421, bf16[]{:T(256)} %broadcast.559), dimensions={1}, to_apply=%bitcast.313.reduce_sub_computation | reduce | bytes 3145730
  2318.2 55.8 %all-to-all-done.7 = bf16[8,2,49152]{2,1,0:T(2,128)(2,1)S(1)} async-done(((bf16[8,2,49152]{2,1,0:T(2,128)(2,1)}), bf16[8,2,49152]{2,1,0:T(2,128)(2,1)S(1)}, u32[]{:S(2)}, u32[]{:S(2)}) %all-to-all-start.7) | async-done | bytes 1572896 | tf_op jit(solution)/shard_map/all_to_all | solution.py:424
  2390.9 14.3 add_convert_fusion
  2405.2 67.3 %convert_reduce_fusion.3 = f32[8,226152]{1,0:T(8,128)} fusion(bf16[8,1,226152]{2,1,0:T(2,128)(2,1)} %all-gather.27.cloned.1.call-done), kind=kLoop, calls=%fused_computation.28 | loop fusion | flops 1809216 | bytes 10855296 | tf_op jit(solution)/shard_map/convert_element_type | solution.py:456
  2472.5 10.3 reshape.1039
  2498.1 55.7 %slice.208 = f32[113076,16]{1,0:T(8,128)} reshape(f32[8,226152]{1,0:T(8,128)} %convert_reduce_fusion.3) | data formatting | bytes 14473728 | tf_op jit(solution)/shard_map/slice | solution.py:463
  2553.7 692.7 %slice.218 = f32[904608,2]{1,0:T(8,128)} reshape(f32[8,226152]{1,0:T(8,128)} %convert_reduce_fusion.3) | data formatting | bytes 14473728 | tf_op jit(solution)/shard_map/slice | solution.py:463
  (640 shorter events, 630.4 us)
Async XLA Ops:
  7.2 619.1 %all-gather.19.cloned.1.call-start = ((), (), s32[]{:S(2)}) async-start(), calls=%async_computation.9 | async-start | bytes 2949120 | tf_op jit(solution)/shard_map/all_gather | solution.py:147
  7.9 680.1 %all-gather.17.cloned.1.call-start = ((), (), s32[]{:S(2)}) async-start(), calls=%async_computation.8 | async-start | bytes 6144000 | tf_op jit(solution)/shard_map/all_gather | solution.py:145
  8.7 718.1 %all-gather.21.cloned.1.call-start = ((), (), s32[]{:S(2)}) async-start(), calls=%async_computation.10 | async-start | bytes 2949120 | tf_op jit(solution)/shard_map/all_gather | solution.py:152
  13.2 21.7 copy-start.107
  13.2 27.0 copy-start.108
  13.2 32.3 copy-start.109
  15.1 35.7 %copy-start.125 = (bf16[192]{0:T(256)(128)(2,1)S(1)}, bf16[192]{0:T(256)(128)(2,1)}, u32[]{:S(2)}) copy-start(bf16[192]{0:T(256)(128)(2,1)} %param.29) | copy-start | bytes 1156
  15.1 35.9 %copy-start.126 = (bf16[192]{0:T(256)(128)(2,1)S(1)}, bf16[192]{0:T(256)(128)(2,1)}, u32[]{:S(2)}) copy-start(bf16[192]{0:T(256)(128)(2,1)} %param.43) | copy-start | bytes 1156
  15.1 36.2 %copy-start.127 = (bf16[64]{0:T(256)(128)(2,1)S(1)}, bf16[64]{0:T(256)(128)(2,1)}, u32[]{:S(2)}) copy-start(bf16[64]{0:T(256)(128)(2,1)} %param.36) | copy-start | bytes 388
  15.1 36.4 %copy-start.128 = (bf16[32]{0:T(256)(128)(2,1)S(1)}, bf16[32]{0:T(256)(128)(2,1)}, u32[]{:S(2)}) copy-start(bf16[32]{0:T(256)(128)(2,1)} %param.35) | copy-start | bytes 196
  15.2 36.6 %copy-start.116 = (bf16[800]{0:T(1024)(128)(2,1)S(1)}, bf16[800]{0:T(1024)(128)(2,1)}, u32[]{:S(2)}) copy-start(bf16[800]{0:T(1024)(128)(2,1)} %param.31) | copy-start | bytes 4804
  18.3 55.3 %all-to-all-start.2 = ((bf16[8,2,49152]{2,1,0:T(2,128)(2,1)}), bf16[8,2,49152]{2,1,0:T(2,128)(2,1)S(1)}, u32[]{:S(2)}, u32[]{:S(2)}) async-start(bf16[8,2,49152]{2,1,0:T(2,128)(2,1)} %reshape.1142), calls=%async_computation.2 | async-start | bytes 3145728 | tf_op jit(solution)/shard_map/all_to_all | solution.py:223
  25.6 718.2 %all-gather.23.cloned.1.call-start = ((), (), s32[]{:S(2)}) async-start(), calls=%async_computation.11 | async-start | bytes 2949120 | tf_op jit(solution)/shard_map/all_gather | solution.py:155
  34.8 30.7 copy-start.67
  40.2 25.4 copy-start.68
  64.7 371.3 %copy-start.104 = (f32[96]{0:T(128)}, f32[96]{0:T(128)S(1)}, u32[]{:S(2)}) copy-start(f32[96]{0:T(128)S(1)} %dynamic_slice.19) | copy-start | bytes 1156
  64.8 73.0 %copy-start.70 = (f32[96,16]{0,1:T(8,128)}, f32[96,16]{0,1:T(8,128)S(1)}, u32[]{:S(2)}) copy-start(f32[96,16]{0,1:T(8,128)S(1)} %get-tuple-element.259) | copy-start | bytes 18436
  64.9 362.6 %copy-start.50 = (f32[96,16]{1,0:T(8,128)}, f32[96,16]{1,0:T(8,128)S(1)}, u32[]{:S(2)}) copy-start(f32[96,16]{1,0:T(8,128)S(1)} %copy.353) | copy-start | bytes 18436
  65.4 158.1 %copy-start.59 = (f32[96,16]{1,0:T(8,128)}, f32[96,16]{1,0:T(8,128)S(1)}, u32[]{:S(2)}) copy-start(f32[96,16]{1,0:T(8,128)S(1)} %copy.356) | copy-start | bytes 18436
  65.5 362.0 %copy-start.57 = (f32[96,16]{1,0:T(8,128)}, f32[96,16]{1,0:T(8,128)S(1)}, u32[]{:S(2)}) copy-start(f32[96,16]{1,0:T(8,128)S(1)} %copy.357) | copy-start | bytes 18436
  73.7 136.2 %all-to-all-start = ((bf16[8,2,49152]{2,1,0:T(2,128)(2,1)}), bf16[8,2,49152]{2,1,0:T(2,128)(2,1)}, u32[]{:S(2)}, u32[]{:S(2)}) async-start(bf16[8,2,49152]{2,1,0:T(2,128)(2,1)} %reshape.1146), calls=%async_computation | async-start | bytes 3145728 | tf_op jit(solution)/shard_map/all_to_all | solution.py:223
  200.4 23.1 copy-start.113
  200.4 227.0 %copy-start.102 = (f32[128]{0:T(128)}, f32[128]{0:T(128)S(1)}, u32[]{:S(2)}) copy-start(f32[128]{0:T(128)S(1)} %iota_add_fusion.1) | copy-start | bytes 1540
  220.9 197.6 %copy-start.5 = (bf16[96,64,128]{2,1,0:T(8,128)(2,1)}, bf16[96,64,128]{2,1,0:T(8,128)(2,1)S(1)}, u32[]{:S(2)}) copy-start(bf16[96,64,128]{2,1,0:T(8,128)(2,1)S(1)} %reshape.990) | copy-start | bytes 4718596
  223.5 94.5 %copy-start.40 = (f32[96,16,64]{2,1,0:T(8,128)}, f32[96,16,64]{2,1,0:T(8,128)S(1)}, u32[]{:S(2)}) copy-start(f32[96,16,64]{2,1,0:T(8,128)S(1)} %fusion.73) | copy-start | bytes 1179652
  226.1 91.8 %copy-start.39 = (f32[96,16,64]{2,1,0:T(8,128)}, f32[96,16,64]{2,1,0:T(8,128)S(1)}, u32[]{:S(2)}) copy-start(f32[96,16,64]{2,1,0:T(8,128)S(1)} %fusion.71) | copy-start | bytes 1179652
  318.0 82.6 %copy-start.17 = (bf16[768,1,1024]{2,0,1:T(8,128)(2,1)S(1)}, bf16[768,1,1024]{2,0,1:T(8,128)(2,1)}, u32[]{:S(2)}) copy-start(bf16[768,1,1024]{2,0,1:T(8,128)(2,1)} %copy-done.16) | copy-start | bytes 4718596
  452.0 60.7 %copy-start.119 = (bf16[384]{0:T(512)(128)(2,1)S(1)}, bf16[384]{0:T(512)(128)(2,1)}, u32[]{:S(2)}) copy-start(bf16[384]{0:T(512)(128)(2,1)} %param.33) | copy-start | bytes 2308
  452.0 60.7 %copy-start.120 = (bf16[384]{0:T(512)(128)(2,1)S(1)}, bf16[384]{0:T(512)(128)(2,1)}, u32[]{:S(2)}) copy-start(bf16[384]{0:T(512)(128)(2,1)} %param.41) | copy-start | bytes 2308
  452.0 60.8 %copy-start.123 = (bf16[32,2]{0,1:T(2,128)(2,1)S(1)}, bf16[32,2]{0,1:T(2,128)(2,1)}, u32[]{:S(2)}) copy-start(bf16[32,2]{0,1:T(2,128)(2,1)} %param.34) | copy-start | bytes 388
  452.0 65.9 %copy-start.117 = (bf16[192,2]{0,1:T(2,128)(2,1)S(1)}, bf16[192,2]{0,1:T(2,128)(2,1)}, u32[]{:S(2)}) copy-start(bf16[192,2]{0,1:T(2,128)(2,1)} %param.38) | copy-start | bytes 2308
  452.0 71.3 %copy-start.118 = (bf16[192,2]{0,1:T(2,128)(2,1)S(1)}, bf16[192,2]{0,1:T(2,128)(2,1)}, u32[]{:S(2)}) copy-start(bf16[192,2]{0,1:T(2,128)(2,1)} %param.39) | copy-start | bytes 2308
  452.0 86.7 %copy-start.115 = (s32[2,1]{0,1:T(1,128)S(1)}, s32[2,1]{0,1:T(1,128)}, u32[]{:S(2)}) copy-start(s32[2,1]{0,1:T(1,128)} %param.24) | copy-start | bytes 28
  452.0 86.8 %copy-start.11 = (bf16[2,1,1024,768]{3,2,1,0:T(8,128)(2,1)S(1)}, bf16[2,1,1024,768]{3,2,1,0:T(8,128)(2,1)}, u32[]{:S(2)}) copy-start(bf16[2,1,1024,768]{3,2,1,0:T(8,128)(2,1)} %param.23) | copy-start | bytes 9437188
  506.1 97.9 %all-to-all-start.1 = ((bf16[8,2,49152]{2,1,0:T(2,128)(2,1)}), bf16[8,2,49152]{2,1,0:T(2,128)(2,1)}, u32[]{:S(2)}, u32[]{:S(2)}) async-start(bf16[8,2,49152]{2,1,0:T(2,128)(2,1)} %reshape.1148), calls=%async_computation.1 | async-start | bytes 3145728 | tf_op jit(solution)/shard_map/all_to_all | solution.py:225
  512.1 242.5 %all-gather.25.cloned.1.call-start = ((), (), s32[]{:S(2)}) async-start(), calls=%async_computation.12 | async-start | bytes 2949120 | tf_op jit(solution)/shard_map/all_gather | solution.py:157
  538.7 282.8 %copy-start.99 = (f32[768]{0:T(1024)}, f32[768]{0:T(1024)S(1)}, u32[]{:S(2)}) copy-start(f32[768]{0:T(1024)S(1)} %get-tuple-element.201) | copy-start | bytes 9220
  596.7 22.4 copy-start.7
  604.0 57.1 %all-to-all-start.3 = ((bf16[8,2,49152]{2,1,0:T(2,128)(2,1)}), bf16[8,2,49152]{2,1,0:T(2,128)(2,1)}, u32[]{:S(2)}, u32[]{:S(2)}) async-start(bf16[8,2,49152]{2,1,0:T(2,128)(2,1)} %reshape.1144), calls=%async_computation.3 | async-start | bytes 3145728 | tf_op jit(solution)/shard_map/all_to_all | solution.py:225
  688.1 22.0 slice-start.4
  688.1 22.0 slice-start.5
  740.3 81.2 %copy-start.77 = (f32[2048]{0:T(1024)}, f32[2048]{0:T(1024)S(1)}, u32[]{:S(2)}) copy-start(f32[2048]{0:T(1024)S(1)} %broadcast_multiply_fusion.4) | copy-start | bytes 24580
  743.8 77.8 %copy-start.87 = (f32[2048]{0:T(1024)}, f32[2048]{0:T(1024)S(1)}, u32[]{:S(2)}) copy-start(f32[2048]{0:T(1024)S(1)} %add_rsqrt_fusion.1) | copy-start | bytes 24580
  775.8 24.1 slice-start.8
  938.5 53.9 %all-to-all-start.4 = ((bf16[8,2,49152]{2,1,0:T(2,128)(2,1)}), bf16[8,2,49152]{2,1,0:T(2,128)(2,1)}, u32[]{:S(2)}, u32[]{:S(2)}) async-start(bf16[8,2,49152]{2,1,0:T(2,128)(2,1)} %reshape.1154), calls=%async_computation.4 | async-start | bytes 3145728 | tf_op jit(solution)/shard_map/all_to_all | solution.py:415
  992.4 51.9 %all-to-all-start.6 = ((bf16[8,2,49152]{2,1,0:T(2,128)(2,1)}), bf16[8,2,49152]{2,1,0:T(2,128)(2,1)}, u32[]{:S(2)}, u32[]{:S(2)}) async-start(bf16[8,2,49152]{2,1,0:T(2,128)(2,1)} %reshape.1150), calls=%async_computation.6 | async-start | bytes 3145728 | tf_op jit(solution)/shard_map/all_to_all | solution.py:415
  1080.5 39.6 %copy-start.9 = (f32[96,64,128]{2,1,0:T(8,128)}, f32[96,64,128]{2,1,0:T(8,128)S(1)}, u32[]{:S(2)}) copy-start(f32[96,64,128]{2,1,0:T(8,128)S(1)} %get-tuple-element.271) | copy-start | bytes 9437188
  1080.5 24.9 slice-start.1
  1084.3 21.1 slice-start.2
  1143.2 47.8 %copy-start.49 = (f32[96,16,1,64]{3,1,0,2:T(8,128)S(1)}, f32[96,16,1,64]{3,1,0,2:T(8,128)}, u32[]{:S(2)}) copy-start(f32[96,16,1,64]{3,1,0,2:T(8,128)} %get-tuple-element.288) | copy-start | bytes 1179652
  1342.3 953.3 %all-to-all-start.5 = ((bf16[8,2,49152]{2,1,0:T(2,128)(2,1)}), bf16[8,2,49152]{2,1,0:T(2,128)(2,1)}, u32[]{:S(2)}, u32[]{:S(2)}) async-start(bf16[8,2,49152]{2,1,0:T(2,128)(2,1)} %reshape.1156), calls=%async_computation.5 | async-start | bytes 3145728 | tf_op jit(solution)/shard_map/all_to_all | solution.py:424
  1348.2 1056.9 %all-gather.27.cloned.1.call-start = ((), (), s32[]{:S(2)}) async-start(), calls=%async_computation.13 | async-start | bytes 8142336 | tf_op jit(solution)/shard_map/all_gather | solution.py:455
  1370.5 23.5 slice-start.6
  1446.4 21.9 copy-start.71
  1462.9 25.6 copy-start.73
  1468.4 21.3 copy-start.75
  1494.6 51.6 %copy-start.81 = (f32[4,800]{1,0:T(4,128)S(1)}, f32[4,800]{1,0:T(4,128)}, u32[]{:S(2)}) copy-start(f32[4,800]{1,0:T(4,128)} %reshape.1023) | copy-start | bytes 38404
  1546.2 27.3 copy-start.94
  1546.2 28.9 copy-start.111
  1546.3 30.3 copy-start.110
  1546.3 31.7 copy-start.112
  1771.0 467.5 %copy-start.43 = (bf16[96,1,8192]{2,0,1:T(8,128)(2,1)S(1)}, bf16[96,1,8192]{2,0,1:T(8,128)(2,1)}, u32[]{:S(2)}) copy-start(bf16[96,1,8192]{2,0,1:T(8,128)(2,1)} %get-tuple-element.269) | copy-start | bytes 4718596
  2295.5 78.4 %all-to-all-start.7 = ((bf16[8,2,49152]{2,1,0:T(2,128)(2,1)}), bf16[8,2,49152]{2,1,0:T(2,128)(2,1)S(1)}, u32[]{:S(2)}, u32[]{:S(2)}) async-start(bf16[8,2,49152]{2,1,0:T(2,128)(2,1)} %reshape.1152), calls=%async_computation.7 | async-start | bytes 3145728 | tf_op jit(solution)/shard_map/all_to_all | solution.py:424
  2553.7 696.1 %copy-start.34 = (f32[614400]{0:T(1024)S(1)}, f32[614400]{0:T(1024)}, u32[]{:S(2)}) copy-start(f32[614400]{0:T(1024)} %slice.254) | copy-start | bytes 7372804
  (94 other events, 801.1 us)
Sparse Core Ops, SparseCore 0:
  9.6 26.9 all-gather.18
  38.1 38.9 all-gather.16
  78.7 24.0 all-gather.20
  104.3 24.0 all-gather.22
  514.2 24.7 all-gather.24
  2238.6 139.7 all-gather.26
where the time goes:
time: 3290 us; the launch traced here: 3270 us
  local copies, waits for them, and re-layouts  1620 us (49%)
  matrix products  595 us (18%)
  blocking collectives  523 us (16%)
  other arithmetic  405 us (12%)
  waiting for transfers between devices  59 us (2%)
  starting transfers between devices  47.9 us (1%)
    slice x13, local copies, waits for them, and re-layouts, body(): final.append(summed[start_at:start_at + piece_size].reshape(member.shape))  766 us
    unnamed x2, blocking collectives  477 us
    unnamed x359, local copies, waits for them, and re-layouts  353 us
    dot_general x4, matrix products, ema_local(): jnp.einsum('chbk,chrk->chrb', reach_table, block_input, precision=HIGHEST)  261 us
    unnamed x15, other arithmetic  191 us
    dot_general x5, matrix products, dot_back(): jnp.einsum('rj,ij->ri', grad_rows, weight, preferred_element_type=jnp.flo...  75.1 us
    convert_element_type x1, other arithmetic, body(): summed = lax.all_gather(mine.astype(jnp.bfloat16), 'seq', axis=0, tiled=T...  67.3 us
    dot_general x5, matrix products, dot_plain(): return jnp.dot(left_op, right_op, preferred_element_type=jnp.float32)  67.1 us
  transfers between devices with their start and end apart: 14, of which 1 were waited for; matrix products, arithmetic and copies ran while one was open for 39% of the time, Pallas kernels for 0%

commit v1 on v0

v1 whole, which is shorter than its diff:
```python
import functools

import jax
import jax.numpy as jnp
from jax import lax
from jax.experimental import pallas as pl
from jax.experimental.pallas import tpu as pltpu
from jax.sharding import PartitionSpec as P

BLOCK = 128
LANES = 128
CH = 8
PAD = 8
CHUNK = 768
STRIP = 32
EPSILON = 1e-05
VMEM_LIMIT = 62 * 1024 * 1024
F32 = jnp.float32
BF16 = jnp.bfloat16


def dot_rows(left_op, right_op):
    return jnp.einsum("ri,rj->ij", left_op, right_op, preferred_element_type=jnp.float32)


def skew_matrix(wrapped):
    lead = wrapped.shape[:-1]
    flat = jnp.tile(wrapped, (1,) * len(lead) + (BLOCK,))[..., : BLOCK * (2 * BLOCK - 1)]
    return flat.reshape(lead + (BLOCK, 2 * BLOCK - 1))[..., :BLOCK]


def power(v, n):
    k = 1
    while k < n:
        v = v * v
        k *= 2
    return v

def rows_of(scr, s, T):
    return scr[pl.ds(s, CH, stride=T+PAD), :]

def spread(scr, v, T):
    for k in range(CH):
        scr[k*(T+PAD):k*(T+PAD)+T, :] = v[k*T:(k+1)*T, :]

def collect(scr, T):
    return jnp.concatenate([scr[k*(T+PAD):k*(T+PAD)+T, :] for k in range(CH)], axis=0)

def ends_kernel(H, T, x_ref, q_ref, e_ref, s_ref, scr):
    spread(scr, x_ref[0].astype(F32), T)
    q = [jnp.broadcast_to(q_ref[h:h+1, :], (CH, LANES)) for h in range(H)]
    def step(s, st):
        xs = rows_of(scr, s, T)
        return tuple(q[h]*st[h] + xs for h in range(H))
    st = lax.fori_loop(0, T, step, tuple(jnp.zeros((CH,LANES),F32) for _ in range(H)), unroll=8)
    for h in range(H):
        e_ref[0, h*CH:(h+1)*CH, :] = st[h]
    qT = power(q_ref[...], T)
    c = jnp.zeros((H,LANES),F32)
    for k in range(CH):
        c = qT*c + e_ref[0, pl.ds(k,H,stride=CH), :]
    s_ref[0] = c

def fwd_kernel(H, T, x_ref, q_ref, w_ref, om_ref, e_ref, c_ref, xp_ref, p_ref, f_ref, scr, cs, ps):
    spread(scr, x_ref[0].astype(F32), T)
    qT = power(q_ref[...], T)
    c = c_ref[0]
    for k in range(CH):
        cs[pl.ds(k,H,stride=CH), :] = c
        c = qT*c + e_ref[0, pl.ds(k,H,stride=CH), :]
    q = [jnp.broadcast_to(q_ref[h:h+1, :], (CH, LANES)) for h in range(H)]
    w = [jnp.broadcast_to(w_ref[h:h+1, :], (CH, LANES)) for h in range(H)]
    om = jnp.broadcast_to(om_ref[...], (CH,LANES))
    def step(s, st):
        xs = rows_of(scr, s, T)
        st = tuple(q[h]*st[h] + xs for h in range(H))
        terms = [w[h]*st[h] for h in range(H)]
        while len(terms) > 1:
            terms = [terms[i]+terms[i+1] for i in range(0,len(terms)-1,2)] + ([terms[-1]] if len(terms)%2 else [])
        ps[pl.ds(s, CH, stride=T+PAD), :] = terms[0] + om*xs
        return st
    st = lax.fori_loop(0, T, step, tuple(cs[h*CH:(h+1)*CH, :] for h in range(H)), unroll=8)
    for h in range(H):
        f_ref[0, h*CH:(h+1)*CH, :] = st[h]
    p = collect(ps, T)
    p_ref[0] = p
    xp_ref[0] = (p*jax.nn.sigmoid(p)).astype(xp_ref.dtype)

def bends_kernel(H, T, dxp_ref, p_ref, q_ref, d_ref, e_ref, s_ref, ds):
    p = p_ref[0]
    sg = jax.nn.sigmoid(p)
    d = dxp_ref[0].astype(F32) * (sg*(1.0+p*(1.0-sg)))
    d_ref[0] = d
    spread(ds, d, T)
    q = [jnp.broadcast_to(q_ref[h:h+1, :], (CH, LANES)) for h in range(H)]
    def step(s, st):
        xs = rows_of(ds, T-1-s, T)
        return tuple(q[h]*st[h] + xs for h in range(H))
    st = lax.fori_loop(0, T, step, tuple(jnp.zeros((CH,LANES),F32) for _ in range(H)), unroll=8)
    for h in range(H):
        e_ref[0, h*CH:(h+1)*CH, :] = st[h]
    qT = power(q_ref[...], T)
    c = jnp.zeros((H,LANES),F32)
    for k in reversed(range(CH)):
        c = qT*c + e_ref[0, pl.ds(k,H,stride=CH), :]
    s_ref[0] = c

def bwd_kernel(H, T, d_ref, x_ref, q_ref, qi_ref, w_ref, om_ref, f_ref, e_ref, c_ref, dx_ref, s1_ref, s3_ref, go_ref, scr, cs, dx, ds):
    g = pl.program_id(1)
    x = x_ref[0].astype(F32)
    spread(scr, x, T)
    dv = d_ref[0]
    spread(ds, dv, T)
    qT = power(q_ref[...], T)
    c = c_ref[0]
    for k in reversed(range(CH)):
        cs[pl.ds(k,H,stride=CH), :] = c
        c = qT*c + e_ref[0, pl.ds(k,H,stride=CH), :]
    om = jnp.broadcast_to(om_ref[...], (CH,LANES))
    HH = H//2
    zero = jnp.zeros((CH,LANES),F32)
    @pl.when(g==0)
    def _():
        go_ref[...] = jnp.zeros_like(go_ref)
        s1_ref[...] = jnp.zeros_like(s1_ref)
        s3_ref[...] = jnp.zeros_like(s3_ref)
    go_ref[...] += jnp.sum(dv*x, axis=0, keepdims=True)
    for half in range(2):
        hs = range(half*HH, half*HH+HH)
        q = [jnp.broadcast_to(q_ref[h:h+1, :], (CH, LANES)) for h in hs]
        qi = [jnp.broadcast_to(qi_ref[h:h+1, :], (CH, LANES)) for h in hs]
        w = [jnp.broadcast_to(w_ref[h:h+1, :], (CH, LANES)) for h in hs]
        def step(s, carry):
            l, st, a1, a3 = carry
            at = pl.ds(T-1-s, CH, stride=T+PAD)
            d = ds[at, :]
            xs = scr[at, :]
            a1 = tuple(a1[i] + d*st[i] for i in range(HH))
            l = tuple(q[i]*l[i] + d for i in range(HH))
            st = tuple((st[i]-xs)*qi[i] for i in range(HH))
            a3 = tuple(a3[i] + l[i]*st[i] for i in range(HH))
            terms = [w[i]*l[i] for i in range(HH)]
            while len(terms) > 1:
                terms = [terms[i]+terms[i+1] for i in range(0,len(terms)-1,2)]
            if half == 0:
                dx[at, :] = terms[0] + om*d
            else:
                dx[at, :] = dx[at, :] + terms[0]
            return l, st, a1, a3
        init = (tuple(cs[h*CH:(h+1)*CH,:] for h in hs), tuple(f_ref[0,h*CH:(h+1)*CH,:] for h in hs), (zero,)*HH, (zero,)*HH)
        l, st, a1, a3 = lax.fori_loop(0, T, step, init, unroll=4)
        for i,h in enumerate(hs):
            s1_ref[h:h+1,:] += jnp.sum(a1[i],axis=0,keepdims=True)
            s3_ref[h:h+1,:] += jnp.sum(a3[i],axis=0,keepdims=True)
    dx_ref[0] = collect(dx, T).astype(dx_ref.dtype)

def specs(L,H):
    blk = pl.BlockSpec((1,L,LANES), lambda c,g:(g,0,c))
    par = pl.BlockSpec((H,LANES), lambda c,g:(0,c))
    one = pl.BlockSpec((1,LANES), lambda c,g:(0,c))
    st = pl.BlockSpec((1,H*CH,LANES), lambda c,g:(g,0,c))
    car = pl.BlockSpec((1,H,LANES), lambda c,g:(g,0,c))
    return blk,par,one,st,car

def ema_ends(x,q):
    G,L,C=x.shape; H=q.shape[0]
    blk,par,one,st,car=specs(L,H)
    return pl.pallas_call(functools.partial(ends_kernel,H,L//CH), grid=(C//LANES,G), in_specs=[blk,par], out_specs=[st,car],
      out_shape=[jax.ShapeDtypeStruct((G,H*CH,C),F32),jax.ShapeDtypeStruct((G,H,C),F32)], scratch_shapes=[pltpu.VMEM((L+CH*PAD,LANES),F32)], name="ema_ends")(x,q)

def ema_forward(x,q,w,om,e,c):
    G,L,C=x.shape; H=q.shape[0]
    blk,par,one,st,car=specs(L,H)
    return pl.pallas_call(functools.partial(fwd_kernel,H,L//CH), grid=(C//LANES,G), in_specs=[blk,par,par,one,st,car], out_specs=[blk,blk,st],
      out_shape=[jax.ShapeDtypeStruct((G,L,C),jnp.bfloat16),jax.ShapeDtypeStruct((G,L,C),F32),jax.ShapeDtypeStruct((G,H*CH,C),F32)],
      scratch_shapes=[pltpu.VMEM((L+CH*PAD,LANES),F32),pltpu.VMEM((H*CH,LANES),F32),pltpu.VMEM((L+CH*PAD,LANES),F32)], name="ema_fwd")(x,q,w,om,e,c)

def ema_back_ends(dxp,p,q):
    G,L,C=p.shape; H=q.shape[0]
    blk,par,one,st,car=specs(L,H)
    return pl.pallas_call(functools.partial(bends_kernel,H,L//CH), grid=(C//LANES,G), in_specs=[blk,blk,par], out_specs=[blk,st,car],
      out_shape=[jax.ShapeDtypeStruct((G,L,C),F32),jax.ShapeDtypeStruct((G,H*CH,C),F32),jax.ShapeDtypeStruct((G,H,C),F32)], scratch_shapes=[pltpu.VMEM((L+CH*PAD,LANES),F32)], name="ema_bends")(dxp,p,q)

def ema_backward(d,x,q,qi,w,om,f,e,c):
    G,L,C=x.shape; H=q.shape[0]
    blk,par,one,st,car=specs(L,H)
    return pl.pallas_call(functools.partial(bwd_kernel,H,L//CH), grid=(C//LANES,G), in_specs=[blk,blk,par,par,par,one,st,st,car], out_specs=[blk,par,par,one],
      out_shape=[jax.ShapeDtypeStruct((G,L,C),jnp.bfloat16),jax.ShapeDtypeStruct((H,C),F32),jax.ShapeDtypeStruct((H,C),F32),jax.ShapeDtypeStruct((1,C),F32)],
      scratch_shapes=[pltpu.VMEM((L+CH*PAD,LANES),F32),pltpu.VMEM((H*CH,LANES),F32),pltpu.VMEM((L+CH*PAD,LANES),F32),pltpu.VMEM((L+CH*PAD,LANES),F32)], name="ema_bwd")(d,x,q,qi,w,om,f,e,c)


def sig(v):
    return 0.5 * jnp.tanh(0.5 * v) + 0.5


def dot_nn(left_op, right_op):
    return jnp.dot(left_op, right_op, preferred_element_type=F32)


def dot_nt(left_op, right_op):
    return lax.dot_general(left_op, right_op, (((1,), (1,)), ((), ())), preferred_element_type=F32)


def dot_tn(left_op, right_op):
    return lax.dot_general(left_op, right_op, (((0,), (0,)), ((), ())), preferred_element_type=F32)


def piece_copies(pieces, target, sem, first):
    own, core, across, across_y, across_core, across_y_core = pieces
    rows = own.shape[0]
    half = across.shape[0]
    j = lax.axis_index("wsh")
    i = lax.axis_index("seq")
    bit = lax.rem(i, 2)
    spots = (
        (own, j * rows),
        (core, (j ^ 1) * rows),
        (across, (j ^ 2) * rows + bit * half),
        (across_y, (j ^ 2) * rows + (1 - bit) * half),
        (across_core, (j ^ 3) * rows + bit * half),
        (across_y_core, (j ^ 3) * rows + (1 - bit) * half),
    )
    copies = []
    for n, (piece, start) in enumerate(spots):
        size = piece.shape[0]
        copies.append(
            pltpu.make_async_copy(
                piece, target.at[pl.ds(pl.multiple_of(start, 32), size), :], sem.at[first + n]
            )
        )
    return copies


def bring(groups, sem):
    @pl.when(pl.program_id(0) == 0)
    def _():
        copies = []
        for n, (pieces, target) in enumerate(groups):
            copies.extend(piece_copies(pieces, target, sem, 6 * n))
        for copy in copies:
            copy.start()
        for copy in copies:
            copy.wait()


def fold(rows):
    total = rows[:8]
    for k in range(8, STRIP, 8):
        total = total + rows[k : k + 8]
    return total


def add_sums(ref, at, rows):
    ref[:, at] += jnp.sum(rows, axis=0, keepdims=True)


def mix_fwd_kernel(R, dims, x_ref, xp_ref, bm_ref, bv_ref, qk_ref, rel_ref, *refs):
    D, Z, V = dims
    pieces, refs = refs[:18], refs[18:]
    u_ref, h_ref, r_ref, v_ref, z_ref, p_ref, m_ref, wm, wv, wo, sem = refs
    bring(((pieces[:6], wm), (pieces[6:12], wv), (pieces[12:], wo)), sem)
    xp = xp_ref[...]
    x = x_ref[...]
    z = dot_nn(xp, wm[:, D : D + Z]) + bm_ref[:, D : D + Z]
    z_ref[...] = z
    shared = z * sig(z)
    query = (shared * qk_ref[0:1, :] + qk_ref[2:3, :]).astype(BF16)
    key = (shared * qk_ref[1:2, :]).astype(BF16)
    probs = []
    row = lax.broadcasted_iota(jnp.int32, (BLOCK, BLOCK), 0)
    col = lax.broadcasted_iota(jnp.int32, (BLOCK, BLOCK), 1)
    for b in range(R // BLOCK):
        at = slice(b * BLOCK, (b + 1) * BLOCK)
        score = dot_nt(query[at], key[at]) * Z ** (-0.5) + rel_ref[...]
        score = jnp.where(row >= col, score, -1e30)
        grown = jnp.exp(score - jnp.max(score, axis=-1, keepdims=True))
        prob = grown / jnp.sum(grown, axis=-1, keepdims=True)
        p_ref[at, :] = prob
        probs.append(prob.astype(BF16))
    for c in range(0, V, CHUNK):
        at = slice(c, c + CHUNK)
        rat = slice(D + Z + c, D + Z + c + CHUNK)
        v = dot_nn(x, wv[:, at]) + bv_ref[:, at]
        v_ref[:, at] = v
        value = (v * sig(v)).astype(BF16)
        r = dot_nn(xp, wm[:, rat]) + bm_ref[:, rat]
        r_ref[:, at] = r
        reset = r * sig(r)
        for b in range(R // BLOCK):
            rows = slice(b * BLOCK, (b + 1) * BLOCK)
            m_ref[rows, at] = (reset[rows] * dot_nn(probs[b], value[rows])).astype(BF16)
    u_ref[...] = dot_nn(xp, wm[:, :D]) + bm_ref[:, :D]
    h_ref[...] = dot_nn(xp, wm[:, D + Z + V :]) + bm_ref[:, D + Z + V :] + dot_nn(m_ref[...], wo[...])


def ffn_kernel(R, dims, x_ref, u_ref, h_ref, cot_ref, live_ref, gn_ref, bf_ref, bo_ref, *refs):
    D, FF = dims
    pieces, refs = refs[:12], refs[12:]
    (
        o_ref, h1_ref, act_ref, dg_ref, df_ref, dm_ref, du_ref, dt_ref, sd_ref, sf_ref,
        wi, wo, f_scr, n1_scr, a_scr, i1_scr, sem,
    ) = refs
    bring(((pieces[:6], wi), (pieces[6:], wo)), sem)

    @pl.when(pl.program_id(0) == 0)
    def _():
        sd_ref[...] = jnp.zeros_like(sd_ref)
        sf_ref[...] = jnp.zeros_like(sf_ref)

    g1, g2, b1, b2 = (gn_ref[k : k + 1, :] for k in range(4))

    def first(s, _):
        at = pl.ds(pl.multiple_of(s * STRIP, STRIP), STRIP)
        x = x_ref[at, :].astype(F32)
        h = h_ref[at, :]
        y = x + sig(u_ref[at, :]) * (h * sig(h) - x)
        center = y - jnp.mean(y, axis=-1, keepdims=True)
        inverse = lax.rsqrt(jnp.mean(center * center, axis=-1, keepdims=True) + EPSILON)
        n1 = center * inverse
        n1_scr[at, :] = n1
        i1_scr[at, :] = jnp.broadcast_to(inverse, (STRIP, 128))
        h1_ref[at, :] = (n1 * g1 + b1).astype(BF16)
        return 0

    lax.fori_loop(0, R // STRIP, first, 0, unroll=2)
    for c in range(0, FF, CHUNK):
        at = slice(c, c + CHUNK)
        f = dot_nn(h1_ref[...], wi[:, at]) + bf_ref[:, at]
        f_scr[:, at] = f
        act_ref[:, at] = (f * sig(f)).astype(BF16)
    a_scr[...] = dot_nn(act_ref[...], wo[...])

    def second(s, sums):
        at = pl.ds(pl.multiple_of(s * STRIP, STRIP), STRIP)
        y2 = n1_scr[at, :] * g1 + b1 + a_scr[at, :] + bo_ref[...]
        center = y2 - jnp.mean(y2, axis=-1, keepdims=True)
        inverse = lax.rsqrt(jnp.mean(center * center, axis=-1, keepdims=True) + EPSILON)
        n2 = center * inverse
        live = live_ref[at, :]
        o_ref[at, :] = ((n2 * g2 + b2) * live).astype(BF16)
        dn = cot_ref[at, :].astype(F32) * live
        w = dn * g2
        dy2 = inverse * (
            w - jnp.mean(w, axis=-1, keepdims=True) - n2 * jnp.mean(w * n2, axis=-1, keepdims=True)
        )
        a_scr[at, :] = dy2
        dg_ref[at, :] = dy2.astype(BF16)
        s_gain, s_shift, s_bias = sums
        return s_gain + fold(dn * n2), s_shift + fold(dn), s_bias + fold(dy2)

    zero = jnp.zeros((8, D), F32)
    s_gain, s_shift, s_bias = lax.fori_loop(0, R // STRIP, second, (zero, zero, zero), unroll=2)
    sd_ref[1:2, :] += jnp.sum(s_gain, axis=0, keepdims=True)
    sd_ref[3:4, :] += jnp.sum(s_shift, axis=0, keepdims=True)
    sd_ref[4:5, :] += jnp.sum(s_bias, axis=0, keepdims=True)
    for c in range(0, FF, CHUNK):
        at = slice(c, c + CHUNK)
        f = f_scr[:, at]
        s = sig(f)
        df = (dot_nt(dg_ref[...], wo[at, :]) * (s * (1.0 + f * (1.0 - s)))).astype(BF16)
        df_ref[:, at] = df
        add_sums(sf_ref, at, df.astype(F32))
    a_scr[...] += dot_nt(df_ref[...], wi[...])

    def third(k, sums):
        at = pl.ds(pl.multiple_of(k * STRIP, STRIP), STRIP)
        dh1 = a_scr[at, :]
        n1 = n1_scr[at, :]
        w = dh1 * g1
        dy = i1_scr[at, 0:1] * (
            w - jnp.mean(w, axis=-1, keepdims=True) - n1 * jnp.mean(w * n1, axis=-1, keepdims=True)
        )
        x = x_ref[at, :].astype(F32)
        h = h_ref[at, :]
        sh = sig(h)
        gate = sig(u_ref[at, :])
        rest = 1.0 - gate
        dyg = dy * gate
        dm_ref[at, :] = (dyg * (sh * (1.0 + h * (1.0 - sh)))).astype(BF16)
        du_ref[at, :] = (dyg * (h * sh - x) * rest).astype(BF16)
        dt_ref[at, :] = dy * rest
        s_gain, s_shift = sums
        return s_gain + fold(dh1 * n1), s_shift + fold(dh1)

    s_gain, s_shift = lax.fori_loop(0, R // STRIP, third, (zero, zero), unroll=2)
    sd_ref[0:1, :] += jnp.sum(s_gain, axis=0, keepdims=True)
    sd_ref[2:3, :] += jnp.sum(s_shift, axis=0, keepdims=True)


def mix_bwd_kernel(R, dims, dm_ref, du_ref, dt_ref, r_ref, v_ref, z_ref, p_ref, qk_ref, *refs):
    D, Z, V = dims
    pieces, refs = refs[:18], refs[18:]
    db_ref, dv_ref, dxp_ref, do_ref, sm_ref, sv_ref, sq_ref, ss_ref, wm, wv, wo, sem = refs
    bring(((pieces[:6], wm), (pieces[6:12], wv), (pieces[12:], wo)), sem)

    @pl.when(pl.program_id(0) == 0)
    def _():
        for ref in (sm_ref, sv_ref, sq_ref, ss_ref):
            ref[...] = jnp.zeros_like(ref)

    dm = dm_ref[...]
    du = du_ref[...]
    db_ref[:, :D] = du
    db_ref[:, D + Z + V :] = dm
    add_sums(sm_ref, slice(0, D), du.astype(F32))
    add_sums(sm_ref, slice(D + Z + V, 2 * D + Z + V), dm.astype(F32))
    blocks = [slice(b * BLOCK, (b + 1) * BLOCK) for b in range(R // BLOCK)]
    full = [p_ref[rows, :] for rows in blocks]
    probs = [prob.astype(BF16) for prob in full]
    dprob = [jnp.zeros((BLOCK, BLOCK), F32) for _ in blocks]
    for c in range(0, V, CHUNK):
        at = slice(c, c + CHUNK)
        rat = slice(D + Z + c, D + Z + c + CHUNK)
        dmix = dot_nt(dm, wo[at, :])
        r = r_ref[:, at]
        v = v_ref[:, at]
        sr = sig(r)
        sv = sig(v)
        value = (v * sv).astype(BF16)
        datt = (dmix * (r * sr)).astype(BF16)
        turned = dmix * (sr * (1.0 + r * (1.0 - sr)))
        slope = sv * (1.0 + v * (1.0 - sv))
        sum_r = jnp.zeros((1, CHUNK), F32)
        sum_v = jnp.zeros((1, CHUNK), F32)
        for b, rows in enumerate(blocks):
            dr = (turned[rows] * dot_nn(probs[b], value[rows])).astype(BF16)
            db_ref[rows, rat] = dr
            sum_r += jnp.sum(dr.astype(F32), axis=0, keepdims=True)
            dprob[b] += dot_nt(datt[rows], value[rows])
            dv = (dot_tn(probs[b], datt[rows]) * slope[rows]).astype(BF16)
            dv_ref[rows, at] = dv
            sum_v += jnp.sum(dv.astype(F32), axis=0, keepdims=True)
        sm_ref[:, rat] += sum_r
        sv_ref[:, at] += sum_v
    for b, rows in enumerate(blocks):
        z = z_ref[rows, :]
        sz = sig(z)
        shared = z * sz
        query = (shared * qk_ref[0:1, :] + qk_ref[2:3, :]).astype(BF16)
        key = (shared * qk_ref[1:2, :]).astype(BF16)
        inner = jnp.sum(full[b] * dprob[b], axis=-1, keepdims=True)
        ds = (full[b] * (dprob[b] - inner)).astype(BF16)
        ss_ref[...] += ds.astype(F32)
        dq = dot_nn(ds, key) * Z ** (-0.5)
        dk = dot_tn(ds, query) * Z ** (-0.5)
        sq_ref[0:1, :] += jnp.sum(dq * shared, axis=0, keepdims=True)
        sq_ref[1:2, :] += jnp.sum(dk * shared, axis=0, keepdims=True)
        sq_ref[2:3, :] += jnp.sum(dq, axis=0, keepdims=True)
        dz = (dq * qk_ref[0:1, :] + dk * qk_ref[1:2, :]) * (sz * (1.0 + z * (1.0 - sz)))
        dz = dz.astype(BF16)
        db_ref[rows, D : D + Z] = dz
        add_sums(sm_ref, slice(D, D + Z), dz.astype(F32))
    do_ref[...] = dt_ref[...] + dot_nt(dv_ref[...], wv[...])
    dxp_ref[...] = dot_nt(db_ref[...], wm[...]).astype(BF16)


def any_specs(n):
    return [pl.BlockSpec(memory_space=pl.ANY)] * n


def tile(R, n):
    return pl.BlockSpec((R, n), lambda t: (t, 0))


def fixed(r, n):
    return pl.BlockSpec((r, n), lambda t: (0, 0))


def shape(r, n, dtype=F32):
    return jax.ShapeDtypeStruct((r, n), dtype)


def mix_forward(R, x, xp, bm, bv, qk, rel, pieces):
    T, D = x.shape
    V = bv.shape[1]
    Z = qk.shape[1]
    E = bm.shape[1]
    return pl.pallas_call(
        functools.partial(mix_fwd_kernel, R, (D, Z, V)),
        grid=(T // R,),
        in_specs=[tile(R, D), tile(R, D), fixed(1, E), fixed(1, V), fixed(8, Z), fixed(BLOCK, BLOCK)]
        + any_specs(18),
        out_specs=[tile(R, D), tile(R, D), tile(R, V), tile(R, V), tile(R, Z), tile(R, BLOCK), tile(R, V)],
        out_shape=[
            shape(T, D), shape(T, D), shape(T, V), shape(T, V), shape(T, Z), shape(T, BLOCK), shape(T, V, BF16),
        ],
        scratch_shapes=[
            pltpu.VMEM((D, E), BF16), pltpu.VMEM((D, V), BF16), pltpu.VMEM((V, D), BF16),
            pltpu.SemaphoreType.DMA((18,)),
        ],
        compiler_params=pltpu.CompilerParams(vmem_limit_bytes=VMEM_LIMIT),
        cost_estimate=pl.CostEstimate(flops=2 * T * D * (E + 2 * V), bytes_accessed=40 * T * D, transcendentals=T * (E + V)),
        name="mix_forward",
    )(x, xp, bm, bv, qk, rel, *pieces)


def ffn_both(R, x, u, h, cot, live, norms, bf, bo, pieces):
    T, D = x.shape
    FF = bf.shape[1]
    return pl.pallas_call(
        functools.partial(ffn_kernel, R, (D, FF)),
        grid=(T // R,),
        in_specs=[tile(R, D), tile(R, D), tile(R, D), tile(R, D), tile(R, 1), fixed(8, D), fixed(1, FF), fixed(1, D)]
        + any_specs(12),
        out_specs=[
            tile(R, D), tile(R, D), tile(R, FF), tile(R, D), tile(R, FF), tile(R, D), tile(R, D), tile(R, D),
            fixed(8, D), fixed(1, FF),
        ],
        out_shape=[
            shape(T, D, BF16), shape(T, D, BF16), shape(T, FF, BF16), shape(T, D, BF16), shape(T, FF, BF16),
            shape(T, D, BF16), shape(T, D, BF16), shape(T, D), shape(8, D), shape(1, FF),
        ],
        scratch_shapes=[
            pltpu.VMEM((D, FF), BF16), pltpu.VMEM((FF, D), BF16), pltpu.VMEM((R, FF), F32), pltpu.VMEM((R, D), F32),
            pltpu.VMEM((R, D), F32), pltpu.VMEM((R, 128), F32), pltpu.SemaphoreType.DMA((12,)),
        ],
        compiler_params=pltpu.CompilerParams(vmem_limit_bytes=VMEM_LIMIT),
        cost_estimate=pl.CostEstimate(flops=8 * T * D * FF, bytes_accessed=40 * T * D, transcendentals=T * 2 * FF),
        name="ffn_both",
    )(x, u, h, cot, live, norms, bf, bo, *pieces)


def mix_backward(R, dm, du, dt, r, v, z, p, qk, pieces):
    T, D = dm.shape
    V = r.shape[1]
    Z = qk.shape[1]
    E = 2 * D + Z + V
    return pl.pallas_call(
        functools.partial(mix_bwd_kernel, R, (D, Z, V)),
        grid=(T // R,),
        in_specs=[
            tile(R, D), tile(R, D), tile(R, D), tile(R, V), tile(R, V), tile(R, Z), tile(R, BLOCK), fixed(8, Z),
        ]
        + any_specs(18),
        out_specs=[
            tile(R, E), tile(R, V), tile(R, D), tile(R, D), fixed(1, E), fixed(1, V), fixed(8, Z), fixed(BLOCK, BLOCK),
        ],
        out_shape=[
            shape(T, E, BF16), shape(T, V, BF16), shape(T, D, BF16), shape(T, D), shape(1, E), shape(1, V),
            shape(8, Z), shape(BLOCK, BLOCK),
        ],
        scratch_shapes=[
            pltpu.VMEM((D, E), BF16), pltpu.VMEM((D, V), BF16), pltpu.VMEM((V, D), BF16),
            pltpu.SemaphoreType.DMA((18,)),
        ],
        compiler_params=pltpu.CompilerParams(vmem_limit_bytes=VMEM_LIMIT),
        cost_estimate=pl.CostEstimate(flops=2 * T * D * (E + 2 * V), bytes_accessed=40 * T * D, transcendentals=T * 2 * V),
        name="mix_backward",
    )(dm, du, dt, r, v, z, p, qk, *pieces)


def exchange(value, axis, step):
    return lax.ppermute(value, axis, [(k, k ^ step) for k in range(lax.axis_size(axis))])


def shift(value, axis, step):
    n = lax.axis_size(axis)
    return lax.ppermute(value, axis, [(k, k + step) for k in range(n) if 0 <= k + step < n])


def weight_pieces(own):
    half = own.shape[0] // 2
    bit = lax.rem(lax.axis_index("seq"), 2)
    part = lax.dynamic_slice_in_dim(own, bit * half, half, 0)
    across = exchange(part, "wsh", 2)
    across_y = exchange(across, "seq", 1)
    core = exchange(own, "wsh", 1)
    return (own, core, across, across_y, exchange(across, "wsh", 1), exchange(across_y, "wsh", 1))


def gather_small(own):
    j = lax.axis_index("wsh")
    pair = jnp.stack([own, exchange(own, "wsh", 1)])
    four = jnp.concatenate([pair, exchange(pair, "wsh", 2)])
    return jnp.stack([lax.dynamic_index_in_dim(four, j ^ k, 0, False) for k in range(4)])


def carry_in(states, decay, sign):
    n = lax.axis_size("seq")
    total = shift(states, "seq", sign)
    factor = decay
    for k in range(2, 5):
        if k < n:
            total = total + factor * shift(states, "seq", sign * k)
        factor = factor * decay
    window, factor = 4, factor
    while window < n:
        grown, scale = total, factor
        for k in range(1, 4):
            if k * window < n:
                grown = grown + scale * shift(total, "seq", sign * k * window)
            scale = scale * factor
        total, factor, window = grown, scale, window * 4
    return total


def pick(value, dim, bit):
    return lax.dynamic_index_in_dim(value, bit, dim, False)


def halve(value, dim, axis, step):
    bit = lax.rem(lax.axis_index(axis) // step, 2)
    sent = exchange(pick(value, dim, 1 - bit).astype(BF16), axis, step)
    return pick(value, dim, bit) + sent.astype(F32)


def reduce_grad(grad, order):
    rows, cols = grad.shape
    n_seq, n_wsh = lax.axis_size("seq"), lax.axis_size("wsh")
    steps = [2**k for k in reversed(range(n_seq.bit_length() - 1))]
    labels = ["x", "c"] + [("seq", s) for s in steps]
    value = grad.reshape((2, 2) + (2,) * len(steps) + (rows // n_wsh // n_seq, cols))
    marks = [("wsh", 2), ("wsh", 1)] + [("seq", s) for s in steps]
    plan = [("wsh", 1)] + (
        [("wsh", 2), ("seq", 1), ("seq", 2)] * 2
    )[order : order + 3]
    plan += [("seq", s) for s in reversed(steps) if ("seq", s) not in plan]
    for mark in plan:
        value = halve(value, marks.index(mark), *mark)
        marks.remove(mark)
    return value.astype(BF16)


def spread_grad(mine):
    i = lax.axis_index("seq")
    n = lax.axis_size("seq")
    steps = []
    step = n // 2
    while step:
        steps.append(step)
        step //= 2
    block = mine[None]
    for step in reversed(steps):
        bit = lax.rem(i // step, 2)
        other = exchange(block, "seq", step)
        first = jnp.where(bit == 0, block, other)
        second = jnp.where(bit == 0, other, block)
        block = jnp.concatenate([first, second], axis=0)
    return block.reshape(-1, mine.shape[-1]).astype(F32)


def sum_small(value):
    j = lax.axis_index("wsh")
    total = lax.dynamic_index_in_dim(value, j, 0, False)
    for d in range(1, 4):
        total = total + exchange(lax.dynamic_index_in_dim(value, j ^ d, 0, False), "wsh", d)
    step = 1
    while step < lax.axis_size("seq"):
        total = total + exchange(total, "seq", step)
        step *= 2
    return total


def body(
    tokens, cotangent, lengths, ema_alpha, ema_delta, ema_beta, ema_eta, ema_omega, mix_weight, mix_bias,
    value_weight, value_bias, qk_gain, qk_bias, rel_bias, out_weight, norm_gain, norm_bias, ffn_in, ffn_in_bias,
    ffn_out, ffn_out_bias,
):
    micro, seqs, L, D = tokens.shape
    G = micro * seqs
    T = G * L
    H = ema_alpha.shape[1]
    R = min(512, T)
    n_wsh = lax.axis_size("wsh")
    i = lax.axis_index("seq")
    Z = qk_gain.shape[0] * n_wsh
    V = value_weight.shape[1]
    FF = ffn_in.shape[1]

    wm, wv, wo, wi, wf = (weight_pieces(w) for w in (mix_weight, value_weight, out_weight, ffn_in, ffn_out))
    chan = gather_small(
        jnp.concatenate(
            [ema_alpha, ema_delta, ema_beta, ema_eta, ema_omega[:, None], norm_gain, norm_bias, ffn_out_bias[:, None]],
            axis=1,
        )
    )
    chan = chan.reshape(D, -1).T.astype(F32)
    flat_parts = (mix_bias, value_bias, ffn_in_bias, rel_bias, qk_gain[:, 0], qk_gain[:, 1], qk_bias)
    flat = gather_small(jnp.concatenate(flat_parts)).astype(F32)
    vectors, start = [], 0
    for part in flat_parts:
        vectors.append(flat[:, start : start + part.shape[0]].reshape(1, -1))
        start += part.shape[0]
    bm, bv, bf, rel, gain_q, gain_k, shift_q = vectors
    rate = jax.nn.sigmoid(chan[0:H])
    damp = jax.nn.sigmoid(chan[H : 2 * H])
    beta = chan[2 * H : 3 * H]
    eta = chan[3 * H : 4 * H]
    omega = chan[4 * H : 4 * H + 1]
    norms = jnp.concatenate([chan[4 * H + 1 : 4 * H + 5], jnp.zeros((4, D), F32)])
    bo = chan[4 * H + 5 : 4 * H + 6]
    qk = jnp.concatenate([gain_q, gain_k, shift_q, jnp.zeros((5, Z), F32)])
    rel_matrix = skew_matrix(jnp.roll(rel[0, ::-1], BLOCK))
    keep = 1.0 - rate * damp
    weight = eta * beta * rate
    decay = power(keep, L)
    x3 = tokens.reshape(G, L, D)
    x = tokens.reshape(T, D)
    position = i * L + jnp.arange(L, dtype=jnp.int32)
    live = (position[None, :] < lengths.reshape(G)[:, None]).astype(F32).reshape(T, 1)

    ends, slice_end = ema_ends(x3, keep)
    xp, pre, finals = ema_forward(x3, keep, weight, omega, ends, carry_in(slice_end, decay, 1))
    xp = xp.reshape(T, D)
    u, h, r, v, z, p, mixed = mix_forward(R, x, xp, bm, bv, qk, rel_matrix, wm + wv + wo)
    output, h1, act, dg, df, dm, du, dt, sum_d, sum_f = ffn_both(
        R, x, u, h, cotangent.reshape(T, D), live, norms, bf, bo, wi + wf
    )
    g_ffn_out = reduce_grad(dot_rows(act, dg), 0)
    g_ffn_in = reduce_grad(dot_rows(h1, df), 1)
    g_out = reduce_grad(dot_rows(mixed, dm), 2)
    db, dv, dxp, dtok, sum_m, sum_v, sum_q, sum_s = mix_backward(R, dm, du, dt, r, v, z, p, qk, wm + wv + wo)
    g_mix = reduce_grad(dot_rows(xp, db), 0)
    g_value = reduce_grad(dot_rows(x, dv), 1)
    dpe, back_ends, slice_start = ema_back_ends(dxp.reshape(G, L, D), pre, keep)
    dx, s1, s3, g_omega = ema_backward(
        dpe, x3, keep, 1.0 / keep, weight, omega, finals, back_ends, carry_in(slice_start, decay, -1)
    )
    input_grad = (dtok + dx.reshape(T, D).astype(F32)).astype(BF16).reshape(tokens.shape)

    g_eta = rate * beta * s1
    g_beta = rate * eta * s1
    g_alpha = eta * beta * rate * (1.0 - rate) * (s1 - damp * rate * s3)
    g_delta = -eta * beta * rate * rate * damp * (1.0 - damp) * s3
    late = jnp.concatenate([g_alpha, g_delta, g_beta, g_eta, g_omega])
    late = sum_small(late.reshape(-1, n_wsh, D // n_wsh).transpose(1, 0, 2))
    widened = jnp.pad(sum_s, ((0, 0), (0, BLOCK - 1))).reshape(-1)
    diagonals = jnp.sum(jnp.pad(widened, (0, BLOCK)).reshape(BLOCK, 2 * BLOCK), axis=0)
    g_rel = jnp.roll(diagonals[::-1], BLOCK)
    early_parts = (
        sum_m[0], sum_v[0], sum_f[0], g_rel, sum_q[0], sum_q[1], sum_q[2],
        sum_d[0], sum_d[1], sum_d[2], sum_d[3], sum_d[4],
    )
    early = sum_small(jnp.concatenate([part.reshape(n_wsh, -1) for part in early_parts], axis=1))
    smalls, start = [], 0
    for part in early_parts:
        size = part.shape[0] // n_wsh
        smalls.append(early[start : start + size])
        start += size
    (
        g_mix_bias, g_value_bias, g_ffn_in_bias, g_rel, g_gain_q, g_gain_k, g_shift, gain_1, gain_2, shift_1, shift_2,
        g_ffn_out_bias,
    ) = smalls
    late = late.T
    return (
        output.reshape(tokens.shape), input_grad,
        late[:, 0:H], late[:, H : 2 * H], late[:, 2 * H : 3 * H], late[:, 3 * H : 4 * H], late[:, 4 * H],
        spread_grad(g_mix), g_mix_bias, spread_grad(g_value), g_value_bias,
        jnp.stack([g_gain_q, g_gain_k], axis=1), g_shift, g_rel, spread_grad(g_out),
        jnp.stack([gain_1, gain_2], axis=1), jnp.stack([shift_1, shift_2], axis=1),
        spread_grad(g_ffn_in), g_ffn_in_bias, spread_grad(g_ffn_out), g_ffn_out_bias,
    )


def solution(mesh):
    in_specs = (
        P(None, "wsh", "seq", None),
        P(None, "wsh", "seq", None),
        P(None, "wsh"),
        P("wsh", None),
        P("wsh", None),
        P("wsh", None),
        P("wsh", None),
        P("wsh"),
        P("wsh", None),
        P("wsh"),
        P("wsh", None),
        P("wsh"),
        P("wsh", None),
        P("wsh"),
        P("wsh"),
        P("wsh", None),
        P("wsh", None),
        P("wsh", None),
        P("wsh", None),
        P("wsh"),
        P("wsh", None),
        P("wsh"),
    )
    out_specs = (
        P(None, "wsh", "seq", None),
        P(None, "wsh", "seq", None),
        P("wsh", None),
        P("wsh", None),
        P("wsh", None),
        P("wsh", None),
        P("wsh"),
        P("wsh", None),
        P("wsh"),
        P("wsh", None),
        P("wsh"),
        P("wsh", None),
        P("wsh"),
        P("wsh"),
        P("wsh", None),
        P("wsh", None),
        P("wsh", None),
        P("wsh", None),
        P("wsh"),
        P("wsh", None),
        P("wsh"),
    )
    return jax.shard_map(body, mesh=mesh, in_specs=in_specs, out_specs=out_specs, check_vma=False)
```

time: 3290 us -> 703 us (0.21)
  local copies, waits for them, and re-layouts: 1620 us -> 61.8 us
  matrix products: 595 us -> 60.7 us
  blocking collectives: 523 us -> 0 us
  other arithmetic: 405 us -> 27.1 us
  Pallas kernels: 0 us -> 247 us
  waiting for transfers between devices: 59 us -> 197 us
  starting transfers between devices: 47.9 us -> 96.8 us
    slice x23 -> x18, local copies, waits for them, and re-layouts: 777 us -> 6.84 us  [the longest x5 3.05 us: body(): smalls.append(early[start:start + size])]
    dot_general x41 -> x0, matrix products: 538 us -> none  [the longest x4 261 us: ema_local(): jnp.einsum('chbk,chrk->chrb', reach_table, block_input, precision=HIGHEST)]
    unnamed x2 -> x0, blocking collectives: 477 us -> none
    unnamed x359 -> x100, local copies, waits for them, and re-layouts: 353 us -> 5.29 us
    pallas_call x0 -> x7, Pallas kernels: none -> 247 us  [the longest x1 70.4 us: ffn_both(): pl.pallas_call(functools.partial(ffn_kernel, R, (D, FF)), grid=(T // R,),...]
    ppermute x0 -> x91, waiting for transfers between devices: none -> 197 us  [the longest x81 187 us: exchange(): lax.ppermute(value, axis, [(k, k ^ step) for k in range(lax.axis_size(axi...]
    unnamed x15 -> x11, other arithmetic: 191 us -> 3.66 us
    reshape x33 -> x7, local copies, waits for them, and re-layouts: 166 us -> 3.15 us  [the longest x1 1.13 us: body(): late = sum_small(late.reshape(-1, n_wsh, D // n_wsh).transpose(1, 0, 2))]
  transfers between devices with their start and end apart: 14 -> 91, of which waited for: 1 -> 40; matrix products, arithmetic and copies ran while one was open for 39% -> 20% of each run, Pallas kernels for 0% -> 16%
where the time goes in v1:
time: 703 us; the launch traced here: 693 us
  Pallas kernels  247 us (35%)
  waiting for transfers between devices  197 us (28%)
  starting transfers between devices  96.8 us (14%)
  local copies, waits for them, and re-layouts  61.8 us (9%)
  matrix products  60.7 us (9%)
  other arithmetic  27.1 us (4%)
    ppermute x81, waiting for transfers between devices, exchange(): lax.ppermute(value, axis, [(k, k ^ step) for k in range(lax.axis_size(axi...  187 us
    ppermute x81, starting transfers between devices, exchange(): lax.ppermute(value, axis, [(k, k ^ step) for k in range(lax.axis_size(axi...  72.3 us
    pallas_call x1, Pallas kernels, ffn_both(): pl.pallas_call(functools.partial(ffn_kernel, R, (D, FF)), grid=(T // R,),...  70.4 us
    dot_general x5, matrix products, dot_rows(): jnp.einsum('ri,rj->ij', left_op, right_op, preferred_element_type=jnp.flo...  60.7 us
    pallas_call x1, Pallas kernels, ema_backward(): pl.pallas_call(functools.partial(bwd_kernel, H, L // CH), grid=(C // LANE...  49.6 us
    pallas_call x1, Pallas kernels, mix_backward(): pl.pallas_call(functools.partial(mix_bwd_kernel, R, (D, Z, V)), grid=(T /...  47.9 us
    pallas_call x1, Pallas kernels, mix_forward(): pl.pallas_call(functools.partial(mix_fwd_kernel, R, (D, Z, V)), grid=(T /...  33.5 us
    ppermute x10, starting transfers between devices, shift(): lax.ppermute(value, axis, [(k, k + step) for k in range(n) if 0 <= k + st...  24.5 us
  transfers between devices with their start and end apart: 91, of which 40 were waited for; matrix products, arithmetic and copies ran while one was open for 20% of the time, Pallas kernels for 16%

profile of v1, /device:TPU:0, one launch (start us, length us, event | category | flops | bytes accessed | tf_op | source)
XLA Modules:
  0.0 692.9 jit_solution(17770637819947914832)
XLA Ops:
  1.4 3.5 concatenate.85
  6.7 3.5 concatenate.83
  11.3 3.0 collective-permute-start.15
  16.5 1.7 constant_dynamic-slice_fusion.12
  23.6 2.8 collective-permute-done.1
  27.6 11.5 %ema_ends.1 = (f32[2,128,768]{2,1,0:T(8,128)}, f32[2,16,768]{2,1,0:T(8,128)}) custom-call(bf16[2,1024,768]{2,1,0:T(8,128)(2,1)} %bitcast.237, f32[16,768]{1,0:T(8,128)} %get-tuple-element.171.q_ref), custom_call_target="tpu_custom_call" | custom-call | tf_op jit(solution)/shard_map/ema_ends/pallas_call | solution.py:168
  39.1 4.5 collective-permute-start.5
  43.6 4.4 collective-permute-start.4
  49.3 3.1 collective-permute-start.2
  56.1 4.8 collective-permute-start.6
  60.9 2.1 collective-permute-done.6
  64.7 4.3 collective-permute-done.30.refs_8_
  69.9 14.9 %collective-permute-done.25.refs_2_ = bf16[96,1536]{1,0:T(8,128)(2,1)} collective-permute-done((bf16[96,1536]{1,0:T(8,128)(2,1)S(1)}, bf16[96,1536]{1,0:T(8,128)(2,1)}, u32[]{:S(2)}, u32[]{:S(2)}) %collective-permute-start.25) | collective-permute-done | bytes 294944 | tf_op jit(solution)/shard_map/ppermute | solution.py:553
  88.0 6.7 collective-permute-done.21.refs_15_
  97.8 3.3 collective-permute-done.31.refs_9_
  102.6 15.1 %collective-permute-done.26.refs_3_ = bf16[96,1536]{1,0:T(8,128)(2,1)} collective-permute-done((bf16[96,1536]{1,0:T(8,128)(2,1)}, bf16[96,1536]{1,0:T(8,128)(2,1)}, u32[]{:S(2)}, u32[]{:S(2)}) %collective-permute-start.26) | collective-permute-done | bytes 294944 | tf_op jit(solution)/shard_map/ppermute | solution.py:553
  121.3 19.5 %ema_fwd.1 = (bf16[2,1024,768]{2,1,0:T(8,128)(2,1)}, f32[2,1024,768]{2,1,0:T(8,128)}, f32[2,128,768]{2,1,0:T(8,128)}) custom-call(bf16[2,1024,768]{2,1,0:T(8,128)(2,1)} %bitcast.238, f32[16,768]{1,0:T(8,128)} %get-tuple-element.171.q_ref, f32[16,768]{1,0:T(8,128)} %get-tuple-element.200.w_ref, f32[1,768]{1,0:T(1,128)} %get-tuple-element.199.om_ref, ...), custom_call_target="tpu_custom_call" | custom-call | tf_op jit(solution)/shard_map/ema_fwd/pallas_call | solution.py:174
  140.8 4.7 copy.62
  146.8 33.5 %mix_forward.1 = (f32[2048,768]{1,0:T(8,128)}, f32[2048,768]{1,0:T(8,128)}, f32[2048,1536]{1,0:T(8,128)}, f32[2048,1536]{1,0:T(8,128)}, f32[2048,128]{1,0:T(8,12...) custom-call(bf16[2048,768]{1,0:T(8,128)(2,1)} %bitcast.239, bf16[2048,768]{1,0:T(8,128)(2,1)} %bitcast.254, ...), custom_call_target="tpu_custom_call" | custom-call | flops 19730006016 | bytes 62914560 | tf_op jit(solution)/shard_map/mix_forward/pallas_call | solution.py:478
  181.2 70.4 %ffn_both.1 = (bf16[2048,768]{1,0:T(8,128)(2,1)}, bf16[2048,768]{1,0:T(8,128)(2,1)}, bf16[2048,1536]{1,0:T(8,128)(2,1)}, bf16[2048,768]{1,0:T(8,128)(2,1)}, bf16...) custom-call(bf16[2048,768]{1,0:T(8,128)(2,1)} %bitcast.240, ...), custom_call_target="tpu_custom_call" | custom-call | flops 19327352832 | bytes 62914560 | tf_op jit(solution)/shard_map/ffn_both/pallas_call | solution.py:500
  251.5 47.9 %mix_backward.1 = (bf16[2048,3200]{1,0:T(8,128)(2,1)}, bf16[2048,1536]{1,0:T(8,128)(2,1)}, bf16[2048,768]{1,0:T(8,128)(2,1)}, f32[2048,768]{1,0:T(8,128)}, f32[1...) custom-call(bf16[2048,768]{1,0:T(8,128)(2,1)} %get-tuple-element.64.dm_ref, ...), custom_call_target="tpu_custom_call" | custom-call | flops 19730006016 | bytes 62914560 | tf_op jit(solution)/shard_map/mix_backward/pallas_call | solution.py:528
  299.4 14.8 %ema_bends.1 = (f32[2,1024,768]{2,1,0:T(8,128)}, f32[2,128,768]{2,1,0:T(8,128)}, f32[2,16,768]{2,1,0:T(8,128)}) custom-call(bf16[2,1024,768]{2,1,0:T(8,128)(2,1)} %bitcast.256, f32[2,1024,768]{2,1,0:T(8,128)} %get-tuple-element.73.p_ref, f32[16,768]{1,0:T(8,128)} %get-tuple-element.171.q_ref), custom_call_target="tpu_custom_call" | custom-call | tf_op jit(solution)/shard_map/ema_bends/pallas_call | solution.py:181
  316.9 17.9 %fusion.66 = f32[1536,768]{1,0:T(8,128)} fusion(bf16[2048,1536]{1,0:T(8,128)(2,1)} %get-tuple-element.90, bf16[2048,768]{1,0:T(8,128)(2,1)} %get-tuple-element.64.dm_ref), kind=kOutput, calls=%fused_computation.246 | convolution fusion | flops 4831838208 | bytes 14155776 | tf_op jit(solution)/shard_map/ri,rj->ij/dot_general | solution.py:23
  351.8 9.7 %fusion.65 = f32[1536,768]{0,1:T(8,128)} fusion(bf16[2048,1536]{1,0:T(8,128)(2,1)} %get-tuple-element.89, bf16[2048,768]{1,0:T(8,128)(2,1)S(1)} %bitcast.242), kind=kOutput, calls=%fused_computation.245 | convolution fusion | flops 4831838208 | bytes 14155776 | tf_op jit(solution)/shard_map/ri,rj->ij/dot_general | solution.py:23
  361.5 7.5 %fusion.67 = f32[768,1536]{1,0:T(8,128)S(1)} fusion(bf16[2048,768]{1,0:T(8,128)(2,1)S(1)} %copy-done.33, bf16[2048,1536]{1,0:T(8,128)(2,1)} %get-tuple-element.92), kind=kOutput, calls=%fused_computation.247 | convolution fusion | flops 4831838208 | bytes 14155776 | tf_op jit(solution)/shard_map/ri,rj->ij/dot_general | solution.py:23
  369.0 9.0 %fusion.68 = f32[1536,768]{1,0:T(8,128)S(1)} fusion(bf16[2048,1536]{1,0:T(8,128)(2,1)} %get-tuple-element.93, bf16[2048,768]{1,0:T(8,128)(2,1)S(1)} %copy-done.32), kind=kOutput, calls=%fused_computation.248 | convolution fusion | flops 4831838208 | bytes 14155776 | tf_op jit(solution)/shard_map/ri,rj->ij/dot_general | solution.py:23
  378.1 16.6 %fusion = f32[2,2,2,2,2,24,3200]{6,5,4,3,2,1,0:T(8,128)S(1)} fusion(bf16[2,2,2,2,2,24,2048]{6,5,4,3,2,1,0:T(8,128)(2,1)S(1)} %bitcast.252, bf16[2048,3200]{1,0:T(8,128)(2,1)} %get-tuple-element.82), kind=kOutput, calls=%fused_computation | convolution fusion | flops 10066329600 | bytes 26083328 | tf_op jit(solution)/shard_map/ri,rj->ij/dot_general | solution.py:23
  394.7 1.9 fusion.3
  396.5 4.6 fusion.5
  403.8 2.7 collective-permute-start.56
  407.6 1.8 collective-permute-done.56
  409.4 2.7 collective-permute-start.57
  412.1 2.8 fusion.6
  414.9 4.4 collective-permute-start.58
  425.1 7.7 %collective-permute-done.38 = f32[2,16,768]{2,1,0:T(8,128)S(1)} collective-permute-done((f32[2,16,768]{2,1,0:T(8,128)S(1)}, f32[2,16,768]{2,1,0:T(8,128)S(1)}, u32[]{:S(2)}, u32[]{:S(2)}) %collective-permute-start.38) | collective-permute-done | bytes 98336 | tf_op jit(solution)/shard_map/ppermute | solution.py:558
  433.5 49.6 %ema_bwd.1 = (bf16[2,1024,768]{2,1,0:T(8,128)(2,1)}, f32[16,768]{1,0:T(8,128)}, f32[16,768]{1,0:T(8,128)}, f32[1,768]{1,0:T(1,128)}) custom-call(f32[2,1024,768]{2,1,0:T(8,128)} %get-tuple-element.74.d_ref, bf16[2,1024,768]{2,1,0:T(8,128)(2,1)} %bitcast.241, f32[16,768]{1,0:T(8,128)} %get-tuple-element.171.q_ref, f32[16,768]{1,0:T(8,128)} %get-tuple-element.170.qi_ref, ...), custom_call_target="tpu_custom_call" | custom-call | tf_op jit(solution)/shard_map/ema_bwd/pallas_call | solution.py:187
  492.9 2.0 collective-permute-done.40
  498.1 2.5 collective-permute-done.42
  502.5 2.6 collective-permute-done.43
  505.2 5.3 fusion.2
  513.7 1.7 bitcast_add_fusion.5
  519.9 9.5 %collective-permute-done.68 = bf16[2,2,2,48,768]{4,3,2,1,0:T(8,128)(2,1)S(1)} collective-permute-done((bf16[2,2,2,48,768]{4,3,2,1,0:T(8,128)(2,1)S(1)}, bf16[2,2,2,48,768]{4,3,2,1,0:T(8,128)(2,1)S(1)}, u32[]{:S(2)}, u32[]{:S(2)}) %collective-permute-start.68) | collective-permute-done | bytes 589856 | tf_op jit(solution)/shard_map/ppermute | solution.py:553
  531.9 1.9 collective-permute-start.61
  533.8 10.1 %collective-permute-done.76 = bf16[2,2,2,24,1536]{4,3,1,0,2:T(8,128)(2,1)S(1)} collective-permute-done((bf16[2,2,2,24,1536]{4,3,1,0,2:T(8,128)(2,1)S(1)}, bf16[2,2,2,24,1536]{4,3,1,0,2:T(8,128)(2,1)S(1)}, u32[]{:S(2)}, u32[]{:S(2)}) %collective-permute-start.76) | collective-permute-done | bytes 589856 | tf_op jit(solution)/shard_map/ppermute | solution.py:553
  544.2 1.6 collective-permute-start.77
  549.8 3.1 collective-permute-done.77
  557.3 2.8 collective-permute-start.71
  560.5 2.8 collective-permute-start.79
  564.9 4.1 collective-permute-done.71
  581.1 2.2 collective-permute-start.74
  583.3 7.4 %collective-permute-done.65 = bf16[2,24,1536]{2,1,0:T(8,128)(2,1)S(1)} collective-permute-done((bf16[2,24,1536]{2,1,0:T(8,128)(2,1)S(1)}, bf16[2,24,1536]{2,1,0:T(8,128)(2,1)S(1)}, u32[]{:S(2)}, u32[]{:S(2)}) %collective-permute-start.65) | collective-permute-done | bytes 147488 | tf_op jit(solution)/shard_map/ppermute | solution.py:553
  591.5 1.9 collective-permute-done.81
  596.7 9.3 %collective-permute-done.46 = bf16[2,2,2,24,3200]{4,3,2,1,0:T(8,128)(2,1)S(1)} collective-permute-done((bf16[2,2,2,24,3200]{4,3,2,1,0:T(8,128)(2,1)S(1)}, bf16[2,2,2,24,3200]{4,3,2,1,0:T(8,128)(2,1)S(1)}, u32[]{:S(2)}, u32[]{:S(2)}) %collective-permute-start.46) | collective-permute-done | bytes 1228832 | tf_op jit(solution)/shard_map/ppermute | solution.py:553
  607.4 16.2 %collective-permute-done.66 = bf16[4,24,1536]{2,1,0:T(8,128)(2,1)S(1)} collective-permute-done((bf16[4,24,1536]{2,1,0:T(8,128)(2,1)S(1)}, bf16[4,24,1536]{2,1,0:T(8,128)(2,1)S(1)}, u32[]{:S(2)}, u32[]{:S(2)}) %collective-permute-start.66) | collective-permute-done | bytes 294944 | tf_op jit(solution)/shard_map/ppermute | solution.py:553
  623.7 5.7 collective-permute-done.82
  629.7 2.8 collective-permute-done.90
  632.6 6.4 collective-permute-done.48
  639.3 8.5 %collective-permute-done.49 = bf16[24,3200]{1,0:T(8,128)(2,1)S(1)} collective-permute-done((bf16[24,3200]{1,0:T(8,128)(2,1)S(1)}, bf16[24,3200]{1,0:T(8,128)(2,1)S(1)}, u32[]{:S(2)}, u32[]{:S(2)}) %collective-permute-start.49) | collective-permute-done | bytes 153632 | tf_op jit(solution)/shard_map/ppermute | solution.py:553
  649.2 4.6 collective-permute-done.50
  654.0 1.7 bitcast_convert_fusion.1
  655.6 6.7 collective-permute-done.51
  663.2 1.8 bitcast_convert_fusion.2
  665.0 25.6 %collective-permute-done.52 = bf16[4,24,3200]{2,1,0:T(8,128)(2,1)S(1)} collective-permute-done((bf16[4,24,3200]{2,1,0:T(8,128)(2,1)S(1)}, bf16[4,24,3200]{2,1,0:T(8,128)(2,1)S(1)}, u32[]{:S(2)}, u32[]{:S(2)}) %collective-permute-start.52) | collective-permute-done | bytes 614432 | tf_op jit(solution)/shard_map/ppermute | solution.py:553
  690.9 1.7 bitcast_convert_fusion
  (424 shorter events, 118.8 us)
Async XLA Ops:
  4.9 13.3 %collective-permute-start.7 = (bf16[1728]{0:T(1024)(128)(2,1)S(1)}, bf16[1728]{0:T(1024)(128)(2,1)S(1)}, u32[]{:S(2)}, u32[]{:S(2)}) collective-permute-start(bf16[1728]{0:T(1024)(128)(2,1)S(1)} %concatenate.85), channel_id=1, source_target_pairs={{0,1},{1,0},{2,3},{3,2},{4,5},{5,4},{6,7},{7,6},{8,9},{9,8},{10,11... | collective-permute-start | bytes 10376 | tf_op jit(solution)/shard_map/ppermute | solution.py:553
  10.2 11.8 %collective-permute-start = (bf16[192,70]{0,1:T(8,128)(2,1)S(1)}, bf16[192,70]{0,1:T(8,128)(2,1)S(1)}, u32[]{:S(2)}, u32[]{:S(2)}) collective-permute-start(bf16[192,70]{0,1:T(8,128)(2,1)S(1)} %concatenate.83), channel_id=1, source_target_pairs={{0,1},{1,0},{2,3},{3,2},{4,5},{5,4},{6,7},{7,6},{8,9},{9,8},{10,11... | collective-permute-start | bytes 80648 | tf_op jit(solution)/shard_map/ppermute | solution.py:553
  11.3 53.3 %collective-permute-start.15 = (bf16[96,1536]{1,0:T(8,128)(2,1)S(1)}, bf16[96,1536]{1,0:T(8,128)(2,1)}, u32[]{:S(2)}, u32[]{:S(2)}) collective-permute-start(bf16[96,1536]{1,0:T(8,128)(2,1)S(1)} %constant_dynamic-slice_fusion.15), channel_id=1, source_target_pairs={{0,2},{1,3},{2,0},{3,1},{4,6},{5,7},{6,4},{7,5},{8,10},{9,11},{10,... | collective-permute-start | bytes 884744 | tf_op jit(solution)/shard_map/ppermute | solution.py:553
  39.1 13.4 %collective-permute-start.5 = (f32[2,16,768]{2,1,0:T(8,128)}, f32[2,16,768]{2,1,0:T(8,128)S(1)}, u32[]{:S(2)}, u32[]{:S(2)}) collective-permute-start(f32[2,16,768]{2,1,0:T(8,128)} %get-tuple-element.59), channel_id=1, source_target_pairs={{0,16},{4,20},{8,24},{12,28},{1,17},{5,21},{9,25},{13,29},{2,18},{... | collective-permute-start | bytes 294920 | tf_op jit(solution)/shard_map/ppermute | solution.py:558
  43.6 10.5 %collective-permute-start.4 = (f32[2,16,768]{2,1,0:T(8,128)}, f32[2,16,768]{2,1,0:T(8,128)S(1)}, u32[]{:S(2)}, u32[]{:S(2)}) collective-permute-start(f32[2,16,768]{2,1,0:T(8,128)} %get-tuple-element.59), channel_id=1, source_target_pairs={{0,12},{4,16},{8,20},{12,24},{16,28},{1,13},{5,17},{9,21},{13,25},... | collective-permute-start | bytes 294920 | tf_op jit(solution)/shard_map/ppermute | solution.py:558
  52.5 12.1 %collective-permute-start.20 = (bf16[192,768]{1,0:T(8,128)(2,1)}, bf16[192,768]{1,0:T(8,128)(2,1)}, u32[]{:S(2)}, u32[]{:S(2)}) collective-permute-start(bf16[192,768]{1,0:T(8,128)(2,1)} %constant_dynamic-slice_fusion.14), channel_id=1, source_target_pairs={{0,2},{1,3},{2,0},{3,1},{4,6},{5,7},{6,4},{7,5},{8,10},{9,11},{10,... | collective-permute-start | bytes 884744 | tf_op jit(solution)/shard_map/ppermute | solution.py:553
  54.0 15.0 %collective-permute-start.30 = (bf16[192,768]{1,0:T(8,128)(2,1)}, bf16[192,768]{1,0:T(8,128)(2,1)S(1)}, u32[]{:S(2)}, u32[]{:S(2)}) collective-permute-start(bf16[192,768]{1,0:T(8,128)(2,1)} %constant_dynamic-slice_fusion.12), channel_id=1, source_target_pairs={{0,2},{1,3},{2,0},{3,1},{4,6},{5,7},{6,4},{7,5},{8,10},{9,11},{10,... | collective-permute-start | bytes 884744 | tf_op jit(solution)/shard_map/ppermute | solution.py:553
  54.6 32.4 %collective-permute-start.10 = (bf16[96,3200]{1,0:T(8,128)(2,1)S(1)}, bf16[96,3200]{1,0:T(8,128)(2,1)}, u32[]{:S(2)}, u32[]{:S(2)}) collective-permute-start(bf16[96,3200]{1,0:T(8,128)(2,1)S(1)} %constant_dynamic-slice_fusion.16), channel_id=1, source_target_pairs={{0,2},{1,3},{2,0},{3,1},{4,6},{5,7},{6,4},{7,5},{8,10},{9,11},{10,... | collective-permute-start | bytes 1843208 | tf_op jit(solution)/shard_map/ppermute | solution.py:553
  63.1 21.8 %collective-permute-start.25 = (bf16[96,1536]{1,0:T(8,128)(2,1)S(1)}, bf16[96,1536]{1,0:T(8,128)(2,1)}, u32[]{:S(2)}, u32[]{:S(2)}) collective-permute-start(bf16[96,1536]{1,0:T(8,128)(2,1)S(1)} %constant_dynamic-slice_fusion.13), channel_id=1, source_target_pairs={{0,2},{1,3},{2,0},{3,1},{4,6},{5,7},{6,4},{7,5},{8,10},{9,11},{10,... | collective-permute-start | bytes 884744 | tf_op jit(solution)/shard_map/ppermute | solution.py:553
  64.6 21.1 %collective-permute-start.17 = (bf16[96,1536]{1,0:T(8,128)(2,1)}, bf16[96,1536]{1,0:T(8,128)(2,1)S(1)}, u32[]{:S(2)}, u32[]{:S(2)}) collective-permute-start(bf16[96,1536]{1,0:T(8,128)(2,1)} %collective-permute-done.15.refs_8_), channel_id=1, source_target_pairs={{0,1},{1,0},{2,3},{3,2},{4,5},{5,4},{6,7},{7,6},{8,9},{9,8},{10,11... | collective-permute-start | bytes 884744 | tf_op jit(solution)/shard_map/ppermute | solution.py:553
  64.6 21.1 %collective-permute-start.16 = (bf16[96,1536]{1,0:T(8,128)(2,1)}, bf16[96,1536]{1,0:T(8,128)(2,1)}, u32[]{:S(2)}, u32[]{:S(2)}) collective-permute-start(bf16[96,1536]{1,0:T(8,128)(2,1)} %collective-permute-done.15.refs_8_), channel_id=1, source_target_pairs={{0,4},{4,0},{8,12},{12,8},{16,20},{20,16},{24,28},{28,24},{1,5},{5... | collective-permute-start | bytes 884744 | tf_op jit(solution)/shard_map/ppermute | solution.py:553
  69.1 18.8 %collective-permute-start.22 = (bf16[192,768]{1,0:T(8,128)(2,1)}, bf16[192,768]{1,0:T(8,128)(2,1)}, u32[]{:S(2)}, u32[]{:S(2)}) collective-permute-start(bf16[192,768]{1,0:T(8,128)(2,1)} %collective-permute-done.20.refs_14_), channel_id=1, source_target_pairs={{0,1},{1,0},{2,3},{3,2},{4,5},{5,4},{6,7},{7,6},{8,9},{9,8},{10,11... | collective-permute-start | bytes 884744 | tf_op jit(solution)/shard_map/ppermute | solution.py:553
  84.8 9.8 %collective-permute-start.21 = (bf16[192,768]{1,0:T(8,128)(2,1)}, bf16[192,768]{1,0:T(8,128)(2,1)S(1)}, u32[]{:S(2)}, u32[]{:S(2)}) collective-permute-start(bf16[192,768]{1,0:T(8,128)(2,1)} %collective-permute-done.20.refs_14_), channel_id=1, source_target_pairs={{0,4},{4,0},{8,12},{12,8},{16,20},{20,16},{24,28},{28,24},{1,5},{5... | collective-permute-start | bytes 884744 | tf_op jit(solution)/shard_map/ppermute | solution.py:553
  85.7 15.4 %collective-permute-start.31 = (bf16[192,768]{1,0:T(8,128)(2,1)}, bf16[192,768]{1,0:T(8,128)(2,1)}, u32[]{:S(2)}, u32[]{:S(2)}) collective-permute-start(bf16[192,768]{1,0:T(8,128)(2,1)} %copy-done.24), channel_id=1, source_target_pairs={{0,4},{4,0},{8,12},{12,8},{16,20},{20,16},{24,28},{28,24},{1,5},{5... | collective-permute-start | bytes 884744 | tf_op jit(solution)/shard_map/ppermute | solution.py:553
  87.0 30.7 %collective-permute-start.11 = (bf16[96,3200]{1,0:T(8,128)(2,1)}, bf16[96,3200]{1,0:T(8,128)(2,1)S(1)}, u32[]{:S(2)}, u32[]{:S(2)}) collective-permute-start(bf16[96,3200]{1,0:T(8,128)(2,1)} %collective-permute-done.10.refs_2_), channel_id=1, source_target_pairs={{0,4},{4,0},{8,12},{12,8},{16,20},{20,16},{24,28},{28,24},{1,5},{5... | collective-permute-start | bytes 1843208 | tf_op jit(solution)/shard_map/ppermute | solution.py:553
  87.8 58.5 %collective-permute-start.9 = (bf16[192,3200]{1,0:T(8,128)(2,1)S(1)}, bf16[192,3200]{1,0:T(8,128)(2,1)}, u32[]{:S(2)}, u32[]{:S(2)}) collective-permute-start(bf16[192,3200]{1,0:T(8,128)(2,1)S(1)} %copy-done.16), channel_id=1, source_target_pairs={{0,1},{1,0},{2,3},{3,2},{4,5},{5,4},{6,7},{7,6},{8,9},{9,8},{10,11... | collective-permute-start | bytes 3686408 | tf_op jit(solution)/shard_map/ppermute | solution.py:553
  94.6 24.2 %collective-permute-start.14 = (bf16[192,1536]{1,0:T(8,128)(2,1)}, bf16[192,1536]{1,0:T(8,128)(2,1)}, u32[]{:S(2)}, u32[]{:S(2)}) collective-permute-start(bf16[192,1536]{1,0:T(8,128)(2,1)} %refs_6_.5), channel_id=1, source_target_pairs={{0,1},{1,0},{2,3},{3,2},{4,5},{5,4},{6,7},{7,6},{8,9},{9,8},{10,11... | collective-permute-start | bytes 1769480 | tf_op jit(solution)/shard_map/ppermute | solution.py:553
  94.7 24.4 %collective-permute-start.19 = (bf16[384,768]{1,0:T(8,128)(2,1)}, bf16[384,768]{1,0:T(8,128)(2,1)}, u32[]{:S(2)}, u32[]{:S(2)}) collective-permute-start(bf16[384,768]{1,0:T(8,128)(2,1)} %refs_12_.3), channel_id=1, source_target_pairs={{0,1},{1,0},{2,3},{3,2},{4,5},{5,4},{6,7},{7,6},{8,9},{9,8},{10,11... | collective-permute-start | bytes 1769480 | tf_op jit(solution)/shard_map/ppermute | solution.py:553
  101.1 16.6 %collective-permute-start.26 = (bf16[96,1536]{1,0:T(8,128)(2,1)}, bf16[96,1536]{1,0:T(8,128)(2,1)}, u32[]{:S(2)}, u32[]{:S(2)}) collective-permute-start(bf16[96,1536]{1,0:T(8,128)(2,1)} %collective-permute-done.25.refs_2_), channel_id=1, source_target_pairs={{0,4},{4,0},{8,12},{12,8},{16,20},{20,16},{24,28},{28,24},{1,5},{5... | collective-permute-start | bytes 884744 | tf_op jit(solution)/shard_map/ppermute | solution.py:553
  117.7 28.5 %collective-permute-start.12 = (bf16[96,3200]{1,0:T(8,128)(2,1)}, bf16[96,3200]{1,0:T(8,128)(2,1)}, u32[]{:S(2)}, u32[]{:S(2)}) collective-permute-start(bf16[96,3200]{1,0:T(8,128)(2,1)} %collective-permute-done.10.refs_2_), channel_id=1, source_target_pairs={{0,1},{1,0},{2,3},{3,2},{4,5},{5,4},{6,7},{7,6},{8,9},{9,8},{10,11... | collective-permute-start | bytes 1843208 | tf_op jit(solution)/shard_map/ppermute | solution.py:553
  117.7 29.0 %collective-permute-start.13 = (bf16[96,3200]{1,0:T(8,128)(2,1)S(1)}, bf16[96,3200]{1,0:T(8,128)(2,1)}, u32[]{:S(2)}, u32[]{:S(2)}) collective-permute-start(bf16[96,3200]{1,0:T(8,128)(2,1)S(1)} %collective-permute-done.11.refs_3_), channel_id=1, source_target_pairs={{0,1},{1,0},{2,3},{3,2},{4,5},{5,4},{6,7},{7,6},{8,9},{9,8},{10,11... | collective-permute-start | bytes 1843208 | tf_op jit(solution)/shard_map/ppermute | solution.py:553
  118.9 26.7 %collective-permute-start.18 = (bf16[96,1536]{1,0:T(8,128)(2,1)}, bf16[96,1536]{1,0:T(8,128)(2,1)S(1)}, u32[]{:S(2)}, u32[]{:S(2)}) collective-permute-start(bf16[96,1536]{1,0:T(8,128)(2,1)} %collective-permute-done.16.refs_9_), channel_id=1, source_target_pairs={{0,1},{1,0},{2,3},{3,2},{4,5},{5,4},{6,7},{7,6},{8,9},{9,8},{10,11... | collective-permute-start | bytes 884744 | tf_op jit(solution)/shard_map/ppermute | solution.py:553
  119.0 26.8 %collective-permute-start.23 = (bf16[192,768]{1,0:T(8,128)(2,1)}, bf16[192,768]{1,0:T(8,128)(2,1)}, u32[]{:S(2)}, u32[]{:S(2)}) collective-permute-start(bf16[192,768]{1,0:T(8,128)(2,1)} %copy-done.26), channel_id=1, source_target_pairs={{0,1},{1,0},{2,3},{3,2},{4,5},{5,4},{6,7},{7,6},{8,9},{9,8},{10,11... | collective-permute-start | bytes 884744 | tf_op jit(solution)/shard_map/ppermute | solution.py:553
  145.6 34.7 %collective-permute-start.24 = (bf16[192,1536]{1,0:T(8,128)(2,1)}, bf16[192,1536]{1,0:T(8,128)(2,1)}, u32[]{:S(2)}, u32[]{:S(2)}) collective-permute-start(bf16[192,1536]{1,0:T(8,128)(2,1)} %refs_0_.4), channel_id=1, source_target_pairs={{0,1},{1,0},{2,3},{3,2},{4,5},{5,4},{6,7},{7,6},{8,9},{9,8},{10,11... | collective-permute-start | bytes 1769480 | tf_op jit(solution)/shard_map/ppermute | solution.py:553
  145.8 34.6 %collective-permute-start.29 = (bf16[384,768]{1,0:T(8,128)(2,1)}, bf16[384,768]{1,0:T(8,128)(2,1)}, u32[]{:S(2)}, u32[]{:S(2)}) collective-permute-start(bf16[384,768]{1,0:T(8,128)(2,1)} %refs_6_.4), channel_id=1, source_target_pairs={{0,1},{1,0},{2,3},{3,2},{4,5},{5,4},{6,7},{7,6},{8,9},{9,8},{10,11... | collective-permute-start | bytes 1769480 | tf_op jit(solution)/shard_map/ppermute | solution.py:553
  146.1 34.2 %collective-permute-start.27 = (bf16[96,1536]{1,0:T(8,128)(2,1)}, bf16[96,1536]{1,0:T(8,128)(2,1)}, u32[]{:S(2)}, u32[]{:S(2)}) collective-permute-start(bf16[96,1536]{1,0:T(8,128)(2,1)} %collective-permute-done.25.refs_2_), channel_id=1, source_target_pairs={{0,1},{1,0},{2,3},{3,2},{4,5},{5,4},{6,7},{7,6},{8,9},{9,8},{10,11... | collective-permute-start | bytes 884744 | tf_op jit(solution)/shard_map/ppermute | solution.py:553
  146.3 34.0 %collective-permute-start.33 = (bf16[192,768]{1,0:T(8,128)(2,1)}, bf16[192,768]{1,0:T(8,128)(2,1)S(1)}, u32[]{:S(2)}, u32[]{:S(2)}) collective-permute-start(bf16[192,768]{1,0:T(8,128)(2,1)} %collective-permute-done.31.refs_9_), channel_id=1, source_target_pairs={{0,1},{1,0},{2,3},{3,2},{4,5},{5,4},{6,7},{7,6},{8,9},{9,8},{10,11... | collective-permute-start | bytes 884744 | tf_op jit(solution)/shard_map/ppermute | solution.py:553
  146.7 33.7 %collective-permute-start.28 = (bf16[96,1536]{1,0:T(8,128)(2,1)}, bf16[96,1536]{1,0:T(8,128)(2,1)S(1)}, u32[]{:S(2)}, u32[]{:S(2)}) collective-permute-start(bf16[96,1536]{1,0:T(8,128)(2,1)} %collective-permute-done.26.refs_3_), channel_id=1, source_target_pairs={{0,1},{1,0},{2,3},{3,2},{4,5},{5,4},{6,7},{7,6},{8,9},{9,8},{10,11... | collective-permute-start | bytes 884744 | tf_op jit(solution)/shard_map/ppermute | solution.py:553
  314.2 107.4 %collective-permute-start.37 = (f32[2,16,768]{2,1,0:T(8,128)}, f32[2,16,768]{2,1,0:T(8,128)}, u32[]{:S(2)}, u32[]{:S(2)}) collective-permute-start(f32[2,16,768]{2,1,0:T(8,128)} %get-tuple-element.77), channel_id=1, source_target_pairs={{16,0},{20,4},{24,8},{28,12},{17,1},{21,5},{25,9},{29,13},{18,2},{... | collective-permute-start | bytes 294920 | tf_op jit(solution)/shard_map/ppermute | solution.py:558
  315.5 106.6 %collective-permute-start.36 = (f32[2,16,768]{2,1,0:T(8,128)}, f32[2,16,768]{2,1,0:T(8,128)}, u32[]{:S(2)}, u32[]{:S(2)}) collective-permute-start(f32[2,16,768]{2,1,0:T(8,128)} %get-tuple-element.77), channel_id=1, source_target_pairs={{12,0},{16,4},{20,8},{24,12},{28,16},{13,1},{17,5},{21,9},{25,13},... | collective-permute-start | bytes 294920 | tf_op jit(solution)/shard_map/ppermute | solution.py:558
  349.6 51.6 %collective-permute-start.53 = (f32[2688]{0:T(1024)S(1)}, f32[2688]{0:T(1024)S(1)}, u32[]{:S(2)}, u32[]{:S(2)}) collective-permute-start(f32[2688]{0:T(1024)S(1)} %get-tuple-element.158), channel_id=1, source_target_pairs={{0,1},{1,0},{2,3},{3,2},{4,5},{5,4},{6,7},{7,6},{8,9},{9,8},{10,11... | collective-permute-start | bytes 32264 | tf_op jit(solution)/shard_map/ppermute | solution.py:553
  350.0 52.4 %collective-permute-start.55 = (f32[2688]{0:T(1024)S(1)}, f32[2688]{0:T(1024)S(1)}, u32[]{:S(2)}, u32[]{:S(2)}) collective-permute-start(f32[2688]{0:T(1024)S(1)} %get-tuple-element.159), channel_id=1, source_target_pairs={{0,3},{1,2},{2,1},{3,0},{4,7},{5,6},{6,5},{7,4},{8,11},{9,10},{10,... | collective-permute-start | bytes 32264 | tf_op jit(solution)/shard_map/ppermute | solution.py:553
  351.2 52.5 %collective-permute-start.54 = (f32[2688]{0:T(1024)S(1)}, f32[2688]{0:T(1024)S(1)}, u32[]{:S(2)}, u32[]{:S(2)}) collective-permute-start(f32[2688]{0:T(1024)S(1)} %get-tuple-element.160), channel_id=1, source_target_pairs={{0,2},{1,3},{2,0},{3,1},{4,6},{5,7},{6,4},{7,5},{8,10},{9,11},{10,... | collective-permute-start | bytes 32264 | tf_op jit(solution)/shard_map/ppermute | solution.py:553
  401.1 21.0 %collective-permute-start.35 = (f32[2,16,768]{2,1,0:T(8,128)S(1)}, f32[2,16,768]{2,1,0:T(8,128)S(1)}, u32[]{:S(2)}, u32[]{:S(2)}) collective-permute-start(f32[2,16,768]{2,1,0:T(8,128)S(1)} %copy-done.31), channel_id=1, source_target_pairs={{8,0},{12,4},{16,8},{20,12},{24,16},{28,20},{9,1},{13,5},{17,9},{2... | collective-permute-start | bytes 294920 | tf_op jit(solution)/shard_map/ppermute | solution.py:558
  402.4 19.7 %collective-permute-start.34 = (f32[2,16,768]{2,1,0:T(8,128)S(1)}, f32[2,16,768]{2,1,0:T(8,128)S(1)}, u32[]{:S(2)}, u32[]{:S(2)}) collective-permute-start(f32[2,16,768]{2,1,0:T(8,128)S(1)} %copy-done.31), channel_id=1, source_target_pairs={{4,0},{8,4},{12,8},{16,12},{20,16},{24,20},{28,24},{5,1},{9,5},{13... | collective-permute-start | bytes 294920 | tf_op jit(solution)/shard_map/ppermute | solution.py:558
  421.0 90.8 %collective-permute-start.67 = (bf16[2,2,2,2,48,768]{5,4,3,2,1,0:T(8,128)(2,1)}, bf16[2,2,2,2,48,768]{5,4,3,2,1,0:T(8,128)(2,1)}, u32[]{:S(2)}, u32[]{:S(2)}) collective-permute-start(bf16[2,2,2,2,48,768]{5,4,3,2,1,0:T(8,128)(2,1)} %fusion.6), channel_id=1, source_target_pairs={{0,1},{1,0},{2,3},{3,2},{4,5},{5,4},{6,7},{7,6},{8,9},{9,8},{10,11... | collective-permute-start | bytes 3538952 | tf_op jit(solution)/shard_map/ppermute | solution.py:553
  421.7 92.0 %collective-permute-start.59 = (bf16[2,2,2,2,24,1536]{5,4,3,2,1,0:T(8,128)(2,1)}, bf16[2,2,2,2,24,1536]{5,4,3,2,1,0:T(8,128)(2,1)}, u32[]{:S(2)}, u32[]{:S(2)}) collective-permute-start(bf16[2,2,2,2,24,1536]{5,4,3,2,1,0:T(8,128)(2,1)} %fusion.5), channel_id=1, source_target_pairs={{0,1},{1,0},{2,3},{3,2},{4,5},{5,4},{6,7},{7,6},{8,9},{9,8},{10,11... | collective-permute-start | bytes 3538952 | tf_op jit(solution)/shard_map/ppermute | solution.py:553
  423.2 9.6 %collective-permute-start.38 = (f32[2,16,768]{2,1,0:T(8,128)S(1)}, f32[2,16,768]{2,1,0:T(8,128)S(1)}, u32[]{:S(2)}, u32[]{:S(2)}) collective-permute-start(f32[2,16,768]{2,1,0:T(8,128)S(1)} %multiply_add_fusion.1), channel_id=1, source_target_pairs={{16,0},{20,4},{24,8},{28,12},{17,1},{21,5},{25,9},{29,13},{18,2},{... | collective-permute-start | bytes 294920 | tf_op jit(solution)/shard_map/ppermute | solution.py:558
  492.6 24.2 %collective-permute-start.75 = (bf16[2,2,2,2,24,1536]{5,4,1,0,2,3:T(8,128)(2,1)}, bf16[2,2,2,2,24,1536]{5,4,1,0,2,3:T(8,128)(2,1)S(1)}, u32[]{:S(2)}, u32[]{:S(2)}) collective-permute-start(bf16[2,2,2,2,24,1536]{5,4,1,0,2,3:T(8,128)(2,1)} %fusion.7), channel_id=1, source_target_pairs={{0,1},{1,0},{2,3},{3,2},{4,5},{5,4},{6,7},{7,6},{8,9},{9,8},{10,11... | collective-permute-start | bytes 3538952 | tf_op jit(solution)/shard_map/ppermute | solution.py:553
  495.0 23.1 %collective-permute-start.83 = (bf16[2,2,2,2,48,768]{5,4,1,2,3,0:T(8,128)(2,1)}, bf16[2,2,2,2,48,768]{5,4,1,2,3,0:T(8,128)(2,1)S(1)}, u32[]{:S(2)}, u32[]{:S(2)}) collective-permute-start(bf16[2,2,2,2,48,768]{5,4,1,2,3,0:T(8,128)(2,1)} %fusion.8), channel_id=1, source_target_pairs={{0,1},{1,0},{2,3},{3,2},{4,5},{5,4},{6,7},{7,6},{8,9},{9,8},{10,11... | collective-permute-start | bytes 3538952 | tf_op jit(solution)/shard_map/ppermute | solution.py:553
  510.6 68.2 %collective-permute-start.45 = (bf16[2,2,2,2,24,3200]{5,4,3,2,1,0:T(8,128)(2,1)S(1)}, bf16[2,2,2,2,24,3200]{5,4,3,2,1,0:T(8,128)(2,1)S(1)}, u32[]{:S(2)}, u32[]{:S(2)}) collective-permute-start(bf16[2,2,2,2,24,3200]{5,4,3,2,1,0:T(8,128)(2,1)S(1)} %copy-done.6), channel_id=1, source_target_pairs={{0,1},{1,0},{2,3},{3,2},{4,5},{5,4},{6,7},{7,6},{8,9},{9,8},{10,11... | collective-permute-start | bytes 7372808 | tf_op jit(solution)/shard_map/ppermute | solution.py:553
  513.6 15.8 %collective-permute-start.68 = (bf16[2,2,2,48,768]{4,3,2,1,0:T(8,128)(2,1)S(1)}, bf16[2,2,2,48,768]{4,3,2,1,0:T(8,128)(2,1)S(1)}, u32[]{:S(2)}, u32[]{:S(2)}) collective-permute-start(bf16[2,2,2,48,768]{4,3,2,1,0:T(8,128)(2,1)S(1)} %fusion.11), channel_id=1, source_target_pairs={{0,8},{4,12},{8,0},{12,4},{16,24},{20,28},{24,16},{28,20},{1,9},{5... | collective-permute-start | bytes 1769480 | tf_op jit(solution)/shard_map/ppermute | solution.py:553
  515.5 16.2 %collective-permute-start.60 = (bf16[2,2,2,24,1536]{4,3,2,1,0:T(8,128)(2,1)S(1)}, bf16[2,2,2,24,1536]{4,3,2,1,0:T(8,128)(2,1)S(1)}, u32[]{:S(2)}, u32[]{:S(2)}) collective-permute-start(bf16[2,2,2,24,1536]{4,3,2,1,0:T(8,128)(2,1)S(1)} %fusion.10), channel_id=1, source_target_pairs={{0,4},{4,0},{8,12},{12,8},{16,20},{20,16},{24,28},{28,24},{1,5},{5... | collective-permute-start | bytes 1769480 | tf_op jit(solution)/shard_map/ppermute | solution.py:553
  517.2 26.7 %collective-permute-start.76 = (bf16[2,2,2,24,1536]{4,3,1,0,2:T(8,128)(2,1)S(1)}, bf16[2,2,2,24,1536]{4,3,1,0,2:T(8,128)(2,1)S(1)}, u32[]{:S(2)}, u32[]{:S(2)}) collective-permute-start(bf16[2,2,2,24,1536]{4,3,1,0,2:T(8,128)(2,1)S(1)} %fusion.12), channel_id=1, source_target_pairs={{0,4},{4,0},{8,12},{12,8},{16,20},{20,16},{24,28},{28,24},{1,5},{5... | collective-permute-start | bytes 1769480 | tf_op jit(solution)/shard_map/ppermute | solution.py:553
  518.5 27.3 %collective-permute-start.84 = (bf16[2,2,2,48,768]{4,3,0,1,2:T(8,128)(2,1)S(1)}, bf16[2,2,2,48,768]{4,3,0,1,2:T(8,128)(2,1)S(1)}, u32[]{:S(2)}, u32[]{:S(2)}) collective-permute-start(bf16[2,2,2,48,768]{4,3,0,1,2:T(8,128)(2,1)S(1)} %fusion.13), channel_id=1, source_target_pairs={{0,2},{1,3},{2,0},{3,1},{4,6},{5,7},{6,4},{7,5},{8,10},{9,11},{10,... | collective-permute-start | bytes 1769480 | tf_op jit(solution)/shard_map/ppermute | solution.py:553
  529.6 17.7 %collective-permute-start.69 = (bf16[2,2,48,768]{3,2,1,0:T(8,128)(2,1)S(1)}, bf16[2,2,48,768]{3,2,1,0:T(8,128)(2,1)S(1)}, u32[]{:S(2)}, u32[]{:S(2)}) collective-permute-start(bf16[2,2,48,768]{3,2,1,0:T(8,128)(2,1)S(1)} %fusion.17), channel_id=1, source_target_pairs={{0,2},{1,3},{2,0},{3,1},{4,6},{5,7},{6,4},{7,5},{8,10},{9,11},{10,... | collective-permute-start | bytes 884744 | tf_op jit(solution)/shard_map/ppermute | solution.py:553
  531.9 16.4 %collective-permute-start.61 = (bf16[2,2,24,1536]{3,2,1,0:T(8,128)(2,1)S(1)}, bf16[2,2,24,1536]{3,2,1,0:T(8,128)(2,1)S(1)}, u32[]{:S(2)}, u32[]{:S(2)}) collective-permute-start(bf16[2,2,24,1536]{3,2,1,0:T(8,128)(2,1)S(1)} %fusion.16), channel_id=1, source_target_pairs={{0,8},{4,12},{8,0},{12,4},{16,24},{20,28},{24,16},{28,20},{1,9},{5... | collective-permute-start | bytes 884744 | tf_op jit(solution)/shard_map/ppermute | solution.py:553
  546.0 9.7 %collective-permute-start.85 = (bf16[2,2,48,768]{3,2,0,1:T(8,128)(2,1)S(1)}, bf16[2,2,48,768]{3,2,0,1:T(8,128)(2,1)S(1)}, u32[]{:S(2)}, u32[]{:S(2)}) collective-permute-start(bf16[2,2,48,768]{3,2,0,1:T(8,128)(2,1)S(1)} %fusion.19), channel_id=1, source_target_pairs={{0,4},{4,0},{8,12},{12,8},{16,20},{20,16},{24,28},{28,24},{1,5},{5... | collective-permute-start | bytes 884744 | tf_op jit(solution)/shard_map/ppermute | solution.py:553
  547.4 9.9 %collective-permute-start.70 = (bf16[2,48,768]{2,1,0:T(8,128)(2,1)S(1)}, bf16[2,48,768]{2,1,0:T(8,128)(2,1)S(1)}, u32[]{:S(2)}, u32[]{:S(2)}) collective-permute-start(bf16[2,48,768]{2,1,0:T(8,128)(2,1)S(1)} %fusion.23), channel_id=1, source_target_pairs={{0,4},{4,0},{8,12},{12,8},{16,20},{20,16},{24,28},{28,24},{1,5},{5... | collective-permute-start | bytes 442376 | tf_op jit(solution)/shard_map/ppermute | solution.py:553
  548.3 11.8 %collective-permute-start.62 = (bf16[2,24,1536]{2,1,0:T(8,128)(2,1)S(1)}, bf16[2,24,1536]{2,1,0:T(8,128)(2,1)S(1)}, u32[]{:S(2)}, u32[]{:S(2)}) collective-permute-start(bf16[2,24,1536]{2,1,0:T(8,128)(2,1)S(1)} %fusion.22), channel_id=1, source_target_pairs={{0,2},{1,3},{2,0},{3,1},{4,6},{5,7},{6,4},{7,5},{8,10},{9,11},{10,... | collective-permute-start | bytes 442376 | tf_op jit(solution)/shard_map/ppermute | solution.py:553
  557.3 11.6 %collective-permute-start.71 = (bf16[48,768]{1,0:T(8,128)(2,1)S(1)}, bf16[48,768]{1,0:T(8,128)(2,1)S(1)}, u32[]{:S(2)}, u32[]{:S(2)}) collective-permute-start(bf16[48,768]{1,0:T(8,128)(2,1)S(1)} %fusion.31), channel_id=1, source_target_pairs={{0,16},{4,20},{8,24},{12,28},{16,0},{20,4},{24,8},{28,12},{1,17},{... | collective-permute-start | bytes 221192 | tf_op jit(solution)/shard_map/ppermute | solution.py:553
  560.2 10.3 %collective-permute-start.63 = (bf16[24,1536]{1,0:T(8,128)(2,1)S(1)}, bf16[24,1536]{1,0:T(8,128)(2,1)S(1)}, u32[]{:S(2)}, u32[]{:S(2)}) collective-permute-start(bf16[24,1536]{1,0:T(8,128)(2,1)S(1)} %fusion.30), channel_id=1, source_target_pairs={{0,16},{4,20},{8,24},{12,28},{16,0},{20,4},{24,8},{28,12},{1,17},{... | collective-permute-start | bytes 221192 | tf_op jit(solution)/shard_map/ppermute | solution.py:553
  560.5 11.5 %collective-permute-start.79 = (bf16[24,1536]{1,0:T(8,128)(2,1)S(1)}, bf16[24,1536]{1,0:T(8,128)(2,1)S(1)}, u32[]{:S(2)}, u32[]{:S(2)}) collective-permute-start(bf16[24,1536]{1,0:T(8,128)(2,1)S(1)} %fusion.32), channel_id=1, source_target_pairs={{0,16},{4,20},{8,24},{12,28},{16,0},{20,4},{24,8},{28,12},{1,17},{... | collective-permute-start | bytes 221192 | tf_op jit(solution)/shard_map/ppermute | solution.py:553
  563.4 9.9 %collective-permute-start.87 = (bf16[48,768]{1,0:T(8,128)(2,1)S(1)}, bf16[48,768]{1,0:T(8,128)(2,1)S(1)}, u32[]{:S(2)}, u32[]{:S(2)}) collective-permute-start(bf16[48,768]{1,0:T(8,128)(2,1)S(1)} %fusion.33), channel_id=1, source_target_pairs={{0,16},{4,20},{8,24},{12,28},{16,0},{20,4},{24,8},{28,12},{1,17},{... | collective-permute-start | bytes 221192 | tf_op jit(solution)/shard_map/ppermute | solution.py:553
  575.5 15.3 %collective-permute-start.65 = (bf16[2,24,1536]{2,1,0:T(8,128)(2,1)S(1)}, bf16[2,24,1536]{2,1,0:T(8,128)(2,1)S(1)}, u32[]{:S(2)}, u32[]{:S(2)}) collective-permute-start(bf16[2,24,1536]{2,1,0:T(8,128)(2,1)S(1)} %pad_maximum_fusion.12), channel_id=1, source_target_pairs={{0,8},{4,12},{8,0},{12,4},{16,24},{20,28},{24,16},{28,20},{1,9},{5... | collective-permute-start | bytes 442376 | tf_op jit(solution)/shard_map/ppermute | solution.py:553
  576.6 16.9 %collective-permute-start.81 = (bf16[2,24,1536]{2,1,0:T(8,128)(2,1)S(1)}, bf16[2,24,1536]{2,1,0:T(8,128)(2,1)S(1)}, u32[]{:S(2)}, u32[]{:S(2)}) collective-permute-start(bf16[2,24,1536]{2,1,0:T(8,128)(2,1)S(1)} %pad_maximum_fusion.14), channel_id=1, source_target_pairs={{0,8},{4,12},{8,0},{12,4},{16,24},{20,28},{24,16},{28,20},{1,9},{5... | collective-permute-start | bytes 442376 | tf_op jit(solution)/shard_map/ppermute | solution.py:553
  577.8 17.3 %collective-permute-start.89 = (bf16[2,48,768]{2,1,0:T(8,128)(2,1)S(1)}, bf16[2,48,768]{2,1,0:T(8,128)(2,1)S(1)}, u32[]{:S(2)}, u32[]{:S(2)}) collective-permute-start(bf16[2,48,768]{2,1,0:T(8,128)(2,1)S(1)} %pad_maximum_fusion.15), channel_id=1, source_target_pairs={{0,8},{4,12},{8,0},{12,4},{16,24},{20,28},{24,16},{28,20},{1,9},{5... | collective-permute-start | bytes 442376 | tf_op jit(solution)/shard_map/ppermute | solution.py:553
  579.5 26.5 %collective-permute-start.46 = (bf16[2,2,2,24,3200]{4,3,2,1,0:T(8,128)(2,1)S(1)}, bf16[2,2,2,24,3200]{4,3,2,1,0:T(8,128)(2,1)S(1)}, u32[]{:S(2)}, u32[]{:S(2)}) collective-permute-start(bf16[2,2,2,24,3200]{4,3,2,1,0:T(8,128)(2,1)S(1)} %fusion.4), channel_id=1, source_target_pairs={{0,2},{1,3},{2,0},{3,1},{4,6},{5,7},{6,4},{7,5},{8,10},{9,11},{10,... | collective-permute-start | bytes 3686408 | tf_op jit(solution)/shard_map/ppermute | solution.py:553
  581.1 48.6 %collective-permute-start.74 = (bf16[4,48,768]{2,1,0:T(8,128)(2,1)S(1)}, bf16[4,48,768]{2,1,0:T(8,128)(2,1)S(1)}, u32[]{:S(2)}, u32[]{:S(2)}) collective-permute-start(bf16[4,48,768]{2,1,0:T(8,128)(2,1)S(1)} %pad_maximum_fusion.8), channel_id=1, source_target_pairs={{0,16},{4,20},{8,24},{12,28},{16,0},{20,4},{24,8},{28,12},{1,17},{... | collective-permute-start | bytes 884744 | tf_op jit(solution)/shard_map/ppermute | solution.py:553
  590.8 32.8 %collective-permute-start.66 = (bf16[4,24,1536]{2,1,0:T(8,128)(2,1)S(1)}, bf16[4,24,1536]{2,1,0:T(8,128)(2,1)S(1)}, u32[]{:S(2)}, u32[]{:S(2)}) collective-permute-start(bf16[4,24,1536]{2,1,0:T(8,128)(2,1)S(1)} %pad_maximum_fusion.7), channel_id=1, source_target_pairs={{0,16},{4,20},{8,24},{12,28},{16,0},{20,4},{24,8},{28,12},{1,17},{... | collective-permute-start | bytes 884744 | tf_op jit(solution)/shard_map/ppermute | solution.py:553
  593.5 35.8 %collective-permute-start.82 = (bf16[4,24,1536]{2,1,0:T(8,128)(2,1)S(1)}, bf16[4,24,1536]{2,1,0:T(8,128)(2,1)S(1)}, u32[]{:S(2)}, u32[]{:S(2)}) collective-permute-start(bf16[4,24,1536]{2,1,0:T(8,128)(2,1)S(1)} %pad_maximum_fusion.9), channel_id=1, source_target_pairs={{0,16},{4,20},{8,24},{12,28},{16,0},{20,4},{24,8},{28,12},{1,17},{... | collective-permute-start | bytes 884744 | tf_op jit(solution)/shard_map/ppermute | solution.py:553
  595.1 37.4 %collective-permute-start.90 = (bf16[4,48,768]{2,1,0:T(8,128)(2,1)S(1)}, bf16[4,48,768]{2,1,0:T(8,128)(2,1)S(1)}, u32[]{:S(2)}, u32[]{:S(2)}) collective-permute-start(bf16[4,48,768]{2,1,0:T(8,128)(2,1)S(1)} %pad_maximum_fusion.10), channel_id=1, source_target_pairs={{0,16},{4,20},{8,24},{12,28},{16,0},{20,4},{24,8},{28,12},{1,17},{... | collective-permute-start | bytes 884744 | tf_op jit(solution)/shard_map/ppermute | solution.py:553
  606.3 23.1 %collective-permute-start.47 = (bf16[2,2,24,3200]{3,2,1,0:T(8,128)(2,1)S(1)}, bf16[2,2,24,3200]{3,2,1,0:T(8,128)(2,1)S(1)}, u32[]{:S(2)}, u32[]{:S(2)}) collective-permute-start(bf16[2,2,24,3200]{3,2,1,0:T(8,128)(2,1)S(1)} %fusion.9), channel_id=1, source_target_pairs={{0,4},{4,0},{8,12},{12,8},{16,20},{20,16},{24,28},{28,24},{1,5},{5... | collective-permute-start | bytes 1843208 | tf_op jit(solution)/shard_map/ppermute | solution.py:553
  662.4 28.1 %collective-permute-start.52 = (bf16[4,24,3200]{2,1,0:T(8,128)(2,1)S(1)}, bf16[4,24,3200]{2,1,0:T(8,128)(2,1)S(1)}, u32[]{:S(2)}, u32[]{:S(2)}) collective-permute-start(bf16[4,24,3200]{2,1,0:T(8,128)(2,1)S(1)} %pad_maximum_fusion.1), channel_id=1, source_target_pairs={{0,16},{4,20},{8,24},{12,28},{16,0},{20,4},{24,8},{28,12},{1,17},{... | collective-permute-start | bytes 1843208 | tf_op jit(solution)/shard_map/ppermute | solution.py:553
  (72 other events, 1222.0 us)

commit v2 on v1

--- a/solution.py
+++ b/solution.py
@@ -61,7 +61,8 @@
         c = qT*c + e_ref[0, pl.ds(k,H,stride=CH), :]
     s_ref[0] = c
 
-def fwd_kernel(H, T, x_ref, q_ref, w_ref, om_ref, e_ref, c_ref, xp_ref, p_ref, f_ref, scr, cs, ps):
+def fwd_kernel(H, T, x_ref, q_ref, w_ref, om_ref, e_ref, c_ref, *refs):
+    xp_ref, p_ref, f_ref, scr, cs, ps = refs[-6:]
     spread(scr, x_ref[0].astype(F32), T)
     qT = power(q_ref[...], T)
     c = c_ref[0]
@@ -105,7 +106,8 @@
         c = qT*c + e_ref[0, pl.ds(k,H,stride=CH), :]
     s_ref[0] = c
 
-def bwd_kernel(H, T, d_ref, x_ref, q_ref, qi_ref, w_ref, om_ref, f_ref, e_ref, c_ref, dx_ref, s1_ref, s3_ref, go_ref, scr, cs, dx, ds):
+def bwd_kernel(H, T, d_ref, x_ref, q_ref, qi_ref, w_ref, om_ref, f_ref, e_ref, c_ref, *refs):
+    dx_ref, s1_ref, s3_ref, go_ref, scr, cs, dx, ds = refs[-8:]
     g = pl.program_id(1)
     x = x_ref[0].astype(F32)
     spread(scr, x, T)
@@ -154,39 +156,97 @@
             s3_ref[h:h+1,:] += jnp.sum(a3[i],axis=0,keepdims=True)
     dx_ref[0] = collect(dx, T).astype(dx_ref.dtype)
 
-def specs(L,H):
-    blk = pl.BlockSpec((1,L,LANES), lambda c,g:(g,0,c))
-    par = pl.BlockSpec((H,LANES), lambda c,g:(0,c))
-    one = pl.BlockSpec((1,LANES), lambda c,g:(0,c))
-    st = pl.BlockSpec((1,H*CH,LANES), lambda c,g:(g,0,c))
-    car = pl.BlockSpec((1,H,LANES), lambda c,g:(g,0,c))
-    return blk,par,one,st,car
-
-def ema_ends(x,q):
-    G,L,C=x.shape; H=q.shape[0]
-    blk,par,one,st,car=specs(L,H)
-    return pl.pallas_call(functools.partial(ends_kernel,H,L//CH), grid=(C//LANES,G), in_specs=[blk,par], out_specs=[st,car],
-      out_shape=[jax.ShapeDtypeStruct((G,H*CH,C),F32),jax.ShapeDtypeStruct((G,H,C),F32)], scratch_shapes=[pltpu.VMEM((L+CH*PAD,LANES),F32)], name="ema_ends")(x,q)
-
-def ema_forward(x,q,w,om,e,c):
-    G,L,C=x.shape; H=q.shape[0]
-    blk,par,one,st,car=specs(L,H)
-    return pl.pallas_call(functools.partial(fwd_kernel,H,L//CH), grid=(C//LANES,G), in_specs=[blk,par,par,one,st,car], out_specs=[blk,blk,st],
-      out_shape=[jax.ShapeDtypeStruct((G,L,C),jnp.bfloat16),jax.ShapeDtypeStruct((G,L,C),F32),jax.ShapeDtypeStruct((G,H*CH,C),F32)],
-      scratch_shapes=[pltpu.VMEM((L+CH*PAD,LANES),F32),pltpu.VMEM((H*CH,LANES),F32),pltpu.VMEM((L+CH*PAD,LANES),F32)], name="ema_fwd")(x,q,w,om,e,c)
-
-def ema_back_ends(dxp,p,q):
-    G,L,C=p.shape; H=q.shape[0]
-    blk,par,one,st,car=specs(L,H)
-    return pl.pallas_call(functools.partial(bends_kernel,H,L//CH), grid=(C//LANES,G), in_specs=[blk,blk,par], out_specs=[blk,st,car],
-      out_shape=[jax.ShapeDtypeStruct((G,L,C),F32),jax.ShapeDtypeStruct((G,H*CH,C),F32),jax.ShapeDtypeStruct((G,H,C),F32)], scratch_shapes=[pltpu.VMEM((L+CH*PAD,LANES),F32)], name="ema_bends")(dxp,p,q)
-
-def ema_backward(d,x,q,qi,w,om,f,e,c):
-    G,L,C=x.shape; H=q.shape[0]
-    blk,par,one,st,car=specs(L,H)
-    return pl.pallas_call(functools.partial(bwd_kernel,H,L//CH), grid=(C//LANES,G), in_specs=[blk,blk,par,par,par,one,st,st,car], out_specs=[blk,par,par,one],
-      out_shape=[jax.ShapeDtypeStruct((G,L,C),jnp.bfloat16),jax.ShapeDtypeStruct((H,C),F32),jax.ShapeDtypeStruct((H,C),F32),jax.ShapeDtypeStruct((1,C),F32)],
-      scratch_shapes=[pltpu.VMEM((L+CH*PAD,LANES),F32),pltpu.VMEM((H*CH,LANES),F32),pltpu.VMEM((L+CH*PAD,LANES),F32),pltpu.VMEM((L+CH*PAD,LANES),F32)], name="ema_bwd")(d,x,q,qi,w,om,f,e,c)
+def specs(L, H, first=0):
+    blk = pl.BlockSpec((1, L, LANES), lambda c, g: (g, 0, c + first))
+    par = pl.BlockSpec((H, LANES), lambda c, g: (0, c + first))
+    one = pl.BlockSpec((1, LANES), lambda c, g: (0, c + first))
+    st = pl.BlockSpec((1, H * CH, LANES), lambda c, g: (g, 0, c + first))
+    car = pl.BlockSpec((1, H, LANES), lambda c, g: (g, 0, c + first))
+    return blk, par, one, st, car
+
+
+def ema_ends(x, q):
+    G, L, C = x.shape
+    H = q.shape[0]
+    blk, par, one, st, car = specs(L, H)
+    return pl.pallas_call(
+        functools.partial(ends_kernel, H, L // CH),
+        grid=(C // LANES, G),
+        in_specs=[blk, par],
+        out_specs=[st, car],
+        out_shape=[jax.ShapeDtypeStruct((G, H * CH, C), F32), jax.ShapeDtypeStruct((G, H, C), F32)],
+        scratch_shapes=[pltpu.VMEM((L + CH * PAD, LANES), F32)],
+        cost_estimate=cost_of(0, 11),
+        name="ema_ends",
+    )(x, q)
+
+
+def ema_forward(span, so_far, x, q, w, om, e, c):
+    G, L, C = x.shape
+    H = q.shape[0]
+    first, count = span
+    blk, par, one, st, car = specs(L, H, first)
+    return pl.pallas_call(
+        functools.partial(fwd_kernel, H, L // CH),
+        grid=(count, G),
+        in_specs=[blk, par, par, one, st, car] + [pl.BlockSpec(memory_space=pl.ANY)] * len(so_far),
+        out_specs=[blk, blk, st],
+        out_shape=[
+            jax.ShapeDtypeStruct((G, L, C), BF16), jax.ShapeDtypeStruct((G, L, C), F32),
+            jax.ShapeDtypeStruct((G, H * CH, C), F32),
+        ],
+        scratch_shapes=[
+            pltpu.VMEM((L + CH * PAD, LANES), F32), pltpu.VMEM((H * CH, LANES), F32),
+            pltpu.VMEM((L + CH * PAD, LANES), F32),
+        ],
+        input_output_aliases={6 + k: k for k in range(len(so_far))},
+        cost_estimate=cost_of(0, 3 * count),
+        name="ema_forward",
+    )(x, q, w, om, e, c, *so_far)
+
+
+def ema_back_ends(dxp, p, q):
+    G, L, C = p.shape
+    H = q.shape[0]
+    blk, par, one, st, car = specs(L, H)
+    return pl.pallas_call(
+        functools.partial(bends_kernel, H, L // CH),
+        grid=(C // LANES, G),
+        in_specs=[blk, blk, par],
+        out_specs=[blk, st, car],
+        out_shape=[
+            jax.ShapeDtypeStruct((G, L, C), F32), jax.ShapeDtypeStruct((G, H * CH, C), F32),
+            jax.ShapeDtypeStruct((G, H, C), F32),
+        ],
+        scratch_shapes=[pltpu.VMEM((L + CH * PAD, LANES), F32)],
+        cost_estimate=cost_of(0, 15),
+        name="ema_back_ends",
+    )(dxp, p, q)
+
+
+def ema_backward(span, so_far, d, x, q, qi, w, om, f, e, c):
+    G, L, C = x.shape
+    H = q.shape[0]
+    first, count = span
+    blk, par, one, st, car = specs(L, H, first)
+    return pl.pallas_call(
+        functools.partial(bwd_kernel, H, L // CH),
+        grid=(count, G),
+        in_specs=[blk, blk, par, par, par, one, st, st, car]
+        + [pl.BlockSpec(memory_space=pl.ANY)] * len(so_far),
+        out_specs=[blk, par, par, one],
+        out_shape=[
+            jax.ShapeDtypeStruct((G, L, C), BF16), jax.ShapeDtypeStruct((H, C), F32),
+            jax.ShapeDtypeStruct((H, C), F32), jax.ShapeDtypeStruct((1, C), F32),
+        ],
+        scratch_shapes=[
+            pltpu.VMEM((L + CH * PAD, LANES), F32), pltpu.VMEM((H * CH, LANES), F32),
+            pltpu.VMEM((L + CH * PAD, LANES), F32), pltpu.VMEM((L + CH * PAD, LANES), F32),
+        ],
+        input_output_aliases={9 + k: k for k in range(len(so_far))},
+        cost_estimate=cost_of(0, 8 * count),
+        name="ema_backward",
+    )(d, x, q, qi, w, om, f, e, c, *so_far)
 
 
 def sig(v):
@@ -222,21 +282,17 @@
     )
     copies = []
     for n, (piece, start) in enumerate(spots):
-        size = piece.shape[0]
-        copies.append(
-            pltpu.make_async_copy(
-                piece, target.at[pl.ds(pl.multiple_of(start, 32), size), :], sem.at[first + n]
-            )
-        )
+        rows_at = pl.ds(pl.multiple_of(start, 32), piece.shape[0])
+        copies.append(pltpu.make_async_copy(piece, target.at[rows_at, :], sem.at[first + n]))
     return copies
 
 
-def bring(groups, sem):
+def bring(pieces, targets, sem):
     @pl.when(pl.program_id(0) == 0)
     def _():
         copies = []
-        for n, (pieces, target) in enumerate(groups):
-            copies.extend(piece_copies(pieces, target, sem, 6 * n))
+        for n, target in enumerate(targets):
+            copies.extend(piece_copies(pieces[6 * n : 6 * n + 6], target, sem, 6 * n))
         for copy in copies:
             copy.start()
         for copy in copies:
@@ -258,7 +314,7 @@
     D, Z, V = dims
     pieces, refs = refs[:18], refs[18:]
     u_ref, h_ref, r_ref, v_ref, z_ref, p_ref, m_ref, wm, wv, wo, sem = refs
-    bring(((pieces[:6], wm), (pieces[6:12], wv), (pieces[12:], wo)), sem)
+    bring(pieces, (wm, wv, wo), sem)
     xp = xp_ref[...]
     x = x_ref[...]
     z = dot_nn(xp, wm[:, D : D + Z]) + bm_ref[:, D : D + Z]
@@ -293,14 +349,22 @@
     h_ref[...] = dot_nn(xp, wm[:, D + Z + V :]) + bm_ref[:, D + Z + V :] + dot_nn(m_ref[...], wo[...])
 
 
+def slope_of(pre, logistic):
+    return logistic * (1.0 + pre * (1.0 - logistic))
+
+
+def mean_of(rows):
+    return jnp.mean(rows, axis=-1, keepdims=True)
+
+
 def ffn_kernel(R, dims, x_ref, u_ref, h_ref, cot_ref, live_ref, gn_ref, bf_ref, bo_ref, *refs):
     D, FF = dims
     pieces, refs = refs[:12], refs[12:]
     (
-        o_ref, h1_ref, act_ref, dg_ref, df_ref, dm_ref, du_ref, dt_ref, sd_ref, sf_ref,
+        o_ref, h1_ref, act_ref, dg_ref, df_ref, dum_ref, dt_ref, sd_ref, sf_ref,
         wi, wo, f_scr, n1_scr, a_scr, i1_scr, sem,
     ) = refs
-    bring(((pieces[:6], wi), (pieces[6:], wo)), sem)
+    bring(pieces, (wi, wo), sem)
 
     @pl.when(pl.program_id(0) == 0)
     def _():
@@ -308,130 +372,155 @@
         sf_ref[...] = jnp.zeros_like(sf_ref)
 
     g1, g2, b1, b2 = (gn_ref[k : k + 1, :] for k in range(4))
-
-    def first(s, _):
-        at = pl.ds(pl.multiple_of(s * STRIP, STRIP), STRIP)
-        x = x_ref[at, :].astype(F32)
-        h = h_ref[at, :]
-        y = x + sig(u_ref[at, :]) * (h * sig(h) - x)
-        center = y - jnp.mean(y, axis=-1, keepdims=True)
-        inverse = lax.rsqrt(jnp.mean(center * center, axis=-1, keepdims=True) + EPSILON)
-        n1 = center * inverse
-        n1_scr[at, :] = n1
-        i1_scr[at, :] = jnp.broadcast_to(inverse, (STRIP, 128))
-        h1_ref[at, :] = (n1 * g1 + b1).astype(BF16)
-        return 0
-
-    lax.fori_loop(0, R // STRIP, first, 0, unroll=2)
-    for c in range(0, FF, CHUNK):
-        at = slice(c, c + CHUNK)
-        f = dot_nn(h1_ref[...], wi[:, at]) + bf_ref[:, at]
-        f_scr[:, at] = f
-        act_ref[:, at] = (f * sig(f)).astype(BF16)
-    a_scr[...] = dot_nn(act_ref[...], wo[...])
-
-    def second(s, sums):
-        at = pl.ds(pl.multiple_of(s * STRIP, STRIP), STRIP)
-        y2 = n1_scr[at, :] * g1 + b1 + a_scr[at, :] + bo_ref[...]
-        center = y2 - jnp.mean(y2, axis=-1, keepdims=True)
-        inverse = lax.rsqrt(jnp.mean(center * center, axis=-1, keepdims=True) + EPSILON)
-        n2 = center * inverse
-        live = live_ref[at, :]
-        o_ref[at, :] = ((n2 * g2 + b2) * live).astype(BF16)
-        dn = cot_ref[at, :].astype(F32) * live
-        w = dn * g2
-        dy2 = inverse * (
-            w - jnp.mean(w, axis=-1, keepdims=True) - n2 * jnp.mean(w * n2, axis=-1, keepdims=True)
-        )
-        a_scr[at, :] = dy2
-        dg_ref[at, :] = dy2.astype(BF16)
-        s_gain, s_shift, s_bias = sums
-        return s_gain + fold(dn * n2), s_shift + fold(dn), s_bias + fold(dy2)
-
-    zero = jnp.zeros((8, D), F32)
-    s_gain, s_shift, s_bias = lax.fori_loop(0, R // STRIP, second, (zero, zero, zero), unroll=2)
-    sd_ref[1:2, :] += jnp.sum(s_gain, axis=0, keepdims=True)
-    sd_ref[3:4, :] += jnp.sum(s_shift, axis=0, keepdims=True)
-    sd_ref[4:5, :] += jnp.sum(s_bias, axis=0, keepdims=True)
-    for c in range(0, FF, CHUNK):
-        at = slice(c, c + CHUNK)
-        f = f_scr[:, at]
-        s = sig(f)
-        df = (dot_nt(dg_ref[...], wo[at, :]) * (s * (1.0 + f * (1.0 - s)))).astype(BF16)
-        df_ref[:, at] = df
-        add_sums(sf_ref, at, df.astype(F32))
-    a_scr[...] += dot_nt(df_ref[...], wi[...])
-
-    def third(k, sums):
-        at = pl.ds(pl.multiple_of(k * STRIP, STRIP), STRIP)
-        dh1 = a_scr[at, :]
-        n1 = n1_scr[at, :]
-        w = dh1 * g1
-        dy = i1_scr[at, 0:1] * (
-            w - jnp.mean(w, axis=-1, keepdims=True) - n1 * jnp.mean(w * n1, axis=-1, keepdims=True)
-        )
-        x = x_ref[at, :].astype(F32)
-        h = h_ref[at, :]
-        sh = sig(h)
-        gate = sig(u_ref[at, :])
-        rest = 1.0 - gate
-        dyg = dy * gate
-        dm_ref[at, :] = (dyg * (sh * (1.0 + h * (1.0 - sh)))).astype(BF16)
-        du_ref[at, :] = (dyg * (h * sh - x) * rest).astype(BF16)
-        dt_ref[at, :] = dy * rest
-        s_gain, s_shift = sums
-        return s_gain + fold(dh1 * n1), s_shift + fold(dh1)
-
-    s_gain, s_shift = lax.fori_loop(0, R // STRIP, third, (zero, zero), unroll=2)
-    sd_ref[0:1, :] += jnp.sum(s_gain, axis=0, keepdims=True)
-    sd_ref[2:3, :] += jnp.sum(s_shift, axis=0, keepdims=True)
-
-
-def mix_bwd_kernel(R, dims, dm_ref, du_ref, dt_ref, r_ref, v_ref, z_ref, p_ref, qk_ref, *refs):
+    part = min(256, R)
+
+    def strips(s):
+        return [slice(k, k + STRIP) for k in range(s * part, (s + 1) * part, STRIP)]
+
+    def first(s):
+        for at in strips(s):
+            x = x_ref[at, :].astype(F32)
+            h = h_ref[at, :]
+            y = x + sig(u_ref[at, :]) * (h * sig(h) - x)
+            center = y - mean_of(y)
+            inverse = lax.rsqrt(mean_of(center * center) + EPSILON)
+            n1 = center * inverse
+            n1_scr[at, :] = n1
+            i1_scr[at, :] = jnp.broadcast_to(inverse, (STRIP, LANES))
+            h1_ref[at, :] = (n1 * g1 + b1).astype(BF16)
+
+    def spread(s):
+        rows = slice(s * part, (s + 1) * part)
+        for c in range(0, FF, CHUNK):
+            at = slice(c, c + CHUNK)
+            f = dot_nn(h1_ref[rows, :], wi[:, at]) + bf_ref[:, at]
+            f_scr[rows, at] = f
+            act_ref[rows, at] = (f * sig(f)).astype(BF16)
+
+    def narrow(s):
+        rows = slice(s * part, (s + 1) * part)
+        a_scr[rows, :] = dot_nn(act_ref[rows, :], wo[...])
+
+    def second(s):
+        zero = jnp.zeros((8, D), F32)
+        s_gain, s_shift, s_bias = zero, zero, zero
+        for at in strips(s):
+            y2 = n1_scr[at, :] * g1 + b1 + a_scr[at, :] + bo_ref[...]
+            center = y2 - mean_of(y2)
+            inverse = lax.rsqrt(mean_of(center * center) + EPSILON)
+            n2 = center * inverse
+            live = live_ref[at, :]
+            o_ref[at, :] = ((n2 * g2 + b2) * live).astype(BF16)
+            dn = cot_ref[at, :].astype(F32) * live
+            w = dn * g2
+            dy2 = inverse * (w - mean_of(w) - n2 * mean_of(w * n2))
+            a_scr[at, :] = dy2
+            dg_ref[at, :] = dy2.astype(BF16)
+            s_gain, s_shift, s_bias = s_gain + fold(dn * n2), s_shift + fold(dn), s_bias + fold(dy2)
+        sd_ref[1:2, :] += jnp.sum(s_gain, axis=0, keepdims=True)
+        sd_ref[3:4, :] += jnp.sum(s_shift, axis=0, keepdims=True)
+        sd_ref[4:5, :] += jnp.sum(s_bias, axis=0, keepdims=True)
+
+    def spread_back(s):
+        rows = slice(s * part, (s + 1) * part)
+        for c in range(0, FF, CHUNK):
+            at = slice(c, c + CHUNK)
+            f = f_scr[rows, at]
+            df = (dot_nt(dg_ref[rows, :], wo[at, :]) * slope_of(f, sig(f))).astype(BF16)
+            df_ref[rows, at] = df
+            add_sums(sf_ref, at, df.astype(F32))
+
+    def narrow_back(s):
+        rows = slice(s * part, (s + 1) * part)
+        a_scr[rows, :] += dot_nt(df_ref[rows, :], wi[...])
+
+    def third(s):
+        zero = jnp.zeros((8, D), F32)
+        s_gain, s_shift = zero, zero
+        for at in strips(s):
+            dh1 = a_scr[at, :]
+            n1 = n1_scr[at, :]
+            w = dh1 * g1
+            dy = i1_scr[at, 0:1] * (w - mean_of(w) - n1 * mean_of(w * n1))
+            x = x_ref[at, :].astype(F32)
+            h = h_ref[at, :]
+            sh = sig(h)
+            gate = sig(u_ref[at, :])
+            rest = 1.0 - gate
+            dyg = dy * gate
+            dum_ref[at, :D] = (dyg * (h * sh - x) * rest).astype(BF16)
+            dum_ref[at, D:] = (dyg * slope_of(h, sh)).astype(BF16)
+            dt_ref[at, :] = dy * rest
+            s_gain, s_shift = s_gain + fold(dh1 * n1), s_shift + fold(dh1)
+        sd_ref[0:1, :] += jnp.sum(s_gain, axis=0, keepdims=True)
+        sd_ref[2:3, :] += jnp.sum(s_shift, axis=0, keepdims=True)
+
+    stages = (first, spread, narrow, second, spread_back, narrow_back, third)
+    count = R // part
+    for tick in range(len(stages) + count - 1):
+        for s in range(count):
+            if 0 <= tick - s < len(stages):
+                stages[tick - s](s)
+
+
+def mix_bwd_kernel(R, dims, dum_ref, dt_ref, r_ref, v_ref, z_ref, p_ref, qk_ref, *refs):
     D, Z, V = dims
     pieces, refs = refs[:18], refs[18:]
-    db_ref, dv_ref, dxp_ref, do_ref, sm_ref, sv_ref, sq_ref, ss_ref, wm, wv, wo, sem = refs
-    bring(((pieces[:6], wm), (pieces[6:12], wv), (pieces[12:], wo)), sem)
+    db_ref, dv_ref, dxp_ref, do_ref, sm_ref, sv_ref, sq_ref, ss_ref, wm, wv, wo, acc, sem = refs
+    bring(pieces, (wm, wv, wo), sem)
 
     @pl.when(pl.program_id(0) == 0)
     def _():
         for ref in (sm_ref, sv_ref, sq_ref, ss_ref):
             ref[...] = jnp.zeros_like(ref)
 
-    dm = dm_ref[...]
-    du = du_ref[...]
-    db_ref[:, :D] = du
-    db_ref[:, D + Z + V :] = dm
-    add_sums(sm_ref, slice(0, D), du.astype(F32))
-    add_sums(sm_ref, slice(D + Z + V, 2 * D + Z + V), dm.astype(F32))
+    last = D + Z + V
     blocks = [slice(b * BLOCK, (b + 1) * BLOCK) for b in range(R // BLOCK)]
     full = [p_ref[rows, :] for rows in blocks]
     probs = [prob.astype(BF16) for prob in full]
     dprob = [jnp.zeros((BLOCK, BLOCK), F32) for _ in blocks]
-    for c in range(0, V, CHUNK):
-        at = slice(c, c + CHUNK)
-        rat = slice(D + Z + c, D + Z + c + CHUNK)
-        dmix = dot_nt(dm, wo[at, :])
-        r = r_ref[:, at]
-        v = v_ref[:, at]
-        sr = sig(r)
-        sv = sig(v)
-        value = (v * sv).astype(BF16)
-        datt = (dmix * (r * sr)).astype(BF16)
-        turned = dmix * (sr * (1.0 + r * (1.0 - sr)))
-        slope = sv * (1.0 + v * (1.0 - sv))
-        sum_r = jnp.zeros((1, CHUNK), F32)
-        sum_v = jnp.zeros((1, CHUNK), F32)
+    size = 512
+
+    def chunk(c):
+        at = slice(c, c + size)
+        rat = slice(D + Z + c, D + Z + c + size)
+        zat = slice(Z + c, Z + c + size)
+        dmix = dot_nt(dum_ref[:, D:], wo[at, :])
+        sum_r = jnp.zeros((1, size), F32)
+        sum_v = jnp.zeros((1, size), F32)
         for b, rows in enumerate(blocks):
-            dr = (turned[rows] * dot_nn(probs[b], value[rows])).astype(BF16)
-            db_ref[rows, rat] = dr
+            r = r_ref[rows, at]
+            v = v_ref[rows, at]
+            sr = sig(r)
+            sv = sig(v)
+            value = (v * sv).astype(BF16)
+            datt = (dmix[rows] * (r * sr)).astype(BF16)
+            dr = (dmix[rows] * slope_of(r, sr) * dot_nn(probs[b], value)).astype(BF16)
+            db_ref[rows, zat] = dr
             sum_r += jnp.sum(dr.astype(F32), axis=0, keepdims=True)
-            dprob[b] += dot_nt(datt[rows], value[rows])
-            dv = (dot_tn(probs[b], datt[rows]) * slope[rows]).astype(BF16)
+            dprob[b] += dot_nt(datt, value)
+            dv = (dot_tn(probs[b], datt) * slope_of(v, sv)).astype(BF16)
             dv_ref[rows, at] = dv
             sum_v += jnp.sum(dv.astype(F32), axis=0, keepdims=True)
         sm_ref[:, rat] += sum_r
         sv_ref[:, at] += sum_v
+
+    def give(c):
+        at = slice(c, c + size)
+        rat = slice(D + Z + c, D + Z + c + size)
+        zat = slice(Z + c, Z + c + size)
+        acc[...] += dot_nt(db_ref[:, zat], wm[:, rat])
+        do_ref[...] += dot_nt(dv_ref[:, at], wv[:, at])
+
+    starts = list(range(0, V, size))
+    chunk(starts[0])
+    acc[...] = dot_nt(dum_ref[:, :D], wm[:, :D]) + dot_nt(dum_ref[:, D:], wm[:, last:])
+    do_ref[...] = dt_ref[...]
+    for n, c in enumerate(starts[1:]):
+        chunk(c)
+        give(starts[n])
+    add_sums(sm_ref, slice(0, D), dum_ref[:, :D].astype(F32))
+    add_sums(sm_ref, slice(last, D + last), dum_ref[:, D:].astype(F32))
     for b, rows in enumerate(blocks):
         z = z_ref[rows, :]
         sz = sig(z)
@@ -446,12 +535,16 @@
         sq_ref[0:1, :] += jnp.sum(dq * shared, axis=0, keepdims=True)
         sq_ref[1:2, :] += jnp.sum(dk * shared, axis=0, keepdims=True)
         sq_ref[2:3, :] += jnp.sum(dq, axis=0, keepdims=True)
-        dz = (dq * qk_ref[0:1, :] + dk * qk_ref[1:2, :]) * (sz * (1.0 + z * (1.0 - sz)))
+        dz = (dq * qk_ref[0:1, :] + dk * qk_ref[1:2, :]) * slope_of(z, sz)
         dz = dz.astype(BF16)
-        db_ref[rows, D : D + Z] = dz
+        db_ref[rows, :Z] = dz
         add_sums(sm_ref, slice(D, D + Z), dz.astype(F32))
-    do_ref[...] = dt_ref[...] + dot_nt(dv_ref[...], wv[...])
-    dxp_ref[...] = dot_nt(db_ref[...], wm[...]).astype(BF16)
+    give(starts[-1])
+    dxp_ref[...] = (acc[...] + dot_nt(db_ref[:, :Z], wm[:, D : D + Z])).astype(BF16)
+
+
+def cost_of(flops, microseconds):
+    return pl.CostEstimate(flops=flops, bytes_accessed=microseconds * 3_600_000, transcendentals=0)
 
 
 def any_specs(n):
@@ -489,7 +582,7 @@
             pltpu.SemaphoreType.DMA((18,)),
         ],
         compiler_params=pltpu.CompilerParams(vmem_limit_bytes=VMEM_LIMIT),
-        cost_estimate=pl.CostEstimate(flops=2 * T * D * (E + 2 * V), bytes_accessed=40 * T * D, transcendentals=T * (E + V)),
+        cost_estimate=cost_of(2 * T * D * (E + 2 * V), 33),
         name="mix_forward",
     )(x, xp, bm, bv, qk, rel, *pieces)
 
@@ -503,25 +596,25 @@
         in_specs=[tile(R, D), tile(R, D), tile(R, D), tile(R, D), tile(R, 1), fixed(8, D), fixed(1, FF), fixed(1, D)]
         + any_specs(12),
         out_specs=[
-            tile(R, D), tile(R, D), tile(R, FF), tile(R, D), tile(R, FF), tile(R, D), tile(R, D), tile(R, D),
+            tile(R, D), tile(R, D), tile(R, FF), tile(R, D), tile(R, FF), tile(R, 2 * D), tile(R, D),
             fixed(8, D), fixed(1, FF),
         ],
         out_shape=[
             shape(T, D, BF16), shape(T, D, BF16), shape(T, FF, BF16), shape(T, D, BF16), shape(T, FF, BF16),
-            shape(T, D, BF16), shape(T, D, BF16), shape(T, D), shape(8, D), shape(1, FF),
+            shape(T, 2 * D, BF16), shape(T, D), shape(8, D), shape(1, FF),
         ],
         scratch_shapes=[
             pltpu.VMEM((D, FF), BF16), pltpu.VMEM((FF, D), BF16), pltpu.VMEM((R, FF), F32), pltpu.VMEM((R, D), F32),
             pltpu.VMEM((R, D), F32), pltpu.VMEM((R, 128), F32), pltpu.SemaphoreType.DMA((12,)),
         ],
         compiler_params=pltpu.CompilerParams(vmem_limit_bytes=VMEM_LIMIT),
-        cost_estimate=pl.CostEstimate(flops=8 * T * D * FF, bytes_accessed=40 * T * D, transcendentals=T * 2 * FF),
+        cost_estimate=cost_of(2 * T * D * 4 * FF, 50),
         name="ffn_both",
     )(x, u, h, cot, live, norms, bf, bo, *pieces)
 
 
-def mix_backward(R, dm, du, dt, r, v, z, p, qk, pieces):
-    T, D = dm.shape
+def mix_backward(R, dum, dt, r, v, z, p, qk, pieces):
+    T, D = dt.shape
     V = r.shape[1]
     Z = qk.shape[1]
     E = 2 * D + Z + V
@@ -529,24 +622,24 @@
         functools.partial(mix_bwd_kernel, R, (D, Z, V)),
         grid=(T // R,),
         in_specs=[
-            tile(R, D), tile(R, D), tile(R, D), tile(R, V), tile(R, V), tile(R, Z), tile(R, BLOCK), fixed(8, Z),
+            tile(R, 2 * D), tile(R, D), tile(R, V), tile(R, V), tile(R, Z), tile(R, BLOCK), fixed(8, Z),
         ]
         + any_specs(18),
         out_specs=[
-            tile(R, E), tile(R, V), tile(R, D), tile(R, D), fixed(1, E), fixed(1, V), fixed(8, Z), fixed(BLOCK, BLOCK),
+            tile(R, Z + V), tile(R, V), tile(R, D), tile(R, D), fixed(1, E), fixed(1, V), fixed(8, Z), fixed(BLOCK, BLOCK),
         ],
         out_shape=[
-            shape(T, E, BF16), shape(T, V, BF16), shape(T, D, BF16), shape(T, D), shape(1, E), shape(1, V),
+            shape(T, Z + V, BF16), shape(T, V, BF16), shape(T, D, BF16), shape(T, D), shape(1, E), shape(1, V),
             shape(8, Z), shape(BLOCK, BLOCK),
         ],
         scratch_shapes=[
-            pltpu.VMEM((D, E), BF16), pltpu.VMEM((D, V), BF16), pltpu.VMEM((V, D), BF16),
+            pltpu.VMEM((D, E), BF16), pltpu.VMEM((D, V), BF16), pltpu.VMEM((V, D), BF16), pltpu.VMEM((R, D), F32),
             pltpu.SemaphoreType.DMA((18,)),
         ],
         compiler_params=pltpu.CompilerParams(vmem_limit_bytes=VMEM_LIMIT),
-        cost_estimate=pl.CostEstimate(flops=2 * T * D * (E + 2 * V), bytes_accessed=40 * T * D, transcendentals=T * 2 * V),
+        cost_estimate=cost_of(2 * T * D * (E + 2 * V), 40),
         name="mix_backward",
-    )(dm, du, dt, r, v, z, p, qk, *pieces)
+    )(dum, dt, r, v, z, p, qk, *pieces)
 
 
 def exchange(value, axis, step):
@@ -558,20 +651,30 @@
     return lax.ppermute(value, axis, [(k, k + step) for k in range(n) if 0 <= k + step < n])
 
 
-def weight_pieces(own):
+def join(*values):
+    return lax.optimization_barrier(values)
+
+
+def own_half(own):
     half = own.shape[0] // 2
-    bit = lax.rem(lax.axis_index("seq"), 2)
-    part = lax.dynamic_slice_in_dim(own, bit * half, half, 0)
-    across = exchange(part, "wsh", 2)
-    across_y = exchange(across, "seq", 1)
-    core = exchange(own, "wsh", 1)
-    return (own, core, across, across_y, exchange(across, "wsh", 1), exchange(across_y, "wsh", 1))
+    return lax.dynamic_slice_in_dim(own, lax.rem(lax.axis_index("seq"), 2) * half, half, 0)
+
+
+def over_x(value):
+    return exchange(value, "wsh", 2)
+
+
+def over_y(value):
+    return exchange(value, "seq", 1)
+
+
+def over_core(value):
+    return exchange(value, "wsh", 1)
 
 
 def gather_small(own):
     j = lax.axis_index("wsh")
-    pair = jnp.stack([own, exchange(own, "wsh", 1)])
-    four = jnp.concatenate([pair, exchange(pair, "wsh", 2)])
+    four = jnp.stack([own] + [exchange(own, "wsh", d) for d in range(1, 4)])
     return jnp.stack([lax.dynamic_index_in_dim(four, j ^ k, 0, False) for k in range(4)])
 
 
@@ -598,45 +701,62 @@
     return lax.dynamic_index_in_dim(value, bit, dim, False)
 
 
-def halve(value, dim, axis, step):
+def send_half(value, dim, mark):
+    axis, step = mark
     bit = lax.rem(lax.axis_index(axis) // step, 2)
-    sent = exchange(pick(value, dim, 1 - bit).astype(BF16), axis, step)
-    return pick(value, dim, bit) + sent.astype(F32)
-
-
-def reduce_grad(grad, order):
+    return exchange(pick(value, dim, 1 - bit).astype(BF16), axis, step), pick(value, dim, bit)
+
+
+def add_half(sent, kept):
+    return kept + sent.astype(F32)
+
+
+def seq_steps():
+    return [2**k for k in range(lax.axis_size("seq").bit_length() - 1)]
+
+
+def send_core(grad):
     rows, cols = grad.shape
-    n_seq, n_wsh = lax.axis_size("seq"), lax.axis_size("wsh")
-    steps = [2**k for k in reversed(range(n_seq.bit_length() - 1))]
-    labels = ["x", "c"] + [("seq", s) for s in steps]
-    value = grad.reshape((2, 2) + (2,) * len(steps) + (rows // n_wsh // n_seq, cols))
-    marks = [("wsh", 2), ("wsh", 1)] + [("seq", s) for s in steps]
-    plan = [("wsh", 1)] + (
-        [("wsh", 2), ("seq", 1), ("seq", 2)] * 2
-    )[order : order + 3]
-    plan += [("seq", s) for s in reversed(steps) if ("seq", s) not in plan]
-    for mark in plan:
-        value = halve(value, marks.index(mark), *mark)
-        marks.remove(mark)
-    return value.astype(BF16)
-
-
-def spread_grad(mine):
-    i = lax.axis_index("seq")
-    n = lax.axis_size("seq")
-    steps = []
-    step = n // 2
-    while step:
-        steps.append(step)
-        step //= 2
-    block = mine[None]
-    for step in reversed(steps):
-        bit = lax.rem(i // step, 2)
-        other = exchange(block, "seq", step)
-        first = jnp.where(bit == 0, block, other)
-        second = jnp.where(bit == 0, other, block)
-        block = jnp.concatenate([first, second], axis=0)
-    return block.reshape(-1, mine.shape[-1]).astype(F32)
+    bits = (2,) * len(seq_steps())
+    rest = rows // lax.axis_size("wsh") // lax.axis_size("seq")
+    return send_half(grad.reshape((2, 2) + bits + (rest, cols)), 1, ("wsh", 1))
+
+
+def merge(parts, cols):
+    pieces = []
+    for part in parts:
+        for c in range(0, part.shape[-1], cols):
+            pieces.append(part[..., c : c + cols])
+    return jnp.concatenate(pieces, axis=-2)
+
+
+class Sum:
+    def __init__(self, value):
+        self.value = value
+        self.marks = [("wsh", 2)] + [("seq", s) for s in reversed(seq_steps())]
+
+    def send(self, mark):
+        dim = self.marks.index(mark)
+        self.marks.pop(dim)
+        sent, self.kept = send_half(self.value, dim, mark)
+        return sent
+
+    def add(self, sent):
+        self.value = add_half(sent, self.kept)
+
+
+def widen(block, other, step):
+    bit = lax.rem(lax.axis_index("seq") // step, 2)
+    first = jnp.where(bit == 0, block, other)
+    second = jnp.where(bit == 0, other, block)
+    return jnp.concatenate([first, second], axis=0)
+
+
+def in_order(block):
+    bits = block.shape[0].bit_length() - 1
+    split = block.reshape((2,) * bits + block.shape[1:])
+    turned = split.transpose(tuple(reversed(range(bits))) + (bits, bits + 1))
+    return turned.reshape(block.shape)
 
 
 def sum_small(value):
@@ -667,7 +787,6 @@
     V = value_weight.shape[1]
     FF = ffn_in.shape[1]
 
-    wm, wv, wo, wi, wf = (weight_pieces(w) for w in (mix_weight, value_weight, out_weight, ffn_in, ffn_out))
     chan = gather_small(
         jnp.concatenate(
             [ema_alpha, ema_delta, ema_beta, ema_eta, ema_omega[:, None], norm_gain, norm_bias, ffn_out_bias[:, None]],
@@ -699,23 +818,116 @@
     position = i * L + jnp.arange(L, dtype=jnp.int32)
     live = (position[None, :] < lengths.reshape(G)[:, None]).astype(F32).reshape(T, 1)
 
+    y_step, z_steps = ("seq", 1), [("seq", s) for s in seq_steps()[1:]]
+    x_step = ("wsh", 2)
+    third = D // LANES // 3
+    half = D // LANES // 2
+
+    keep, *owns = join(keep, mix_weight, value_weight, out_weight, ffn_in, ffn_out)
+    o_mix, o_value, o_out, o_in, o_fout = owns
+    x_mix, x_value, x_out = over_x(own_half(o_mix)), over_x(own_half(o_value)), over_x(own_half(o_out))
+    c_mix, c_value, c_out = over_core(o_mix), over_core(o_value), over_core(o_out)
     ends, slice_end = ema_ends(x3, keep)
-    xp, pre, finals = ema_forward(x3, keep, weight, omega, ends, carry_in(slice_end, decay, 1))
+    ends, slice_end, x_mix, c_mix = join(ends, slice_end, x_mix, c_mix)
+    y_mix = over_y(x_mix)
+    state_in = carry_in(slice_end, decay, 1)
+    state_in, x_value, x_out, c_value, c_out = join(state_in, x_value, x_out, c_value, c_out)
+    y_value, y_out = over_y(x_value), over_y(x_out)
+    xc_mix = over_core(x_mix)
+    x_in, x_fout = over_x(own_half(o_in)), over_x(own_half(o_fout))
+    so_far = ema_forward((0, half), (), x3, keep, weight, omega, ends, state_in)
+    *so_far, y_mix, xc_mix = join(*so_far, y_mix, xc_mix)
+    yc_mix, xc_value, xc_out = over_core(y_mix), over_core(x_value), over_core(x_out)
+    c_in, c_fout = over_core(o_in), over_core(o_fout)
+    xp, pre, finals = ema_forward((half, half), tuple(so_far), x3, keep, weight, omega, ends, state_in)
+    xp, x_in, x_fout, c_in, c_fout, y_value, y_out, yc_mix, xc_value, xc_out = join(
+        xp, x_in, x_fout, c_in, c_fout, y_value, y_out, yc_mix, xc_value, xc_out
+    )
+    yc_value, yc_out = over_core(y_value), over_core(y_out)
+    y_in, y_fout, xc_in, xc_fout = over_y(x_in), over_y(x_fout), over_core(x_in), over_core(x_fout)
+    mix_pieces = (
+        (o_mix, c_mix, x_mix, y_mix, xc_mix, yc_mix) + (o_value, c_value, x_value, y_value, xc_value, yc_value)
+        + (o_out, c_out, x_out, y_out, xc_out, yc_out)
+    )
     xp = xp.reshape(T, D)
-    u, h, r, v, z, p, mixed = mix_forward(R, x, xp, bm, bv, qk, rel_matrix, wm + wv + wo)
-    output, h1, act, dg, df, dm, du, dt, sum_d, sum_f = ffn_both(
-        R, x, u, h, cotangent.reshape(T, D), live, norms, bf, bo, wi + wf
+    forward = mix_forward(R, x, xp, bm, bv, qk, rel_matrix, mix_pieces)
+    (u, h, r, v, z, p, mixed), y_in, y_fout, xc_in, xc_fout = join(forward, y_in, y_fout, xc_in, xc_fout)
+    ffn_pieces = (o_in, c_in, x_in, y_in, xc_in, over_core(y_in)) + (
+        o_fout, c_fout, x_fout, y_fout, xc_fout, over_core(y_fout)
     )
-    g_ffn_out = reduce_grad(dot_rows(act, dg), 0)
-    g_ffn_in = reduce_grad(dot_rows(h1, df), 1)
-    g_out = reduce_grad(dot_rows(mixed, dm), 2)
-    db, dv, dxp, dtok, sum_m, sum_v, sum_q, sum_s = mix_backward(R, dm, du, dt, r, v, z, p, qk, wm + wv + wo)
-    g_mix = reduce_grad(dot_rows(xp, db), 0)
-    g_value = reduce_grad(dot_rows(x, dv), 1)
+    output, h1, act, dg, df, dum, dt, sum_d, sum_f = ffn_both(
+        R, x, u, h, cotangent.reshape(T, D), live, norms, bf, bo, ffn_pieces
+    )
+
+    (sent_1, kept_1), (sent_2, kept_2) = send_core(dot_rows(act, dg)), send_core(dot_rows(h1, df))
+    d_out, d_edge = dot_rows(mixed, dum[:, D:]), dot_rows(xp, dum)
+    d_out, d_edge, sent_1, sent_2 = join(d_out, d_edge, sent_1, sent_2)
+    sum_a = Sum(merge([add_half(sent_1, kept_1), add_half(sent_2, kept_2)], D))
+    over_a = sum_a.send(x_step)
+    (sent_1, kept_1), (sent_2, kept_2) = send_core(d_out), send_core(d_edge)
+    sum_b = Sum(merge([add_half(sent_1, kept_1), add_half(sent_2, kept_2)], D))
+    over_b = sum_b.send(y_step)
+    back = mix_backward(R, dum, dt, r, v, z, p, qk, mix_pieces)
+    (db, dv, dxp, dtok, sum_m, sum_v, sum_q, sum_s), over_a, over_b = join(back, over_a, over_b)
+    sum_a.add(over_a)
+    sum_b.add(over_b)
+    over_a, over_b = sum_a.send(y_step), sum_b.send(x_step)
+    d_side, over_a, over_b = join(dot_rows(xp, db), over_a, over_b)
+    sum_a.add(over_a)
+    sum_b.add(over_b)
+    rows_a = sum_a.value.shape[-2]
+    sum_a.value = jnp.concatenate([sum_a.value, sum_b.value], axis=-2)
+    over_a = sum_a.send(z_steps[0])
+    sent_1, kept_1 = send_core(d_side)
+    d_value, over_a, sent_1 = join(dot_rows(x, dv), over_a, sent_1)
+    sum_c = Sum(add_half(sent_1, kept_1))
+    sum_a.add(over_a)
+    over_a = sum_a.send(z_steps[1])
+    sent_2, kept_2 = send_core(d_value)
     dpe, back_ends, slice_start = ema_back_ends(dxp.reshape(G, L, D), pre, keep)
-    dx, s1, s3, g_omega = ema_backward(
-        dpe, x3, keep, 1.0 / keep, weight, omega, finals, back_ends, carry_in(slice_start, decay, -1)
-    )
+    dpe, back_ends, slice_start, over_a, sent_2 = join(dpe, back_ends, slice_start, over_a, sent_2)
+    sum_a.add(over_a)
+    sum_d_ = Sum(add_half(sent_2, kept_2))
+    back_in = carry_in(slice_start, decay, -1)
+    over_c, over_d = sum_c.send(x_step), sum_d_.send(y_step)
+    for mark in z_steps[2:]:
+        sum_a.add(sum_a.send(mark))
+    block = sum_a.value.astype(BF16)[None]
+    consts = (dpe, x3, keep, 1.0 / keep, weight, omega, finals, back_ends, back_in)
+    order = list(reversed(seq_steps()))
+    more = exchange(block, "seq", order[0])
+    so_far = ema_backward((0, third), (), *consts)
+    *so_far, over_c, over_d, more = join(*so_far, over_c, over_d, more)
+    sum_c.add(over_c)
+    sum_d_.add(over_d)
+    over_c, over_d = sum_c.send(y_step), sum_d_.send(x_step)
+    block = widen(block, more, order[0])
+    more = exchange(block, "seq", order[1])
+    so_far = ema_backward((third, third), tuple(so_far), *consts)
+    *so_far, over_c, over_d, more = join(*so_far, over_c, over_d, more)
+    sum_c.add(over_c)
+    sum_d_.add(over_d)
+    cols_c = sum_c.value.shape[-1]
+    sum_c.value = jnp.concatenate([sum_c.value, sum_d_.value], axis=-1)
+    over_c = sum_c.send(z_steps[0])
+    block = widen(block, more, order[1])
+    more = exchange(block, "seq", order[2])
+    so_far = ema_backward((2 * third, third), tuple(so_far), *consts)
+    *so_far, over_c = join(*so_far, over_c)
+    sum_c.add(over_c)
+    for mark in z_steps[1:]:
+        sum_c.add(sum_c.send(mark))
+    block = widen(block, more, order[2])
+    for step in order[3:]:
+        block = widen(block, exchange(block, "seq", step), step)
+    small = sum_c.value.astype(BF16)[None]
+    for step in order:
+        small = widen(small, exchange(small, "seq", step), step)
+    block, small = in_order(block), in_order(small)
+    g_a, g_b = block[:, :rows_a].reshape(-1, D).astype(F32), block[:, rows_a:].reshape(-1, D).astype(F32)
+    small = small.reshape(-1, small.shape[-1]).astype(F32)
+    g_c, g_d = small[:, :cols_c], small[:, cols_c:]
+    dx, s1, s3, g_omega = so_far
     input_grad = (dtok + dx.reshape(T, D).astype(F32)).astype(BF16).reshape(tokens.shape)
 
     g_eta = rate * beta * s1
@@ -742,13 +954,26 @@
         g_ffn_out_bias,
     ) = smalls
     late = late.T
+    tall_rows, wide_rows = ffn_out.shape[0], ffn_in.shape[0]
+    n_seq = lax.axis_size("seq")
+    first_rows = tall_rows // n_seq
+
+    def unmerge(merged):
+        parts = merged.reshape(n_seq, -1, D)
+        top = parts[:, :first_rows].reshape(tall_rows, D)
+        sides = parts[:, first_rows:].reshape(n_seq, 2, wide_rows // n_seq, D)
+        return top, jnp.concatenate([sides[:, k].reshape(wide_rows, D) for k in range(2)], axis=1)
+
+    g_ffn_out, g_ffn_in = unmerge(g_a)
+    g_out, g_edges = unmerge(g_b)
+    g_mix = jnp.concatenate([g_edges[:, :D], g_c, g_edges[:, D:]], axis=1)
     return (
         output.reshape(tokens.shape), input_grad,
         late[:, 0:H], late[:, H : 2 * H], late[:, 2 * H : 3 * H], late[:, 3 * H : 4 * H], late[:, 4 * H],
-        spread_grad(g_mix), g_mix_bias, spread_grad(g_value), g_value_bias,
-        jnp.stack([g_gain_q, g_gain_k], axis=1), g_shift, g_rel, spread_grad(g_out),
+        g_mix, g_mix_bias, g_d, g_value_bias,
+        jnp.stack([g_gain_q, g_gain_k], axis=1), g_shift, g_rel, g_out,
         jnp.stack([gain_1, gain_2], axis=1), jnp.stack([shift_1, shift_2], axis=1),
-        spread_grad(g_ffn_in), g_ffn_in_bias, spread_grad(g_ffn_out), g_ffn_out_bias,
+        g_ffn_in, g_ffn_in_bias, g_ffn_out, g_ffn_out_bias,
     )
 
 

time: 703 us -> 539 us (0.77)
  waiting for transfers between devices: 197 us -> 82.1 us
  Pallas kernels: 247 us -> 222 us
  starting transfers between devices: 96.8 us -> 79.6 us
  matrix products: 60.7 us -> 45.5 us
  other arithmetic: 27.1 us -> 38.4 us
    ppermute x81 -> x67, waiting for transfers between devices: 187 us -> 61.2 us  [exchange(): lax.ppermute(value, axis, [(k, k ^ step) for k in range(lax.axis_size(axi...]
    pallas_call x1, Pallas kernels: 70.4 us -> 42.7 us  [ffn_both(): pl.pallas_call(functools.partial(ffn_kernel, R, (D, FF)), grid=(T // R,),...]
    ppermute x81 -> x67, starting transfers between devices: 72.3 us -> 56.8 us  [exchange(): lax.ppermute(value, axis, [(k, k ^ step) for k in range(lax.axis_size(axi...]
    dot_general x5 -> x6, matrix products: 60.7 us -> 45.5 us  [dot_rows(): jnp.einsum('ri,rj->ij', left_op, right_op, preferred_element_type=jnp.flo...]
    add x20 -> x15, other arithmetic: 5.72 us -> 17.1 us  [add_half(): return kept + sent.astype(F32)]
    ppermute x10, waiting for transfers between devices: 9.83 us -> 20.8 us  [shift(): lax.ppermute(value, axis, [(k, k + step) for k in range(n) if 0 <= k + st...]
    unnamed x100 -> x122, local copies, waits for them, and re-layouts: 5.29 us -> 14 us
    pallas_call x2 -> x5, Pallas kernels: 69.1 us -> 74.8 us  [the longest x3 53.4 us: ema_backward(): pl.pallas_call(functools.partial(bwd_kernel, H, L // CH), grid=(count, G)...]
  transfers between devices with their start and end apart: 91 -> 77, of which waited for: 40 -> 20; matrix products, arithmetic and copies ran while one was open for 20% -> 18% of each run, Pallas kernels for 16% -> 34%
where the time goes in v2:
time: 539 us; the launch traced here: 529 us
  Pallas kernels  222 us (41%)
  waiting for transfers between devices  82.1 us (15%)
  starting transfers between devices  79.6 us (15%)
  local copies, waits for them, and re-layouts  59.2 us (11%)
  matrix products  45.5 us (8%)
  other arithmetic  38.4 us (7%)
    ppermute x67, waiting for transfers between devices, exchange(): lax.ppermute(value, axis, [(k, k ^ step) for k in range(lax.axis_size(axi...  61.2 us
    ppermute x67, starting transfers between devices, exchange(): lax.ppermute(value, axis, [(k, k ^ step) for k in range(lax.axis_size(axi...  56.8 us
    pallas_call x3, Pallas kernels, ema_backward(): pl.pallas_call(functools.partial(bwd_kernel, H, L // CH), grid=(count, G)...  53.4 us
    dot_general x6, matrix products, dot_rows(): jnp.einsum('ri,rj->ij', left_op, right_op, preferred_element_type=jnp.flo...  45.5 us
    pallas_call x1, Pallas kernels, mix_backward(): pl.pallas_call(functools.partial(mix_bwd_kernel, R, (D, Z, V)), grid=(T /...  44.4 us
    pallas_call x1, Pallas kernels, ffn_both(): pl.pallas_call(functools.partial(ffn_kernel, R, (D, FF)), grid=(T // R,),...  42.7 us
    pallas_call x1, Pallas kernels, mix_forward(): pl.pallas_call(functools.partial(mix_fwd_kernel, R, (D, Z, V)), grid=(T /...  33.4 us
    ppermute x10, starting transfers between devices, shift(): lax.ppermute(value, axis, [(k, k + step) for k in range(n) if 0 <= k + st...  22.8 us
  transfers between devices with their start and end apart: 77, of which 20 were waited for; matrix products, arithmetic and copies ran while one was open for 18% of the time, Pallas kernels for 34%

profile of v2, /device:TPU:0, one launch (start us, length us, event | category | flops | bytes accessed | tf_op | source)
XLA Modules:
  0.0 529.1 jit_solution(17956279698660073629)
XLA Ops:
  2.1 3.5 concatenate.66
  6.1 2.6 collective-permute-start.1
  9.4 3.5 concatenate.67
  13.3 1.4 collective-permute-start.27
  17.5 2.8 collective-permute-done.2
  23.5 1.8 collective-permute-start.10
  25.3 11.4 %ema_ends.1 = (f32[2,128,768]{2,1,0:T(8,128)}, f32[2,16,768]{2,1,0:T(8,128)}) custom-call(bf16[2,1024,768]{2,1,0:T(8,128)(2,1)} %bitcast.207, f32[16,768]{1,0:T(8,128)} %get-tuple-element.153.q_ref), custom_call_target="tpu_custom_call" | custom-call | bytes 39600000 | tf_op jit(solution)/shard_map/ema_ends/pallas_call | solution.py:172
  39.1 3.4 collective-permute-start.5
  42.5 3.5 collective-permute-start.6
  46.0 4.4 collective-permute-start.7
  52.0 2.0 collective-permute-start.8
  56.5 2.0 collective-permute-done.11.refs_14_
  58.6 3.1 collective-permute-start.9
  63.0 1.4 collective-permute-done.9
  65.0 1.5 collective-permute-start.16
  66.6 10.7 %ema_forward.2 = (bf16[2,1024,768]{2,1,0:T(8,128)(2,1)}, f32[2,1024,768]{2,1,0:T(8,128)}, f32[2,128,768]{2,1,0:T(8,128)}) custom-call(bf16[2,1024,768]{2,1,0:T(8,128)(2,1)} %bitcast.208, f32[16,768]{1,0:T(8,128)} %get-tuple-element.153.q_ref, f32[16,768]{1,0:T(8,128)} %get-tuple-element.394.w_ref, f32[1,768]{1,0:T(1,128)} %get-tuple-element.393.om_ref, ...), custom_call_target="tpu_custom_call" | custom-call | bytes 32400000 | tf_op jit(solution)/shard_map/ema_forward/pallas_call | solution.py:189
  79.6 7.0 %collective-permute-done.17.refs_8_ = bf16[192,768]{1,0:T(8,128)(2,1)} collective-permute-done((bf16[192,768]{1,0:T(8,128)(2,1)S(1)}, bf16[192,768]{1,0:T(8,128)(2,1)}, u32[]{:S(2)}, u32[]{:S(2)}) %collective-permute-start.17) | collective-permute-done | bytes 294944 | tf_op jit(solution)/shard_map/ppermute | solution.py:646
  87.8 10.7 %ema_forward.3 = (bf16[2,1024,768]{2,1,0:T(8,128)(2,1)}, f32[2,1024,768]{2,1,0:T(8,128)}, f32[2,128,768]{2,1,0:T(8,128)}) custom-call(bf16[2,1024,768]{2,1,0:T(8,128)(2,1)} %bitcast.209, f32[16,768]{1,0:T(8,128)} %get-tuple-element.153.q_ref, f32[16,768]{1,0:T(8,128)} %get-tuple-element.394.w_ref, ...), custom_call_target="tpu_custom_call", output_to_operand_aliasing={{0}: (6, {}), {1}: (7, {}), {2}: (8, {})} | custom-call | bytes 32400000 | tf_op jit(solution)/shard_map/ema_forward/pallas_call | solution.py:189
  105.5 33.4 %mix_forward.1 = (f32[2048,768]{1,0:T(8,128)}, f32[2048,768]{1,0:T(8,128)}, f32[2048,1536]{1,0:T(8,128)}, f32[2048,1536]{1,0:T(8,128)}, f32[2048,128]{1,0:T(8,12...) custom-call(bf16[2048,768]{1,0:T(8,128)(2,1)} %bitcast.210, bf16[2048,768]{1,0:T(8,128)(2,1)} %bitcast.236, ...), custom_call_target="tpu_custom_call" | custom-call | flops 19730006016 | bytes 118800000 | tf_op jit(solution)/shard_map/mix_forward/pallas_call | solution.py:571
  142.3 42.7 %ffn_both.1 = (bf16[2048,768]{1,0:T(8,128)(2,1)}, bf16[2048,768]{1,0:T(8,128)(2,1)}, bf16[2048,1536]{1,0:T(8,128)(2,1)}, bf16[2048,768]{1,0:T(8,128)(2,1)}, bf16...) custom-call(bf16[2048,768]{1,0:T(8,128)(2,1)} %bitcast.211, ...), custom_call_target="tpu_custom_call" | custom-call | flops 19327352832 | bytes 180000000 | tf_op jit(solution)/shard_map/ffn_both/pallas_call | solution.py:593
  185.0 8.9 %fusion.70 = f32[768,1536]{1,0:T(8,128)S(1)} fusion(bf16[2048,768]{1,0:T(8,128)(2,1)} %get-tuple-element.220, bf16[2048,1536]{1,0:T(8,128)(2,1)} %get-tuple-element.221), kind=kOutput, calls=%fused_computation.213 | convolution fusion | flops 4831838208 | bytes 14155776 | tf_op jit(solution)/shard_map/ri,rj->ij/dot_general | solution.py:23
  194.4 1.9 copy-done.16
  196.3 5.4 %fusion.68 = f32[1536,768]{1,0:T(8,128)S(1)} fusion(bf16[2048,1536]{1,0:T(8,128)(2,1)S(1)} %copy-done.46, bf16[2048,768]{1,0:T(8,128)(2,1)S(1)} %copy-done.47), kind=kOutput, calls=%fused_computation.211 | convolution fusion | flops 4831838208 | bytes 14155776 | tf_op jit(solution)/shard_map/ri,rj->ij/dot_general | solution.py:23
  203.3 7.0 %fusion.69 = f32[768,1536]{1,0:T(8,128)} fusion(bf16[2048,768]{1,0:T(8,128)(2,1)S(1)} %bitcast.237, bf16[2048,1536]{1,0:T(8,128)(2,1)S(1)} %bitcast.282), kind=kOutput, calls=%fused_computation.212 | convolution fusion | flops 4831838208 | bytes 14155776 | tf_op jit(solution)/shard_map/ri,rj->ij/dot_general | solution.py:23
  210.8 8.5 %fusion.1 = f32[1536,768]{1,0:T(8,128)S(1)} fusion(bf16[2048,1536]{1,0:T(8,128)(2,1)} %get-tuple-element.219, bf16[2048,1536]{1,0:T(8,128)(2,1)} %get-tuple-element.203.dum_ref), kind=kOutput, calls=%fused_computation.5 | convolution fusion | flops 4831838208 | bytes 14155776 | tf_op jit(solution)/shard_map/ri,rj->ij/dot_general | solution.py:23
  220.3 1.4 copy-done.18
  221.7 1.5 bitcast_add_fusion.7
  223.2 2.3 bitcast_add_fusion.6
  230.1 2.1 copy-done.3
  234.5 44.4 %mix_backward.1 = (bf16[2048,1664]{1,0:T(8,128)(2,1)}, bf16[2048,1536]{1,0:T(8,128)(2,1)}, bf16[2048,768]{1,0:T(8,128)(2,1)}, f32[2048,768]{1,0:T(8,128)}, f32[1...) custom-call(bf16[2048,1536]{1,0:T(8,128)(2,1)} %get-tuple-element.203.dum_ref, ...), custom_call_target="tpu_custom_call" | custom-call | flops 19730006016 | bytes 144000000 | tf_op jit(solution)/shard_map/mix_backward/pallas_call | solution.py:621
  279.0 2.3 bitcast_add_fusion.2
  281.4 1.4 copy-done.6
  288.1 2.5 bitcast_add_fusion.3
  290.7 7.6 %collective-permute-done.72 = f32[2688]{0:T(1024)S(1)} collective-permute-done((f32[2688]{0:T(1024)S(1)}, f32[2688]{0:T(1024)S(1)}, u32[]{:S(2)}, u32[]{:S(2)}) %collective-permute-start.72) | collective-permute-done | bytes 10784 | tf_op jit(solution)/shard_map/ppermute | solution.py:646
  300.5 1.7 collective-permute-done.74
  302.2 3.1 collective-permute-start.75
  305.3 8.9 %fusion.71 = f32[768,1664]{1,0:T(8,128)S(1)} fusion(bf16[2048,768]{1,0:T(8,128)(2,1)S(1)} %bitcast.238, bf16[2048,1664]{1,0:T(8,128)(2,1)} %get-tuple-element.233), kind=kOutput, calls=%fused_computation.214 | convolution fusion | flops 5234491392 | bytes 15073280 | tf_op jit(solution)/shard_map/ri,rj->ij/dot_general | solution.py:23
  314.2 3.5 collective-permute-start.76
  320.4 6.9 %convolution_bitcast_fusion = f32[768,1536]{0,1:T(8,128)} fusion(bf16[2048,1536]{1,0:T(8,128)(2,1)S(1)} %bitcast.280, bf16[2048,768]{1,0:T(8,128)(2,1)S(1)} %bitcast.215), kind=kOutput, calls=%fused_computation.4 | convolution fusion | flops 4831838208 | bytes 14155776 | tf_op jit(solution)/shard_map/ri,rj->ij/dot_general | solution.py:23
  327.2 14.8 %ema_back_ends.1 = (f32[2,1024,768]{2,1,0:T(8,128)}, f32[2,128,768]{2,1,0:T(8,128)}, f32[2,16,768]{2,1,0:T(8,128)}) custom-call(bf16[2,1024,768]{2,1,0:T(8,128)(2,1)} %bitcast.234, f32[2,1024,768]{2,1,0:T(8,128)} %get-tuple-element.228.p_ref, f32[16,768]{1,0:T(8,128)} %get-tuple-element.153.q_ref), custom_call_target="tpu_custom_call" | custom-call | bytes 54000000 | tf_op jit(solution)/shard_map/ema_back_ends/pallas_call | solution.py:212
  342.7 6.4 %copy.93 = f32[768,1536]{1,0:T(8,128)} copy(f32[768,1536]{0,1:T(8,128)} %convolution_bitcast_fusion) | data formatting | bytes 9437184 | tf_op jit(solution)/shard_map/optimization_barrier | solution.py:655
  349.1 1.8 fusion.7
  351.6 3.4 collective-permute-start.46
  355.1 2.3 bitcast_add_fusion
  359.4 9.1 %collective-permute-done.46 = bf16[192,768]{1,0:T(8,128)(2,1)S(1)} collective-permute-done((bf16[192,768]{1,0:T(8,128)(2,1)S(1)}, bf16[192,768]{1,0:T(8,128)(2,1)S(1)}, u32[]{:S(2)}, u32[]{:S(2)}) %collective-permute-start.46) | collective-permute-done | bytes 294944 | tf_op jit(solution)/shard_map/ppermute | solution.py:646
  374.2 1.4 copy-done.4
  376.5 5.7 %collective-permute-start.55 = (bf16[1,192,768]{2,1,0:T(8,128)(2,1)S(1)}, bf16[1,192,768]{2,1,0:T(8,128)(2,1)}, u32[]{:S(2)}, u32[]{:S(2)}) collective-permute-start(bf16[1,192,768]{2,1,0:T(8,128)(2,1)S(1)} %fusion.32), channel_id=1, source_target_pairs={{0,16},{4,20},{8,24},{12,28},{16,0},{20,4},{24,8},{28,12},{1,17},{... | collective-permute-start | bytes 884744 | tf_op jit(solution)/shard_map/ppermute | solution.py:646
  382.2 1.5 collective-permute-start.54
  383.7 12.8 %collective-permute-done.51 = f32[2,16,768]{2,1,0:T(8,128)S(1)} collective-permute-done((f32[2,16,768]{2,1,0:T(8,128)S(1)}, f32[2,16,768]{2,1,0:T(8,128)S(1)}, u32[]{:S(2)}, u32[]{:S(2)}) %collective-permute-start.51) | collective-permute-done | bytes 98336 | tf_op jit(solution)/shard_map/ppermute | solution.py:651
  398.5 5.6 %collective-permute-done.52 = f32[2,16,768]{2,1,0:T(8,128)S(1)} collective-permute-done((f32[2,16,768]{2,1,0:T(8,128)S(1)}, f32[2,16,768]{2,1,0:T(8,128)S(1)}, u32[]{:S(2)}, u32[]{:S(2)}) %collective-permute-start.52) | collective-permute-done | bytes 98336 | tf_op jit(solution)/shard_map/ppermute | solution.py:651
  404.7 17.8 %ema_backward.3 = (bf16[2,1024,768]{2,1,0:T(8,128)(2,1)}, f32[16,768]{1,0:T(8,128)}, f32[16,768]{1,0:T(8,128)}, f32[1,768]{1,0:T(1,128)}) custom-call(f32[2,1024,768]{2,1,0:T(8,128)} %get-tuple-element.241.d_ref, bf16[2,1024,768]{2,1,0:T(8,128)(2,1)} %bitcast.212, f32[16,768]{1,0:T(8,128)} %get-tuple-element.153.q_ref, ...), custom_call_target="tpu_custom_call" | custom-call | bytes 57600000 | tf_op jit(solution)/shard_map/ema_backward/pallas_call | solution.py:232
  431.6 17.9 %ema_backward.4 = (bf16[2,1024,768]{2,1,0:T(8,128)(2,1)}, f32[16,768]{1,0:T(8,128)}, f32[16,768]{1,0:T(8,128)}, f32[1,768]{1,0:T(1,128)}) custom-call(f32[2,1024,768]{2,1,0:T(8,128)} %get-tuple-element.241.d_ref, bf16[2,1024,768]{2,1,0:T(8,128)(2,1)} %bitcast.213, ...), custom_call_target="tpu_custom_call", output_to_operand_aliasing={{0}: (9, {}), {1}: (10, {}), {2}: (11, {}), {3}: (12, {})} | custom-call | bytes 57600000 | tf_op jit(solution)/shard_map/ema_backward/pallas_call | solution.py:232
  451.6 2.0 collective-permute-start.59
  455.3 17.8 %ema_backward.5 = (bf16[2,1024,768]{2,1,0:T(8,128)(2,1)}, f32[16,768]{1,0:T(8,128)}, f32[16,768]{1,0:T(8,128)}, f32[1,768]{1,0:T(1,128)}) custom-call(f32[2,1024,768]{2,1,0:T(8,128)} %get-tuple-element.241.d_ref, bf16[2,1024,768]{2,1,0:T(8,128)(2,1)} %bitcast.214, ...), custom_call_target="tpu_custom_call", output_to_operand_aliasing={{0}: (9, {}), {1}: (10, {}), {2}: (11, {}), {3}: (12, {})} | custom-call | bytes 57600000 | tf_op jit(solution)/shard_map/ema_backward/pallas_call | solution.py:232
  478.2 3.2 collective-permute-done.61
  482.1 2.1 collective-permute-start.63
  484.3 2.5 collective-permute-done.63
  488.2 5.2 fusion
  493.4 3.0 collective-permute-start.65
  496.3 3.4 collective-permute-done.68
  502.5 6.6 %collective-permute-done.69 = bf16[2,24,3200]{2,1,0:T(8,128)(2,1)S(1)} collective-permute-done((bf16[2,24,3200]{2,1,0:T(8,128)(2,1)S(1)}, bf16[2,24,3200]{2,1,0:T(8,128)(2,1)S(1)}, u32[]{:S(2)}, u32[]{:S(2)}) %collective-permute-start.69) | collective-permute-done | bytes 307232 | tf_op jit(solution)/shard_map/ppermute | solution.py:646
  509.9 3.3 collective-permute-done.66
  517.9 7.5 %collective-permute-done.70 = bf16[4,24,3200]{2,1,0:T(8,128)(2,1)S(1)} collective-permute-done((bf16[4,24,3200]{2,1,0:T(8,128)(2,1)S(1)}, bf16[4,24,3200]{2,1,0:T(8,128)(2,1)S(1)}, u32[]{:S(2)}, u32[]{:S(2)}) %collective-permute-start.70) | collective-permute-done | bytes 614432 | tf_op jit(solution)/shard_map/ppermute | solution.py:646
  527.1 1.6 pad_maximum_fusion.2
  (402 shorter events, 93.6 us)
Async XLA Ops:
  5.6 11.9 %collective-permute-start = (bf16[192,70]{0,1:T(8,128)(2,1)S(1)}, bf16[192,70]{0,1:T(8,128)(2,1)S(1)}, u32[]{:S(2)}, u32[]{:S(2)}) collective-permute-start(bf16[192,70]{0,1:T(8,128)(2,1)S(1)} %concatenate.66), channel_id=1, source_target_pairs={{0,1},{1,0},{2,3},{3,2},{4,5},{5,4},{6,7},{7,6},{8,9},{9,8},{10,11... | collective-permute-start | bytes 80648 | tf_op jit(solution)/shard_map/ppermute | solution.py:646
  6.1 11.4 %collective-permute-start.1 = (bf16[192,70]{0,1:T(8,128)(2,1)S(1)}, bf16[192,70]{0,1:T(8,128)(2,1)S(1)}, u32[]{:S(2)}, u32[]{:S(2)}) collective-permute-start(bf16[192,70]{0,1:T(8,128)(2,1)S(1)} %concatenate.66), channel_id=1, source_target_pairs={{0,2},{1,3},{2,0},{3,1},{4,6},{5,7},{6,4},{7,5},{8,10},{9,11},{10,... | collective-permute-start | bytes 80648 | tf_op jit(solution)/shard_map/ppermute | solution.py:646
  21.5 17.6 %collective-permute-start.4 = (bf16[192,3200]{1,0:T(8,128)(2,1)S(1)}, bf16[192,3200]{1,0:T(8,128)(2,1)}, u32[]{:S(2)}, u32[]{:S(2)}) collective-permute-start(bf16[192,3200]{1,0:T(8,128)(2,1)S(1)} %copy-done.27), channel_id=1, source_target_pairs={{0,1},{1,0},{2,3},{3,2},{4,5},{5,4},{6,7},{7,6},{8,9},{9,8},{10,11... | collective-permute-start | bytes 3686408 | tf_op jit(solution)/shard_map/ppermute | solution.py:646
  22.2 16.9 %collective-permute-start.3 = (bf16[96,3200]{1,0:T(8,128)(2,1)S(1)}, bf16[96,3200]{1,0:T(8,128)(2,1)}, u32[]{:S(2)}, u32[]{:S(2)}) collective-permute-start(bf16[96,3200]{1,0:T(8,128)(2,1)S(1)} %constant_dynamic-slice_fusion.20), channel_id=1, source_target_pairs={{0,2},{1,3},{2,0},{3,1},{4,6},{5,7},{6,4},{7,5},{8,10},{9,11},{10,... | collective-permute-start | bytes 1843208 | tf_op jit(solution)/shard_map/ppermute | solution.py:646
  22.5 40.2 %collective-permute-start.12 = (bf16[192,1536]{1,0:T(8,128)(2,1)}, bf16[192,1536]{1,0:T(8,128)(2,1)}, u32[]{:S(2)}, u32[]{:S(2)}) collective-permute-start(bf16[192,1536]{1,0:T(8,128)(2,1)} %refs_6_.2), channel_id=1, source_target_pairs={{0,1},{1,0},{2,3},{3,2},{4,5},{5,4},{6,7},{7,6},{8,9},{9,8},{10,11... | collective-permute-start | bytes 1769480 | tf_op jit(solution)/shard_map/ppermute | solution.py:646
  23.5 27.9 %collective-permute-start.10 = (bf16[96,1536]{1,0:T(8,128)(2,1)S(1)}, bf16[96,1536]{1,0:T(8,128)(2,1)}, u32[]{:S(2)}, u32[]{:S(2)}) collective-permute-start(bf16[96,1536]{1,0:T(8,128)(2,1)S(1)} %constant_dynamic-slice_fusion.19), channel_id=1, source_target_pairs={{0,2},{1,3},{2,0},{3,1},{4,6},{5,7},{6,4},{7,5},{8,10},{9,11},{10,... | collective-permute-start | bytes 884744 | tf_op jit(solution)/shard_map/ppermute | solution.py:646
  39.1 13.0 %collective-permute-start.5 = (f32[2,16,768]{2,1,0:T(8,128)}, f32[2,16,768]{2,1,0:T(8,128)S(1)}, u32[]{:S(2)}, u32[]{:S(2)}) collective-permute-start(f32[2,16,768]{2,1,0:T(8,128)} %get-tuple-element.158), channel_id=1, source_target_pairs={{0,4},{4,8},{8,12},{12,16},{16,20},{20,24},{24,28},{1,5},{5,9},{9,... | collective-permute-start | bytes 294920 | tf_op jit(solution)/shard_map/ppermute | solution.py:651
  42.5 11.5 %collective-permute-start.6 = (f32[2,16,768]{2,1,0:T(8,128)}, f32[2,16,768]{2,1,0:T(8,128)S(1)}, u32[]{:S(2)}, u32[]{:S(2)}) collective-permute-start(f32[2,16,768]{2,1,0:T(8,128)} %get-tuple-element.158), channel_id=1, source_target_pairs={{0,8},{4,12},{8,16},{12,20},{16,24},{20,28},{1,9},{5,13},{9,17},{1... | collective-permute-start | bytes 294920 | tf_op jit(solution)/shard_map/ppermute | solution.py:651
  46.0 8.9 %collective-permute-start.7 = (f32[2,16,768]{2,1,0:T(8,128)}, f32[2,16,768]{2,1,0:T(8,128)S(1)}, u32[]{:S(2)}, u32[]{:S(2)}) collective-permute-start(f32[2,16,768]{2,1,0:T(8,128)} %get-tuple-element.158), channel_id=1, source_target_pairs={{0,12},{4,16},{8,20},{12,24},{16,28},{1,13},{5,17},{9,21},{13,25},... | collective-permute-start | bytes 294920 | tf_op jit(solution)/shard_map/ppermute | solution.py:651
  51.4 7.1 %collective-permute-start.11 = (bf16[192,768]{1,0:T(8,128)(2,1)S(1)}, bf16[192,768]{1,0:T(8,128)(2,1)S(1)}, u32[]{:S(2)}, u32[]{:S(2)}) collective-permute-start(bf16[192,768]{1,0:T(8,128)(2,1)S(1)} %constant_dynamic-slice_fusion.18), channel_id=1, source_target_pairs={{0,2},{1,3},{2,0},{3,1},{4,6},{5,7},{6,4},{7,5},{8,10},{9,11},{10,... | collective-permute-start | bytes 884744 | tf_op jit(solution)/shard_map/ppermute | solution.py:646
  54.0 23.3 %collective-permute-start.14 = (bf16[96,3200]{1,0:T(8,128)(2,1)}, bf16[96,3200]{1,0:T(8,128)(2,1)S(1)}, u32[]{:S(2)}, u32[]{:S(2)}) collective-permute-start(bf16[96,3200]{1,0:T(8,128)(2,1)} %collective-permute-done.3.refs_2_), channel_id=1, source_target_pairs={{0,4},{4,0},{8,12},{12,8},{16,20},{20,16},{24,28},{28,24},{1,5},{5... | collective-permute-start | bytes 1843208 | tf_op jit(solution)/shard_map/ppermute | solution.py:646
  54.9 23.3 %collective-permute-start.15 = (bf16[96,3200]{1,0:T(8,128)(2,1)}, bf16[96,3200]{1,0:T(8,128)(2,1)S(1)}, u32[]{:S(2)}, u32[]{:S(2)}) collective-permute-start(bf16[96,3200]{1,0:T(8,128)(2,1)} %collective-permute-done.3.refs_2_), channel_id=1, source_target_pairs={{0,1},{1,0},{2,3},{3,2},{4,5},{5,4},{6,7},{7,6},{8,9},{9,8},{10,11... | collective-permute-start | bytes 1843208 | tf_op jit(solution)/shard_map/ppermute | solution.py:646
  56.5 8.5 %collective-permute-start.13 = (bf16[384,768]{1,0:T(8,128)(2,1)}, bf16[384,768]{1,0:T(8,128)(2,1)S(1)}, u32[]{:S(2)}, u32[]{:S(2)}) collective-permute-start(bf16[384,768]{1,0:T(8,128)(2,1)} %refs_12_.1), channel_id=1, source_target_pairs={{0,1},{1,0},{2,3},{3,2},{4,5},{5,4},{6,7},{7,6},{8,9},{9,8},{10,11... | collective-permute-start | bytes 1769480 | tf_op jit(solution)/shard_map/ppermute | solution.py:646
  58.6 5.8 %collective-permute-start.9 = (f32[2,16,768]{2,1,0:T(8,128)S(1)}, f32[2,16,768]{2,1,0:T(8,128)S(1)}, u32[]{:S(2)}, u32[]{:S(2)}) collective-permute-start(f32[2,16,768]{2,1,0:T(8,128)S(1)} %multiply_add_fusion.3), channel_id=1, source_target_pairs={{0,16},{4,20},{8,24},{12,28},{1,17},{5,21},{9,25},{13,29},{2,18},{... | collective-permute-start | bytes 294920 | tf_op jit(solution)/shard_map/ppermute | solution.py:651
  62.7 23.9 %collective-permute-start.18 = (bf16[192,1536]{1,0:T(8,128)(2,1)}, bf16[192,1536]{1,0:T(8,128)(2,1)}, u32[]{:S(2)}, u32[]{:S(2)}) collective-permute-start(bf16[192,1536]{1,0:T(8,128)(2,1)} %refs_0_.1), channel_id=1, source_target_pairs={{0,1},{1,0},{2,3},{3,2},{4,5},{5,4},{6,7},{7,6},{8,9},{9,8},{10,11... | collective-permute-start | bytes 1769480 | tf_op jit(solution)/shard_map/ppermute | solution.py:646
  64.4 23.2 %collective-permute-start.19 = (bf16[384,768]{1,0:T(8,128)(2,1)}, bf16[384,768]{1,0:T(8,128)(2,1)}, u32[]{:S(2)}, u32[]{:S(2)}) collective-permute-start(bf16[384,768]{1,0:T(8,128)(2,1)} %refs_6_.1), channel_id=1, source_target_pairs={{0,1},{1,0},{2,3},{3,2},{4,5},{5,4},{6,7},{7,6},{8,9},{9,8},{10,11... | collective-permute-start | bytes 1769480 | tf_op jit(solution)/shard_map/ppermute | solution.py:646
  65.0 13.6 %collective-permute-start.16 = (bf16[96,1536]{1,0:T(8,128)(2,1)S(1)}, bf16[96,1536]{1,0:T(8,128)(2,1)}, u32[]{:S(2)}, u32[]{:S(2)}) collective-permute-start(bf16[96,1536]{1,0:T(8,128)(2,1)S(1)} %constant_dynamic-slice_fusion.17), channel_id=1, source_target_pairs={{0,2},{1,3},{2,0},{3,1},{4,6},{5,7},{6,4},{7,5},{8,10},{9,11},{10,... | collective-permute-start | bytes 884744 | tf_op jit(solution)/shard_map/ppermute | solution.py:646
  77.3 9.3 %collective-permute-start.17 = (bf16[192,768]{1,0:T(8,128)(2,1)S(1)}, bf16[192,768]{1,0:T(8,128)(2,1)}, u32[]{:S(2)}, u32[]{:S(2)}) collective-permute-start(bf16[192,768]{1,0:T(8,128)(2,1)S(1)} %constant_dynamic-slice_fusion.16), channel_id=1, source_target_pairs={{0,2},{1,3},{2,0},{3,1},{4,6},{5,7},{6,4},{7,5},{8,10},{9,11},{10,... | collective-permute-start | bytes 884744 | tf_op jit(solution)/shard_map/ppermute | solution.py:646
  78.2 20.4 %collective-permute-start.22 = (bf16[96,3200]{1,0:T(8,128)(2,1)S(1)}, bf16[96,3200]{1,0:T(8,128)(2,1)}, u32[]{:S(2)}, u32[]{:S(2)}) collective-permute-start(bf16[96,3200]{1,0:T(8,128)(2,1)S(1)} %collective-permute-done.14.refs_3_), channel_id=1, source_target_pairs={{0,1},{1,0},{2,3},{3,2},{4,5},{5,4},{6,7},{7,6},{8,9},{9,8},{10,11... | collective-permute-start | bytes 1843208 | tf_op jit(solution)/shard_map/ppermute | solution.py:646
  78.7 19.8 %collective-permute-start.20 = (bf16[96,1536]{1,0:T(8,128)(2,1)}, bf16[96,1536]{1,0:T(8,128)(2,1)S(1)}, u32[]{:S(2)}, u32[]{:S(2)}) collective-permute-start(bf16[96,1536]{1,0:T(8,128)(2,1)} %collective-permute-done.10.refs_8_), channel_id=1, source_target_pairs={{0,4},{4,0},{8,12},{12,8},{16,20},{20,16},{24,28},{28,24},{1,5},{5... | collective-permute-start | bytes 884744 | tf_op jit(solution)/shard_map/ppermute | solution.py:646
  86.6 11.9 %collective-permute-start.23 = (bf16[96,1536]{1,0:T(8,128)(2,1)}, bf16[96,1536]{1,0:T(8,128)(2,1)S(1)}, u32[]{:S(2)}, u32[]{:S(2)}) collective-permute-start(bf16[96,1536]{1,0:T(8,128)(2,1)} %collective-permute-done.10.refs_8_), channel_id=1, source_target_pairs={{0,1},{1,0},{2,3},{3,2},{4,5},{5,4},{6,7},{7,6},{8,9},{9,8},{10,11... | collective-permute-start | bytes 884744 | tf_op jit(solution)/shard_map/ppermute | solution.py:646
  86.6 11.9 %collective-permute-start.21 = (bf16[192,768]{1,0:T(8,128)(2,1)S(1)}, bf16[192,768]{1,0:T(8,128)(2,1)}, u32[]{:S(2)}, u32[]{:S(2)}) collective-permute-start(bf16[192,768]{1,0:T(8,128)(2,1)S(1)} %collective-permute-done.11.refs_14_), channel_id=1, source_target_pairs={{0,4},{4,0},{8,12},{12,8},{16,20},{20,16},{24,28},{28,24},{1,5},{5... | collective-permute-start | bytes 884744 | tf_op jit(solution)/shard_map/ppermute | solution.py:646
  87.5 11.0 %collective-permute-start.24 = (bf16[192,768]{1,0:T(8,128)(2,1)S(1)}, bf16[192,768]{1,0:T(8,128)(2,1)}, u32[]{:S(2)}, u32[]{:S(2)}) collective-permute-start(bf16[192,768]{1,0:T(8,128)(2,1)S(1)} %collective-permute-done.11.refs_14_), channel_id=1, source_target_pairs={{0,1},{1,0},{2,3},{3,2},{4,5},{5,4},{6,7},{7,6},{8,9},{9,8},{10,11... | collective-permute-start | bytes 884744 | tf_op jit(solution)/shard_map/ppermute | solution.py:646
  98.6 6.0 %collective-permute-start.28 = (bf16[96,1536]{1,0:T(8,128)(2,1)S(1)}, bf16[96,1536]{1,0:T(8,128)(2,1)S(1)}, u32[]{:S(2)}, u32[]{:S(2)}) collective-permute-start(bf16[96,1536]{1,0:T(8,128)(2,1)S(1)} %collective-permute-done.20.refs_9_), channel_id=1, source_target_pairs={{0,1},{1,0},{2,3},{3,2},{4,5},{5,4},{6,7},{7,6},{8,9},{9,8},{10,11... | collective-permute-start | bytes 884744 | tf_op jit(solution)/shard_map/ppermute | solution.py:646
  98.9 5.8 %collective-permute-start.29 = (bf16[192,768]{1,0:T(8,128)(2,1)}, bf16[192,768]{1,0:T(8,128)(2,1)S(1)}, u32[]{:S(2)}, u32[]{:S(2)}) collective-permute-start(bf16[192,768]{1,0:T(8,128)(2,1)} %collective-permute-done.21.refs_15_), channel_id=1, source_target_pairs={{0,1},{1,0},{2,3},{3,2},{4,5},{5,4},{6,7},{7,6},{8,9},{9,8},{10,11... | collective-permute-start | bytes 884744 | tf_op jit(solution)/shard_map/ppermute | solution.py:646
  102.5 36.5 %collective-permute-start.30 = (bf16[96,1536]{1,0:T(8,128)(2,1)}, bf16[96,1536]{1,0:T(8,128)(2,1)}, u32[]{:S(2)}, u32[]{:S(2)}) collective-permute-start(bf16[96,1536]{1,0:T(8,128)(2,1)} %collective-permute-done.16.refs_2_), channel_id=1, source_target_pairs={{0,4},{4,0},{8,12},{12,8},{16,20},{20,16},{24,28},{28,24},{1,5},{5... | collective-permute-start | bytes 884744 | tf_op jit(solution)/shard_map/ppermute | solution.py:646
  103.6 35.4 %collective-permute-start.32 = (bf16[96,1536]{1,0:T(8,128)(2,1)}, bf16[96,1536]{1,0:T(8,128)(2,1)}, u32[]{:S(2)}, u32[]{:S(2)}) collective-permute-start(bf16[96,1536]{1,0:T(8,128)(2,1)} %collective-permute-done.16.refs_2_), channel_id=1, source_target_pairs={{0,1},{1,0},{2,3},{3,2},{4,5},{5,4},{6,7},{7,6},{8,9},{9,8},{10,11... | collective-permute-start | bytes 884744 | tf_op jit(solution)/shard_map/ppermute | solution.py:646
  103.6 35.4 %collective-permute-start.31 = (bf16[192,768]{1,0:T(8,128)(2,1)}, bf16[192,768]{1,0:T(8,128)(2,1)}, u32[]{:S(2)}, u32[]{:S(2)}) collective-permute-start(bf16[192,768]{1,0:T(8,128)(2,1)} %collective-permute-done.17.refs_8_), channel_id=1, source_target_pairs={{0,4},{4,0},{8,12},{12,8},{16,20},{20,16},{24,28},{28,24},{1,5},{5... | collective-permute-start | bytes 884744 | tf_op jit(solution)/shard_map/ppermute | solution.py:646
  104.5 34.5 %collective-permute-start.33 = (bf16[192,768]{1,0:T(8,128)(2,1)}, bf16[192,768]{1,0:T(8,128)(2,1)}, u32[]{:S(2)}, u32[]{:S(2)}) collective-permute-start(bf16[192,768]{1,0:T(8,128)(2,1)} %collective-permute-done.17.refs_8_), channel_id=1, source_target_pairs={{0,1},{1,0},{2,3},{3,2},{4,5},{5,4},{6,7},{7,6},{8,9},{9,8},{10,11... | collective-permute-start | bytes 884744 | tf_op jit(solution)/shard_map/ppermute | solution.py:646
  194.1 25.2 %collective-permute-start.37 = (bf16[2,2,2,2,24,1536]{5,4,3,2,1,0:T(8,128)(2,1)S(1)}, bf16[2,2,2,2,24,1536]{5,4,3,2,1,0:T(8,128)(2,1)}, u32[]{:S(2)}, u32[]{:S(2)}) collective-permute-start(bf16[2,2,2,2,24,1536]{5,4,3,2,1,0:T(8,128)(2,1)S(1)} %fusion.10), channel_id=1, source_target_pairs={{0,1},{1,0},{2,3},{3,2},{4,5},{5,4},{6,7},{7,6},{8,9},{9,8},{10,11... | collective-permute-start | bytes 3538952 | tf_op jit(solution)/shard_map/ppermute | solution.py:646
  203.0 16.3 %collective-permute-start.36 = (bf16[2,2,2,2,48,768]{5,4,3,2,1,0:T(8,128)(2,1)}, bf16[2,2,2,2,48,768]{5,4,3,2,1,0:T(8,128)(2,1)}, u32[]{:S(2)}, u32[]{:S(2)}) collective-permute-start(bf16[2,2,2,2,48,768]{5,4,3,2,1,0:T(8,128)(2,1)} %fusion.4), channel_id=1, source_target_pairs={{0,1},{1,0},{2,3},{3,2},{4,5},{5,4},{6,7},{7,6},{8,9},{9,8},{10,11... | collective-permute-start | bytes 3538952 | tf_op jit(solution)/shard_map/ppermute | solution.py:646
  219.5 9.9 %collective-permute-start.39 = (bf16[2,2,2,2,48,768]{5,4,2,1,0,3:T(8,128)(2,1)S(1)}, bf16[2,2,2,2,48,768]{5,4,2,1,0,3:T(8,128)(2,1)S(1)}, u32[]{:S(2)}, u32[]{:S(2)}) collective-permute-start(bf16[2,2,2,2,48,768]{5,4,2,1,0,3:T(8,128)(2,1)S(1)} %fusion.8), channel_id=1, source_target_pairs={{0,1},{1,0},{2,3},{3,2},{4,5},{5,4},{6,7},{7,6},{8,9},{9,8},{10,11... | collective-permute-start | bytes 3538952 | tf_op jit(solution)/shard_map/ppermute | solution.py:646
  219.9 8.8 %collective-permute-start.40 = (bf16[2,2,2,2,24,1536]{5,4,2,1,0,3:T(8,128)(2,1)S(1)}, bf16[2,2,2,2,24,1536]{5,4,2,1,0,3:T(8,128)(2,1)S(1)}, u32[]{:S(2)}, u32[]{:S(2)}) collective-permute-start(bf16[2,2,2,2,24,1536]{5,4,2,1,0,3:T(8,128)(2,1)S(1)} %fusion.9), channel_id=1, source_target_pairs={{0,1},{1,0},{2,3},{3,2},{4,5},{5,4},{6,7},{7,6},{8,9},{9,8},{10,11... | collective-permute-start | bytes 3538952 | tf_op jit(solution)/shard_map/ppermute | solution.py:646
  227.6 51.3 %collective-permute-start.38 = (bf16[2,2,2,96,768]{4,3,2,1,0:T(8,128)(2,1)}, bf16[2,2,2,96,768]{4,3,2,1,0:T(8,128)(2,1)}, u32[]{:S(2)}, u32[]{:S(2)}) collective-permute-start(bf16[2,2,2,96,768]{4,3,2,1,0:T(8,128)(2,1)} %fusion.5), channel_id=1, source_target_pairs={{0,2},{1,3},{2,0},{3,1},{4,6},{5,7},{6,4},{7,5},{8,10},{9,11},{10,... | collective-permute-start | bytes 3538952 | tf_op jit(solution)/shard_map/ppermute | solution.py:646
  233.4 45.6 %collective-permute-start.41 = (bf16[2,2,2,96,768]{4,3,2,1,0:T(8,128)(2,1)}, bf16[2,2,2,96,768]{4,3,2,1,0:T(8,128)(2,1)}, u32[]{:S(2)}, u32[]{:S(2)}) collective-permute-start(bf16[2,2,2,96,768]{4,3,2,1,0:T(8,128)(2,1)} %fusion.6), channel_id=1, source_target_pairs={{0,4},{4,0},{8,12},{12,8},{16,20},{20,16},{24,28},{28,24},{1,5},{5... | collective-permute-start | bytes 3538952 | tf_op jit(solution)/shard_map/ppermute | solution.py:646
  282.8 34.8 %collective-permute-start.43 = (bf16[2,2,96,768]{3,2,1,0:T(8,128)(2,1)S(1)}, bf16[2,2,96,768]{3,2,1,0:T(8,128)(2,1)S(1)}, u32[]{:S(2)}, u32[]{:S(2)}) collective-permute-start(bf16[2,2,96,768]{3,2,1,0:T(8,128)(2,1)S(1)} %fusion.23), channel_id=1, source_target_pairs={{0,2},{1,3},{2,0},{3,1},{4,6},{5,7},{6,4},{7,5},{8,10},{9,11},{10,... | collective-permute-start | bytes 1769480 | tf_op jit(solution)/shard_map/ppermute | solution.py:646
  286.2 12.0 %collective-permute-start.72 = (f32[2688]{0:T(1024)S(1)}, f32[2688]{0:T(1024)S(1)}, u32[]{:S(2)}, u32[]{:S(2)}) collective-permute-start(f32[2688]{0:T(1024)S(1)} %get-tuple-element.350), channel_id=1, source_target_pairs={{0,2},{1,3},{2,0},{3,1},{4,6},{5,7},{6,4},{7,5},{8,10},{9,11},{10,... | collective-permute-start | bytes 32264 | tf_op jit(solution)/shard_map/ppermute | solution.py:646
  287.4 10.9 %collective-permute-start.73 = (f32[2688]{0:T(1024)S(1)}, f32[2688]{0:T(1024)S(1)}, u32[]{:S(2)}, u32[]{:S(2)}) collective-permute-start(f32[2688]{0:T(1024)S(1)} %get-tuple-element.349), channel_id=1, source_target_pairs={{0,3},{1,2},{2,1},{3,0},{4,7},{5,6},{6,5},{7,4},{8,11},{9,10},{10,... | collective-permute-start | bytes 32264 | tf_op jit(solution)/shard_map/ppermute | solution.py:646
  299.4 18.3 %collective-permute-start.42 = (bf16[2,2,96,768]{3,2,1,0:T(8,128)(2,1)S(1)}, bf16[2,2,96,768]{3,2,1,0:T(8,128)(2,1)S(1)}, u32[]{:S(2)}, u32[]{:S(2)}) collective-permute-start(bf16[2,2,96,768]{3,2,1,0:T(8,128)(2,1)S(1)} %fusion.22), channel_id=1, source_target_pairs={{0,4},{4,0},{8,12},{12,8},{16,20},{20,16},{24,28},{28,24},{1,5},{5... | collective-permute-start | bytes 1769480 | tf_op jit(solution)/shard_map/ppermute | solution.py:646
  302.2 12.0 %collective-permute-start.75 = (f32[2688]{0:T(1024)S(1)}, f32[2688]{0:T(1024)S(1)}, u32[]{:S(2)}, u32[]{:S(2)}) collective-permute-start(f32[2688]{0:T(1024)S(1)} %add.313), channel_id=1, source_target_pairs={{0,8},{4,12},{8,0},{12,4},{16,24},{20,28},{24,16},{28,20},{1,9},{5... | collective-permute-start | bytes 32264 | tf_op jit(solution)/shard_map/ppermute | solution.py:646
  314.2 27.9 %collective-permute-start.76 = (f32[2688]{0:T(1024)S(1)}, f32[2688]{0:T(1024)S(1)}, u32[]{:S(2)}, u32[]{:S(2)}) collective-permute-start(f32[2688]{0:T(1024)S(1)} %add.314), channel_id=1, source_target_pairs={{0,16},{4,20},{8,24},{12,28},{16,0},{20,4},{24,8},{28,12},{1,17},{... | collective-permute-start | bytes 32264 | tf_op jit(solution)/shard_map/ppermute | solution.py:646
  318.8 23.9 %collective-permute-start.44 = (bf16[2,192,768]{2,1,0:T(8,128)(2,1)}, bf16[2,192,768]{2,1,0:T(8,128)(2,1)S(1)}, u32[]{:S(2)}, u32[]{:S(2)}) collective-permute-start(bf16[2,192,768]{2,1,0:T(8,128)(2,1)} %fusion.25), channel_id=1, source_target_pairs={{0,8},{4,12},{8,0},{12,4},{16,24},{20,28},{24,16},{28,20},{1,9},{5... | collective-permute-start | bytes 1769480 | tf_op jit(solution)/shard_map/ppermute | solution.py:646
  320.3 22.4 %collective-permute-start.45 = (bf16[2,2,2,2,24,1664]{5,4,3,2,1,0:T(8,128)(2,1)}, bf16[2,2,2,2,24,1664]{5,4,3,2,1,0:T(8,128)(2,1)}, u32[]{:S(2)}, u32[]{:S(2)}) collective-permute-start(bf16[2,2,2,2,24,1664]{5,4,3,2,1,0:T(8,128)(2,1)} %fusion.3), channel_id=1, source_target_pairs={{0,1},{1,0},{2,3},{3,2},{4,5},{5,4},{6,7},{7,6},{8,9},{9,8},{10,11... | collective-permute-start | bytes 3833864 | tf_op jit(solution)/shard_map/ppermute | solution.py:646
  350.9 17.7 %collective-permute-start.47 = (bf16[2,2,2,2,24,1536]{5,4,3,2,1,0:T(8,128)(2,1)S(1)}, bf16[2,2,2,2,24,1536]{5,4,3,2,1,0:T(8,128)(2,1)S(1)}, u32[]{:S(2)}, u32[]{:S(2)}) collective-permute-start(bf16[2,2,2,2,24,1536]{5,4,3,2,1,0:T(8,128)(2,1)S(1)} %fusion.7), channel_id=1, source_target_pairs={{0,1},{1,0},{2,3},{3,2},{4,5},{5,4},{6,7},{7,6},{8,9},{9,8},{10,11... | collective-permute-start | bytes 3538952 | tf_op jit(solution)/shard_map/ppermute | solution.py:646
  351.6 17.0 %collective-permute-start.46 = (bf16[192,768]{1,0:T(8,128)(2,1)S(1)}, bf16[192,768]{1,0:T(8,128)(2,1)S(1)}, u32[]{:S(2)}, u32[]{:S(2)}) collective-permute-start(bf16[192,768]{1,0:T(8,128)(2,1)S(1)} %fusion.30), channel_id=1, source_target_pairs={{0,16},{4,20},{8,24},{12,28},{16,0},{20,4},{24,8},{28,12},{1,17},{... | collective-permute-start | bytes 884744 | tf_op jit(solution)/shard_map/ppermute | solution.py:646
  358.3 64.2 %collective-permute-start.53 = (bf16[2,2,2,24,1664]{4,3,2,1,0:T(8,128)(2,1)}, bf16[2,2,2,24,1664]{4,3,2,1,0:T(8,128)(2,1)}, u32[]{:S(2)}, u32[]{:S(2)}) collective-permute-start(bf16[2,2,2,24,1664]{4,3,2,1,0:T(8,128)(2,1)} %fusion.16), channel_id=1, source_target_pairs={{0,2},{1,3},{2,0},{3,1},{4,6},{5,7},{6,4},{7,5},{8,10},{9,11},{10,... | collective-permute-start | bytes 1916936 | tf_op jit(solution)/shard_map/ppermute | solution.py:646
  368.6 7.9 %collective-permute-start.48 = (f32[2,16,768]{2,1,0:T(8,128)S(1)}, f32[2,16,768]{2,1,0:T(8,128)S(1)}, u32[]{:S(2)}, u32[]{:S(2)}) collective-permute-start(f32[2,16,768]{2,1,0:T(8,128)S(1)} %copy-done.45), channel_id=1, source_target_pairs={{4,0},{8,4},{12,8},{16,12},{20,16},{24,20},{28,24},{5,1},{9,5},{13... | collective-permute-start | bytes 294920 | tf_op jit(solution)/shard_map/ppermute | solution.py:651
  369.9 12.3 %collective-permute-start.49 = (f32[2,16,768]{2,1,0:T(8,128)S(1)}, f32[2,16,768]{2,1,0:T(8,128)S(1)}, u32[]{:S(2)}, u32[]{:S(2)}) collective-permute-start(f32[2,16,768]{2,1,0:T(8,128)S(1)} %copy-done.45), channel_id=1, source_target_pairs={{8,0},{12,4},{16,8},{20,12},{24,16},{28,20},{9,1},{13,5},{17,9},{2... | collective-permute-start | bytes 294920 | tf_op jit(solution)/shard_map/ppermute | solution.py:651
  371.2 12.5 %collective-permute-start.50 = (f32[2,16,768]{2,1,0:T(8,128)S(1)}, f32[2,16,768]{2,1,0:T(8,128)S(1)}, u32[]{:S(2)}, u32[]{:S(2)}) collective-permute-start(f32[2,16,768]{2,1,0:T(8,128)S(1)} %copy-done.45), channel_id=1, source_target_pairs={{12,0},{16,4},{20,8},{24,12},{28,16},{13,1},{17,5},{21,9},{25,13},... | collective-permute-start | bytes 294920 | tf_op jit(solution)/shard_map/ppermute | solution.py:651
  372.5 24.1 %collective-permute-start.51 = (f32[2,16,768]{2,1,0:T(8,128)S(1)}, f32[2,16,768]{2,1,0:T(8,128)S(1)}, u32[]{:S(2)}, u32[]{:S(2)}) collective-permute-start(f32[2,16,768]{2,1,0:T(8,128)S(1)} %copy-done.45), channel_id=1, source_target_pairs={{16,0},{20,4},{24,8},{28,12},{17,1},{21,5},{25,9},{29,13},{18,2},{... | collective-permute-start | bytes 294920 | tf_op jit(solution)/shard_map/ppermute | solution.py:651
  376.5 46.0 %collective-permute-start.55 = (bf16[1,192,768]{2,1,0:T(8,128)(2,1)S(1)}, bf16[1,192,768]{2,1,0:T(8,128)(2,1)}, u32[]{:S(2)}, u32[]{:S(2)}) collective-permute-start(bf16[1,192,768]{2,1,0:T(8,128)(2,1)S(1)} %fusion.32), channel_id=1, source_target_pairs={{0,16},{4,20},{8,24},{12,28},{16,0},{20,4},{24,8},{28,12},{1,17},{... | collective-permute-start | bytes 884744 | tf_op jit(solution)/shard_map/ppermute | solution.py:646
  382.2 40.3 %collective-permute-start.54 = (bf16[2,2,2,24,1536]{4,3,2,1,0:T(8,128)(2,1)}, bf16[2,2,2,24,1536]{4,3,2,1,0:T(8,128)(2,1)}, u32[]{:S(2)}, u32[]{:S(2)}) collective-permute-start(bf16[2,2,2,24,1536]{4,3,2,1,0:T(8,128)(2,1)} %fusion.24), channel_id=1, source_target_pairs={{0,4},{4,0},{8,12},{12,8},{16,20},{20,16},{24,28},{28,24},{1,5},{5... | collective-permute-start | bytes 1769480 | tf_op jit(solution)/shard_map/ppermute | solution.py:646
  396.6 7.5 %collective-permute-start.52 = (f32[2,16,768]{2,1,0:T(8,128)S(1)}, f32[2,16,768]{2,1,0:T(8,128)S(1)}, u32[]{:S(2)}, u32[]{:S(2)}) collective-permute-start(f32[2,16,768]{2,1,0:T(8,128)S(1)} %multiply_add_fusion.1), channel_id=1, source_target_pairs={{16,0},{20,4},{24,8},{28,12},{17,1},{21,5},{25,9},{29,13},{18,2},{... | collective-permute-start | bytes 294920 | tf_op jit(solution)/shard_map/ppermute | solution.py:651
  424.6 24.9 %collective-permute-start.58 = (bf16[2,192,768]{2,1,0:T(8,128)(2,1)}, bf16[2,192,768]{2,1,0:T(8,128)(2,1)}, u32[]{:S(2)}, u32[]{:S(2)}) collective-permute-start(bf16[2,192,768]{2,1,0:T(8,128)(2,1)} %pad_maximum_fusion.8), channel_id=1, source_target_pairs={{0,8},{4,12},{8,0},{12,4},{16,24},{20,28},{24,16},{28,20},{1,9},{5... | collective-permute-start | bytes 1769480 | tf_op jit(solution)/shard_map/ppermute | solution.py:646
  426.9 22.5 %collective-permute-start.57 = (bf16[2,2,24,1536]{3,2,1,0:T(8,128)(2,1)}, bf16[2,2,24,1536]{3,2,1,0:T(8,128)(2,1)}, u32[]{:S(2)}, u32[]{:S(2)}) collective-permute-start(bf16[2,2,24,1536]{3,2,1,0:T(8,128)(2,1)} %fusion.31), channel_id=1, source_target_pairs={{0,2},{1,3},{2,0},{3,1},{4,6},{5,7},{6,4},{7,5},{8,10},{9,11},{10,... | collective-permute-start | bytes 884744 | tf_op jit(solution)/shard_map/ppermute | solution.py:646
  430.3 19.2 %collective-permute-start.56 = (bf16[2,2,24,1664]{3,2,1,0:T(8,128)(2,1)S(1)}, bf16[2,2,24,1664]{3,2,1,0:T(8,128)(2,1)S(1)}, u32[]{:S(2)}, u32[]{:S(2)}) collective-permute-start(bf16[2,2,24,1664]{3,2,1,0:T(8,128)(2,1)S(1)} %fusion.27), channel_id=1, source_target_pairs={{0,4},{4,0},{8,12},{12,8},{16,20},{20,16},{24,28},{28,24},{1,5},{5... | collective-permute-start | bytes 958472 | tf_op jit(solution)/shard_map/ppermute | solution.py:646
  451.6 22.8 %collective-permute-start.59 = (bf16[2,24,3200]{2,1,0:T(8,128)(2,1)}, bf16[2,24,3200]{2,1,0:T(8,128)(2,1)}, u32[]{:S(2)}, u32[]{:S(2)}) collective-permute-start(bf16[2,24,3200]{2,1,0:T(8,128)(2,1)} %fusion.28), channel_id=1, source_target_pairs={{0,8},{4,12},{8,0},{12,4},{16,24},{20,28},{24,16},{28,20},{1,9},{5... | collective-permute-start | bytes 921608 | tf_op jit(solution)/shard_map/ppermute | solution.py:646
  478.2 9.9 %collective-permute-start.67 = (bf16[24,3200]{1,0:T(8,128)(2,1)S(1)}, bf16[24,3200]{1,0:T(8,128)(2,1)S(1)}, u32[]{:S(2)}, u32[]{:S(2)}) collective-permute-start(bf16[24,3200]{1,0:T(8,128)(2,1)S(1)} %fusion.33), channel_id=1, source_target_pairs={{0,16},{4,20},{8,24},{12,28},{16,0},{20,4},{24,8},{28,12},{1,17},{... | collective-permute-start | bytes 460808 | tf_op jit(solution)/shard_map/ppermute | solution.py:646
  484.3 28.9 %collective-permute-start.66 = (bf16[4,192,768]{2,1,0:T(8,128)(2,1)S(1)}, bf16[4,192,768]{2,1,0:T(8,128)(2,1)S(1)}, u32[]{:S(2)}, u32[]{:S(2)}) collective-permute-start(bf16[4,192,768]{2,1,0:T(8,128)(2,1)S(1)} %pad_maximum_fusion.5), channel_id=1, source_target_pairs={{0,4},{4,0},{8,12},{12,8},{16,20},{20,16},{24,28},{28,24},{1,5},{5... | collective-permute-start | bytes 3538952 | tf_op jit(solution)/shard_map/ppermute | solution.py:646
  486.9 6.5 %collective-permute-start.64 = (f32[65,192]{1,0:T(8,128)S(1)}, f32[65,192]{1,0:T(8,128)S(1)}, u32[]{:S(2)}, u32[]{:S(2)}) collective-permute-start(f32[65,192]{1,0:T(8,128)S(1)} %add.305), channel_id=1, source_target_pairs={{0,8},{4,12},{8,0},{12,4},{16,24},{20,28},{24,16},{28,20},{1,9},{5... | collective-permute-start | bytes 149768 | tf_op jit(solution)/shard_map/ppermute | solution.py:646
  488.1 11.7 %collective-permute-start.68 = (bf16[1,24,3200]{2,1,0:T(8,128)(2,1)S(1)}, bf16[1,24,3200]{2,1,0:T(8,128)(2,1)S(1)}, u32[]{:S(2)}, u32[]{:S(2)}) collective-permute-start(bf16[1,24,3200]{2,1,0:T(8,128)(2,1)S(1)} %fusion.34), channel_id=1, source_target_pairs={{0,16},{4,20},{8,24},{12,28},{16,0},{20,4},{24,8},{28,12},{1,17},{... | collective-permute-start | bytes 460808 | tf_op jit(solution)/shard_map/ppermute | solution.py:646
  493.4 7.9 %collective-permute-start.65 = (f32[65,192]{1,0:T(8,128)S(1)}, f32[65,192]{1,0:T(8,128)S(1)}, u32[]{:S(2)}, u32[]{:S(2)}) collective-permute-start(f32[65,192]{1,0:T(8,128)S(1)} %add.306), channel_id=1, source_target_pairs={{0,16},{4,20},{8,24},{12,28},{16,0},{20,4},{24,8},{28,12},{1,17},{... | collective-permute-start | bytes 149768 | tf_op jit(solution)/shard_map/ppermute | solution.py:646
  499.9 9.2 %collective-permute-start.69 = (bf16[2,24,3200]{2,1,0:T(8,128)(2,1)S(1)}, bf16[2,24,3200]{2,1,0:T(8,128)(2,1)S(1)}, u32[]{:S(2)}, u32[]{:S(2)}) collective-permute-start(bf16[2,24,3200]{2,1,0:T(8,128)(2,1)S(1)} %pad_maximum_fusion.9), channel_id=1, source_target_pairs={{0,8},{4,12},{8,0},{12,4},{16,24},{20,28},{24,16},{28,20},{1,9},{5... | collective-permute-start | bytes 921608 | tf_op jit(solution)/shard_map/ppermute | solution.py:646
  509.2 16.2 %collective-permute-start.70 = (bf16[4,24,3200]{2,1,0:T(8,128)(2,1)S(1)}, bf16[4,24,3200]{2,1,0:T(8,128)(2,1)S(1)}, u32[]{:S(2)}, u32[]{:S(2)}) collective-permute-start(bf16[4,24,3200]{2,1,0:T(8,128)(2,1)S(1)} %pad_maximum_fusion.7), channel_id=1, source_target_pairs={{0,4},{4,0},{8,12},{12,8},{16,20},{20,16},{24,28},{28,24},{1,5},{5... | collective-permute-start | bytes 1843208 | tf_op jit(solution)/shard_map/ppermute | solution.py:646
  (70 other events, 759.7 us)
